TPU v7x, 32 devices: a whole 2x2x4 slice. The times are simulated.
32 devices in a mesh: expert: 16 (over z, y, x), fsdp: 2 (over core).
Axes of the slice: x: 2, y: 2, z: 4, core: 2. Of those that a mesh axis runs over, the one named last changes fastest.
Arguments:
- tokens: bfloat16 [4096, 2048], P(('expert', 'fsdp')), may hold values from -6 to 6
- segments: int32 [4096], P('expert'), may hold values from 0 to 47, as said below
- routes: int32 [4096, 6], P(('expert', 'fsdp')), may hold values from 0 to 15, all different within a row; in each aligned block of 128 rows (0 to 127, 128 to 255, ...) at most 96 rows name the same one
- norm_attn: bfloat16 [2048], P(('expert', 'fsdp')), may hold values from 0.5 to 1.5
- query_proj: bfloat16 [2048, 3072], P(('expert', 'fsdp')), may hold values from -0.125 to 0.125
- latent_proj: bfloat16 [2048, 576], P(('expert', 'fsdp')), may hold values from -0.125 to 0.125
- norm_latent: bfloat16 [512], P(('expert', 'fsdp')), may hold values from 0.5 to 1.5
- expand_proj: bfloat16 [512, 4096], P(('expert', 'fsdp')), may hold values from -0.25 to 0.25
- output_proj: bfloat16 [2048, 2048], P(('expert', 'fsdp')), may hold values from -1.0546875 to 1.0546875
- norm_ffn: bfloat16 [2048], P(('expert', 'fsdp')), may hold values from 0.5 to 1.5
- router: bfloat16 [2048, 16], P(('expert', 'fsdp')), may hold values from -0.06591797 to 0.06591797
- shared_gate: bfloat16 [2048, 2816], P(('expert', 'fsdp')), may hold values from -0.125 to 0.125
- shared_up: bfloat16 [2048, 2816], P(('expert', 'fsdp')), may hold values from -0.125 to 0.125
- shared_down: bfloat16 [2816, 2048], P(('expert', 'fsdp')), may hold values from -0.109375 to 0.109375
- expert_gate: bfloat16 [16, 2048, 1408], P('expert', 'fsdp'), may hold values from -0.125 to 0.125
- expert_up: bfloat16 [16, 2048, 1408], P('expert', 'fsdp'), may hold values from -0.125 to 0.125
- expert_down: bfloat16 [16, 1408, 2048], P('expert', 'fsdp'), may hold values from -0.15625 to 0.15625
- cotangent: bfloat16 [4096, 2048], P(('expert', 'fsdp')), may hold values from -6 to 6
Outputs:
- block_out: bfloat16 [4096, 2048], P(('expert', 'fsdp'))
- tokens_grad: bfloat16 [4096, 2048], P(('expert', 'fsdp'))
- norm_attn_grad: float32 [2048], P(('expert', 'fsdp'))
- query_proj_grad: float32 [2048, 3072], P(('expert', 'fsdp'))
- latent_proj_grad: float32 [2048, 576], P(('expert', 'fsdp'))
- norm_latent_grad: float32 [512], P(('expert', 'fsdp'))
- expand_proj_grad: float32 [512, 4096], P(('expert', 'fsdp'))
- output_proj_grad: float32 [2048, 2048], P(('expert', 'fsdp'))
- norm_ffn_grad: float32 [2048], P(('expert', 'fsdp'))
- router_grad: float32 [2048, 16], P(('expert', 'fsdp'))
- shared_gate_grad: float32 [2048, 2816], P(('expert', 'fsdp'))
- shared_up_grad: float32 [2048, 2816], P(('expert', 'fsdp'))
- shared_down_grad: float32 [2816, 2048], P(('expert', 'fsdp'))
- expert_gate_grad: float32 [16, 2048, 1408], P('expert', 'fsdp')
- expert_up_grad: float32 [16, 2048, 1408], P('expert', 'fsdp')
- expert_down_grad: float32 [16, 1408, 2048], P('expert', 'fsdp')
Inputs may be any that keep to these rules, and one draw needn't show every extreme that they name: `segments`: within each sequence of 256 tokens the numbers never fall; sequence s holds documents 3 s, 3 s + 1, 3 s + 2, and the middle one begins among its first 128 tokens and ends among its last 128. `routes`: each row names 6 different experts; in each aligned block of 128 rows no expert is named more than 96 times, a bound that some block reaches.
All inputs are finite; a program needn't handle non-finite values.
Results may differ from a plain program's by a relative error of at most 0.019.
Values may be sent and summed in bfloat16 or wider, within the bound.
No kernel may reach another device: no remote copies, remote signals or barrier semaphores. Data moves between devices by JAX's collectives and lax.ppermute only.
A program may use at most 384 MiB of HBM per device.

v0:
```python
import math

import jax
import jax.numpy as jnp
from jax import lax
from jax.sharding import PartitionSpec as P

D = 2048
H = 16
DN = 128
DR = 64
DV = 128
KVR = 512
TOPK = 6
SEQ_DEV = 128


NORM_EPS = 1e-06
ROPE_THETA = 50000.0
GATE_SCALE = 2.446


def rms_scale(values, gain_vec):
    return (
        values * lax.rsqrt(jnp.mean(values * values, axis=-1, keepdims=True) + NORM_EPS) * gain_vec
    )


def rotate(values, cos_table, sin_table):
    middle = values.shape[-1] // 2
    lower_half = values[..., :middle]
    upper_half = values[..., middle:]
    return jnp.concatenate(
        [
            lower_half * cos_table - upper_half * sin_table,
            upper_half * cos_table + lower_half * sin_table,
        ],
        axis=-1,
    )


def rope_tables(positions):
    steps_float = jnp.arange(DR // 2).astype(jnp.float32) * (2.0 / DR)
    inverse = jnp.exp(-steps_float * math.log(ROPE_THETA))
    turned = positions.astype(jnp.float32)[:, None] * inverse[None, :]
    return (jnp.cos(turned), jnp.sin(turned))


def product(left_side, right_side):
    return jnp.dot(left_side, right_side, preferred_element_type=jnp.float32)


def inner_rows(left_side, right_side):
    return lax.dot_general(
        left_side, right_side, (((0,), (0,)), ((), ())), preferred_element_type=jnp.float32
    )


def outer_cols(left_side, right_side):
    return lax.dot_general(
        left_side, right_side, (((1,), (1,)), ((), ())), preferred_element_type=jnp.float32
    )


def swiglu(gate_act, up_act):
    return jax.nn.silu(gate_act) * up_act


def body(
    tokens,
    segments,
    routes,
    norm_attn,
    query_proj,
    latent_proj,
    norm_latent,
    expand_proj,
    output_proj,
    norm_ffn,
    router,
    shared_gate,
    shared_up,
    shared_down,
    expert_gate,
    expert_up,
    expert_down,
    cotangent,
):
    gathered = (
        lax.all_gather(norm_attn, ("expert", "fsdp"), axis=0, tiled=True),
        lax.all_gather(query_proj, ("expert", "fsdp"), axis=0, tiled=True),
        lax.all_gather(latent_proj, ("expert", "fsdp"), axis=0, tiled=True),
        lax.all_gather(norm_latent, ("expert", "fsdp"), axis=0, tiled=True),
        lax.all_gather(expand_proj, ("expert", "fsdp"), axis=0, tiled=True),
        lax.all_gather(output_proj, ("expert", "fsdp"), axis=0, tiled=True),
        lax.all_gather(norm_ffn, ("expert", "fsdp"), axis=0, tiled=True),
        lax.all_gather(router, ("expert", "fsdp"), axis=0, tiled=True),
        lax.all_gather(shared_gate, ("expert", "fsdp"), axis=0, tiled=True),
        lax.all_gather(shared_up, ("expert", "fsdp"), axis=0, tiled=True),
        lax.all_gather(shared_down, ("expert", "fsdp"), axis=0, tiled=True),
    )
    gain_attn = gathered[0].astype(jnp.float32)
    query_weight = gathered[1]
    latent_weight = gathered[2]
    gain_latent = gathered[3].astype(jnp.float32)
    expand_weight = gathered[4]
    output_weight = gathered[5]
    gain_ffn = gathered[6].astype(jnp.float32)
    router_all = gathered[7]
    shared_gate_w = gathered[8]
    shared_up_w = gathered[9]
    shared_down_w = gathered[10]
    n_expert = lax.axis_size("expert")
    sequence_len = SEQ_DEV * lax.axis_size("fsdp")
    fsdp_index = lax.axis_index("fsdp")
    positions = fsdp_index * SEQ_DEV + jnp.arange(SEQ_DEV, dtype=jnp.int32)
    cos_table, sin_table = rope_tables(positions)
    inputs_f = tokens.astype(jnp.float32)
    normed = rms_scale(inputs_f, gain_attn).astype(jnp.bfloat16)
    query_all = product(normed, query_weight).reshape(SEQ_DEV, H, DN + DR)
    query_nope = query_all[..., :DN].astype(jnp.bfloat16)
    query_rope = rotate(query_all[..., DN:], cos_table[:, None, :], sin_table[:, None, :]).astype(
        jnp.bfloat16
    )
    latent = product(normed, latent_weight)
    latent_norm = rms_scale(latent[:, :KVR], gain_latent).astype(jnp.bfloat16)
    key_rope_own = rotate(latent[:, KVR:], cos_table, sin_table).astype(jnp.bfloat16)
    expanded_own = product(latent_norm, expand_weight).astype(jnp.bfloat16)
    expanded, key_rope = (
        lax.all_gather(expanded_own, "fsdp", axis=0, tiled=True),
        lax.all_gather(key_rope_own, "fsdp", axis=0, tiled=True),
    )
    expanded = expanded.reshape(sequence_len, H, DN + DV)
    key_nope = expanded[..., :DN]
    values_all = expanded[..., DN:]
    doc_query = lax.dynamic_slice_in_dim(segments, fsdp_index * SEQ_DEV, SEQ_DEV)
    key_places = jnp.arange(sequence_len, dtype=jnp.int32)
    allowed = (positions[:, None] >= key_places[None, :]) & (
        doc_query[:, None] == segments[None, :]
    )
    score_scale = (DN + DR) ** (-0.5)

    def scores_of():
        raw_scores = jnp.einsum(
            "thd,shd->hts", query_nope, key_nope, preferred_element_type=jnp.float32
        )
        raw_scores = raw_scores + jnp.einsum(
            "thd,sd->hts", query_rope, key_rope, preferred_element_type=jnp.float32
        )
        return jnp.where(allowed[None], raw_scores * score_scale, -1e30)

    scores = scores_of()
    row_top = jnp.max(scores, axis=-1, keepdims=True)
    shifted = jnp.exp(scores - row_top)
    row_total = jnp.sum(shifted, axis=-1, keepdims=True)
    log_total = row_top + jnp.log(row_total)
    weights_attn = (shifted / row_total).astype(jnp.bfloat16)
    attended = jnp.einsum(
        "hts,shd->thd", weights_attn, values_all, preferred_element_type=jnp.float32
    )
    attended = attended.reshape(SEQ_DEV, H * DV).astype(jnp.bfloat16)
    hidden = inputs_f + product(attended, output_weight)
    normed_ffn = rms_scale(hidden, gain_ffn).astype(jnp.bfloat16)
    logits = product(normed_ffn, router_all)
    expert_count = router_all.shape[1]
    route_hot = (
        routes[:, :, None] == jnp.arange(expert_count, dtype=jnp.int32)[None, None, :]
    ).astype(jnp.float32)

    def gate_values(logit_in):
        chosen = jnp.sum(route_hot * jax.nn.sigmoid(logit_in)[:, None, :], axis=2)
        return GATE_SCALE * chosen / jnp.sum(chosen, axis=1, keepdims=True)

    gate_weights, gate_pull = jax.vjp(gate_values, logits)
    shared_gate_act = product(normed_ffn, shared_gate_w)
    shared_up_act = product(normed_ffn, shared_up_w)
    shared_hidden = swiglu(shared_gate_act, shared_up_act).astype(jnp.bfloat16)
    shared_out = product(shared_hidden, shared_down_w)
    capacity = 2 * SEQ_DEV * TOPK // expert_count
    pair_count = SEQ_DEV * TOPK
    flat_routes = routes.reshape(-1)
    pair_hot = (flat_routes[:, None] == jnp.arange(expert_count, dtype=jnp.int32)[None, :]).astype(
        jnp.int32
    )
    rank_of_pair = jnp.sum((jnp.cumsum(pair_hot, axis=0) - 1) * pair_hot, axis=1)
    pair_slot = flat_routes * capacity + rank_of_pair
    slot_pair = (
        jnp.full((expert_count * capacity,), pair_count, jnp.int32)
        .at[pair_slot]
        .set(jnp.arange(pair_count, dtype=jnp.int32))
    )
    slot_filled = slot_pair < pair_count
    slot_clipped = jnp.minimum(slot_pair, pair_count - 1)
    send_rows = jnp.where(
        slot_filled[:, None], normed_ffn[slot_clipped // TOPK], jnp.zeros((), jnp.bfloat16)
    )
    received = lax.all_to_all(send_rows, "expert", split_axis=0, concat_axis=0, tiled=True)
    gate_full, up_full, down_full = (
        lax.all_gather(expert_gate, "fsdp", axis=1, tiled=True),
        lax.all_gather(expert_up, "fsdp", axis=1, tiled=True),
        lax.all_gather(expert_down, "fsdp", axis=1, tiled=True),
    )
    local_experts = expert_gate.shape[0]
    grouped = received.reshape(n_expert, local_experts, capacity, D)
    expert_gate_act = jnp.einsum(
        "sxcd,xdf->sxcf", grouped, gate_full, preferred_element_type=jnp.float32
    )
    expert_up_act = jnp.einsum(
        "sxcd,xdf->sxcf", grouped, up_full, preferred_element_type=jnp.float32
    )
    expert_hidden = swiglu(expert_gate_act, expert_up_act).astype(jnp.bfloat16)
    expert_out = jnp.einsum(
        "sxcf,xfd->sxcd", expert_hidden, down_full, preferred_element_type=jnp.float32
    ).astype(jnp.bfloat16)
    returned = lax.all_to_all(
        expert_out.reshape(-1, D), "expert", split_axis=0, concat_axis=0, tiled=True
    )
    picked = returned[pair_slot].reshape(SEQ_DEV, TOPK, D)
    routed = jnp.sum(gate_weights[:, :, None] * picked.astype(jnp.float32), axis=1)
    block_out = (hidden + shared_out + routed).astype(jnp.bfloat16)
    grad_out = cotangent.astype(jnp.float32)
    picked_grad = (
        (gate_weights[:, :, None] * grad_out[:, None, :]).astype(jnp.bfloat16).reshape(-1, D)
    )
    gate_grad = jnp.sum(picked.astype(jnp.float32) * grad_out[:, None, :], axis=2)
    send_grad = jnp.where(
        slot_filled[:, None], picked_grad[slot_clipped], jnp.zeros((), jnp.bfloat16)
    )
    received_grad = lax.all_to_all(
        send_grad, "expert", split_axis=0, concat_axis=0, tiled=True
    ).reshape(n_expert, local_experts, capacity, D)
    hidden_grad_ex = jnp.einsum(
        "sxcd,xfd->sxcf", received_grad, down_full, preferred_element_type=jnp.float32
    )
    down_grad = jnp.einsum(
        "sxcf,sxcd->xfd", expert_hidden, received_grad, preferred_element_type=jnp.float32
    )
    unused_value, expert_pull = jax.vjp(swiglu, expert_gate_act, expert_up_act)
    gate_act_grad, up_act_grad = expert_pull(hidden_grad_ex)
    gate_act_grad = gate_act_grad.astype(jnp.bfloat16)
    up_act_grad = up_act_grad.astype(jnp.bfloat16)
    gate_w_grad = jnp.einsum(
        "sxcd,sxcf->xdf", grouped, gate_act_grad, preferred_element_type=jnp.float32
    )
    up_w_grad = jnp.einsum(
        "sxcd,sxcf->xdf", grouped, up_act_grad, preferred_element_type=jnp.float32
    )
    input_grad = jnp.einsum(
        "sxcf,xdf->sxcd", gate_act_grad, gate_full, preferred_element_type=jnp.float32
    )
    input_grad = input_grad + jnp.einsum(
        "sxcf,xdf->sxcd", up_act_grad, up_full, preferred_element_type=jnp.float32
    )
    input_back = lax.all_to_all(
        input_grad.astype(jnp.bfloat16).reshape(-1, D),
        "expert",
        split_axis=0,
        concat_axis=0,
        tiled=True,
    )
    ffn_grad = jnp.sum(input_back[pair_slot].astype(jnp.float32).reshape(SEQ_DEV, TOPK, D), axis=1)
    expert_grads = (
        lax.psum_scatter(
            gate_w_grad.astype(jnp.bfloat16), "fsdp", scatter_dimension=1, tiled=True
        ).astype(jnp.float32),
        lax.psum_scatter(
            up_w_grad.astype(jnp.bfloat16), "fsdp", scatter_dimension=1, tiled=True
        ).astype(jnp.float32),
        lax.psum_scatter(
            down_grad.astype(jnp.bfloat16), "fsdp", scatter_dimension=1, tiled=True
        ).astype(jnp.float32),
    )
    logit_grad = gate_pull(gate_grad)[0].astype(jnp.bfloat16)
    router_grad = inner_rows(normed_ffn, logit_grad)
    ffn_grad = ffn_grad + outer_cols(logit_grad, router_all)
    shared_out_grad = grad_out.astype(jnp.bfloat16)
    shared_down_grad = inner_rows(shared_hidden, shared_out_grad)
    unused_shared, shared_pull = jax.vjp(swiglu, shared_gate_act, shared_up_act)
    shared_gate_back, shared_up_back = shared_pull(outer_cols(shared_out_grad, shared_down_w))
    shared_gate_back = shared_gate_back.astype(jnp.bfloat16)
    shared_up_back = shared_up_back.astype(jnp.bfloat16)
    shared_gate_grad = inner_rows(normed_ffn, shared_gate_back)
    shared_up_grad = inner_rows(normed_ffn, shared_up_back)
    ffn_grad = (
        ffn_grad
        + outer_cols(shared_gate_back, shared_gate_w)
        + outer_cols(shared_up_back, shared_up_w)
    )
    unused_norm, norm_pull = jax.vjp(rms_scale, hidden, gain_ffn)
    hidden_part, gain_ffn_grad = norm_pull(ffn_grad)
    hidden_grad = grad_out + hidden_part
    attn_grad = hidden_grad.astype(jnp.bfloat16)
    output_weight_grad = inner_rows(attended, attn_grad)
    attended_grad = (
        outer_cols(attn_grad, output_weight).astype(jnp.bfloat16).reshape(SEQ_DEV, H, DV)
    )
    probs_again = jnp.exp(scores_of() - log_total)
    prob_grad = jnp.einsum(
        "thd,shd->hts", attended_grad, values_all, preferred_element_type=jnp.float32
    )
    weighted = jnp.sum(probs_again * prob_grad, axis=-1, keepdims=True)
    score_grad = (probs_again * (prob_grad - weighted)).astype(jnp.bfloat16)
    query_nope_grad = score_scale * jnp.einsum(
        "hts,shd->thd", score_grad, key_nope, preferred_element_type=jnp.float32
    )
    query_rope_grad = score_scale * jnp.einsum(
        "hts,sd->thd", score_grad, key_rope, preferred_element_type=jnp.float32
    )
    key_nope_grad = score_scale * jnp.einsum(
        "hts,thd->shd", score_grad, query_nope, preferred_element_type=jnp.float32
    )
    key_rope_grad = score_scale * jnp.einsum(
        "hts,thd->sd", score_grad, query_rope, preferred_element_type=jnp.float32
    )
    values_grad = jnp.einsum(
        "hts,thd->shd",
        probs_again.astype(jnp.bfloat16),
        attended_grad,
        preferred_element_type=jnp.float32,
    )
    expanded_grad = jnp.concatenate([key_nope_grad, values_grad], axis=2).reshape(
        sequence_len, H * (DN + DV)
    )
    own_expanded_grad, own_rope_grad = (
        lax.psum_scatter(
            expanded_grad.astype(jnp.bfloat16), "fsdp", scatter_dimension=0, tiled=True
        ).astype(jnp.float32),
        lax.psum_scatter(
            key_rope_grad.astype(jnp.bfloat16), "fsdp", scatter_dimension=0, tiled=True
        ).astype(jnp.float32),
    )
    own_expanded_grad = own_expanded_grad.astype(jnp.bfloat16)
    expand_weight_grad = inner_rows(latent_norm, own_expanded_grad)
    unused_latent, latent_pull = jax.vjp(rms_scale, latent[:, :KVR], gain_latent)
    latent_nope_grad, gain_latent_grad = latent_pull(outer_cols(own_expanded_grad, expand_weight))
    latent_rope_grad = rotate(own_rope_grad, cos_table, -sin_table)
    latent_grad = jnp.concatenate([latent_nope_grad, latent_rope_grad], axis=1).astype(jnp.bfloat16)
    latent_weight_grad = inner_rows(normed, latent_grad)
    normed_grad = outer_cols(latent_grad, latent_weight)
    query_back = jnp.concatenate(
        [query_nope_grad, rotate(query_rope_grad, cos_table[:, None, :], -sin_table[:, None, :])],
        axis=2,
    )
    query_back = query_back.reshape(SEQ_DEV, H * (DN + DR)).astype(jnp.bfloat16)
    query_weight_grad = inner_rows(normed, query_back)
    normed_grad = normed_grad + outer_cols(query_back, query_weight)
    unused_first, first_pull = jax.vjp(rms_scale, inputs_f, gain_attn)
    input_part, gain_attn_grad = first_pull(normed_grad)
    tokens_grad = (hidden_grad + input_part).astype(jnp.bfloat16)
    layer_grads = (
        lax.psum_scatter(gain_attn_grad, ("expert", "fsdp"), scatter_dimension=0, tiled=True),
        lax.psum_scatter(query_weight_grad, ("expert", "fsdp"), scatter_dimension=0, tiled=True),
        lax.psum_scatter(latent_weight_grad, ("expert", "fsdp"), scatter_dimension=0, tiled=True),
        lax.psum_scatter(gain_latent_grad, ("expert", "fsdp"), scatter_dimension=0, tiled=True),
        lax.psum_scatter(expand_weight_grad, ("expert", "fsdp"), scatter_dimension=0, tiled=True),
        lax.psum_scatter(output_weight_grad, ("expert", "fsdp"), scatter_dimension=0, tiled=True),
        lax.psum_scatter(gain_ffn_grad, ("expert", "fsdp"), scatter_dimension=0, tiled=True),
        lax.psum_scatter(router_grad, ("expert", "fsdp"), scatter_dimension=0, tiled=True),
        lax.psum_scatter(shared_gate_grad, ("expert", "fsdp"), scatter_dimension=0, tiled=True),
        lax.psum_scatter(shared_up_grad, ("expert", "fsdp"), scatter_dimension=0, tiled=True),
        lax.psum_scatter(shared_down_grad, ("expert", "fsdp"), scatter_dimension=0, tiled=True),
    )
    return (
        block_out,
        tokens_grad,
        layer_grads[0],
        layer_grads[1],
        layer_grads[2],
        layer_grads[3],
        layer_grads[4],
        layer_grads[5],
        layer_grads[6],
        layer_grads[7],
        layer_grads[8],
        layer_grads[9],
        layer_grads[10],
        expert_grads[0],
        expert_grads[1],
        expert_grads[2],
    )


def solution(mesh):
    placed = (
        P(("expert", "fsdp"), None),
        P("expert"),
        P(("expert", "fsdp"), None),
        P(("expert", "fsdp")),
        P(("expert", "fsdp"), None),
        P(("expert", "fsdp"), None),
        P(("expert", "fsdp")),
        P(("expert", "fsdp"), None),
        P(("expert", "fsdp"), None),
        P(("expert", "fsdp")),
        P(("expert", "fsdp"), None),
        P(("expert", "fsdp"), None),
        P(("expert", "fsdp"), None),
        P(("expert", "fsdp"), None),
        P("expert", "fsdp", None),
        P("expert", "fsdp", None),
        P("expert", "fsdp", None),
        P(("expert", "fsdp"), None),
    )
    return jax.shard_map(
        body,
        mesh=mesh,
        in_specs=placed,
        out_specs=(
            P(("expert", "fsdp"), None),
            P(("expert", "fsdp"), None),
            P(("expert", "fsdp")),
            P(("expert", "fsdp"), None),
            P(("expert", "fsdp"), None),
            P(("expert", "fsdp")),
            P(("expert", "fsdp"), None),
            P(("expert", "fsdp"), None),
            P(("expert", "fsdp")),
            P(("expert", "fsdp"), None),
            P(("expert", "fsdp"), None),
            P(("expert", "fsdp"), None),
            P(("expert", "fsdp"), None),
            P("expert", "fsdp", None),
            P("expert", "fsdp", None),
            P("expert", "fsdp", None),
        ),
        check_vma=False,
    )
```

profile of v0, /device:TPU:0, one launch (start us, length us, event | category | flops | bytes accessed | tf_op | source)
XLA Modules:
  0.0 2868.5 jit_solution(1078076467140463890)
XLA Ops:
  11.3 42.2 %all-reduce.7 = (bf16[2048]{0:T(1024)(128)(2,1)S(1)}, bf16[512]{0:T(512)(128)(2,1)S(1)}, bf16[2048]{0:T(1024)(128)(2,1)S(1)}) all-reduce(bf16[2048]{0:T(1024)(128)(2,1)S(1)} %dynamic-update-slice, bf16[512]{0:T(512)(128)(2,1)S(1)} %dynamic-update-slice.1, ...), channel_id=1, replica_groups=mesh['expert'=16,'fsdp'=2] {'expert','fsdp'}, use_global_device_ids=true, to_apply=%add | all-reduce | flops 4608 | bytes 18432
  54.8 16.8 all-gather.13.cloned.1.call-done
  74.8 60.7 %all-gather.15.cloned.1.call-done = bf16[512,4096]{1,0:T(8,128)(2,1)} async-done(((bf16[16,4096]{1,0:T(8,128)(2,1)}), bf16[512,4096]{1,0:T(8,128)(2,1)}) %all-gather.15.cloned.1.call-update) | async-done | bytes 4194320 | tf_op jit(solution)/shard_map/all_gather | solution.py:94
  150.4 40.0 %all-gather = bf16[32,64,16]{1,2,0:T(8,128)(2,1)S(1)} all-gather(bf16[1,64,16]{1,2,0:T(8,128)(2,1)S(1)} %bitcast.240), channel_id=1, replica_groups=mesh['expert'=16,'fsdp'=2] {'expert','fsdp'}, dimensions={0}, use_global_device_ids=true | all-gather | bytes 67584 | tf_op jit(solution)/shard_map/all_gather | solution.py:97
  195.0 8.3 mul.552
  211.2 37.7 %all-gather.19.cloned.1.call-done = bf16[2048,3072]{1,0:T(8,128)(2,1)} async-done(((bf16[64,3072]{1,0:T(8,128)(2,1)}), bf16[2048,3072]{1,0:T(8,128)(2,1)}) %all-gather.19.cloned.1.call-update) | async-done | bytes 12582928 | tf_op jit(solution)/shard_map/all_gather | solution.py:91
  249.0 8.1 fusion.114
  260.9 66.5 %all-gather.21.cloned.1.call-done = bf16[2048,2048]{1,0:T(8,128)(2,1)} async-done(((bf16[64,2048]{1,0:T(8,128)(2,1)}), bf16[2048,2048]{1,0:T(8,128)(2,1)}) %all-gather.21.cloned.1.call-update) | async-done | bytes 8388624 | tf_op jit(solution)/shard_map/all_gather | solution.py:95
  346.4 15.1 gather_fusion.2
  361.5 8.2 broadcast_select_fusion
  369.7 205.7 %all_to_all.30 = bf16[16,96,2048]{2,1,0:T(8,128)(2,1)} all-to-all(bf16[16,96,2048]{2,1,0:T(8,128)(2,1)S(1)} %get-tuple-element.50), channel_id=1, replica_groups=mesh['expert'=16,'fsdp'=2] {'expert'}, dimensions={0} | all-to-all | bytes 12582912 | tf_op jit(solution)/shard_map/all_to_all | solution.py:229
  580.8 15.4 fusion.11
  596.2 137.8 %all-to-all-done = bf16[16,96,2048]{2,1,0:T(8,128)(2,1)} async-done(((bf16[16,96,2048]{2,1,0:T(8,128)(2,1)}), bf16[16,96,2048]{2,1,0:T(8,128)(2,1)}, u32[]{:S(2)}, u32[]{:S(2)}) %all-to-all-start) | async-done | bytes 6291488 | tf_op jit(solution)/shard_map/all_to_all | solution.py:197
  734.0 15.2 fusion.17
  749.2 21.6 fusion.2
  772.8 14.2 fusion.23
  787.1 39.1 %all-to-all-start.1 = ((bf16[16,96,2048]{2,1,0:T(8,128)(2,1)}), bf16[16,96,2048]{2,1,0:T(8,128)(2,1)}, u32[]{:S(2)}, u32[]{:S(2)}) async-start(bf16[16,96,2048]{2,1,0:T(8,128)(2,1)} %fusion.23), calls=%async_computation.1 | async-start | bytes 12582912 | tf_op jit(solution)/shard_map/all_to_all | solution.py:215
  826.2 16.2 fusion.15
  842.4 15.1 add_convert_fusion
  857.5 87.1 %all-to-all-done.1 = bf16[16,96,2048]{2,1,0:T(8,128)(2,1)} async-done(((bf16[16,96,2048]{2,1,0:T(8,128)(2,1)}), bf16[16,96,2048]{2,1,0:T(8,128)(2,1)}, u32[]{:S(2)}, u32[]{:S(2)}) %all-to-all-start.1) | async-done | bytes 6291488 | tf_op jit(solution)/shard_map/all_to_all | solution.py:215
  944.6 30.2 %all-to-all-start.3 = ((bf16[16,96,2048]{2,1,0:T(8,128)(2,1)}), bf16[16,96,2048]{2,1,0:T(8,128)(2,1)}, u32[]{:S(2)}, u32[]{:S(2)}) async-start(bf16[16,96,2048]{2,1,0:T(8,128)(2,1)} %add_convert_fusion), calls=%async_computation.3 | async-start | bytes 12582912 | tf_op jit(solution)/shard_map/all_to_all | solution.py:254
  975.2 9.3 fusion.123
  984.6 7.1 fusion.122
  991.7 8.3 fusion.44
  1000.0 8.6 fusion.124
  1013.5 10.9 gather_fusion.1
  1031.0 7.3 multiply_reduce_fusion
  1038.4 52.2 %all-to-all-done.3 = bf16[16,96,2048]{2,1,0:T(8,128)(2,1)} async-done(((bf16[16,96,2048]{2,1,0:T(8,128)(2,1)}), bf16[16,96,2048]{2,1,0:T(8,128)(2,1)}, u32[]{:S(2)}, u32[]{:S(2)}) %all-to-all-start.3) | async-done | bytes 6291488 | tf_op jit(solution)/shard_map/all_to_all | solution.py:254
  1090.6 10.7 gather_fusion.3
  1108.1 7.1 reduce_sum.184
  1119.2 7.2 convolution_convert_fusion.1
  1141.5 15.5 fusion.8
  1157.1 15.0 fusion.9
  1172.2 14.4 fusion.10
  1203.3 11.8 fusion.127
  1216.3 9.7 fusion.128
  1227.3 10.1 fusion.129
  1238.8 8.1 fusion.71
  1250.5 10.4 fusion.112
  1288.1 83.8 %reduce-scatter.44.cloned.1.call-done = f32[64,16]{1,0:T(8,128)} async-done(((f32[2048,16]{1,0:T(8,128)}), f32[64,16]{1,0:T(8,128)}) %reduce-scatter.44.cloned.1.call-update) | async-done | bytes 4112
  1377.2 37.7 %all-reduce.6 = (f32[2048]{0:T(1024)S(1)}, f32[512]{0:T(512)S(1)}, f32[2048]{0:T(1024)S(1)}) all-reduce(f32[2048]{0:T(1024)S(1)} %get-tuple-element.20, f32[512]{0:T(512)S(1)} %get-tuple-element.22, f32[2048]{0:T(1024)S(1)} %copy-done.62), channel_id=4, replica_groups=mesh['expert'=16,'fsdp'=2] {'expert','fsdp'}, use_global_device_ids=true, to_apply=%region_23.24.clone | all-reduce | flops 4608 | bytes 36864
  1419.0 94.8 %reduce-scatter.22.cloned.1.call-done = f32[64,576]{1,0:T(8,128)} async-done(((f32[2048,576]{1,0:T(8,128)}), f32[64,576]{1,0:T(8,128)}) %reduce-scatter.22.cloned.1.call-update) | async-done | bytes 147472 | tf_op jit(solution)/shard_map/reduce_scatter | solution.py:353
  1513.8 147.7 %reduce-scatter.24.cloned.1.call-done = f32[16,4096]{1,0:T(8,128)} async-done(((f32[512,4096]{1,0:T(8,128)}), f32[16,4096]{1,0:T(8,128)}) %reduce-scatter.24.cloned.1.call-update) | async-done | bytes 262160 | tf_op jit(solution)/shard_map/reduce_scatter | solution.py:355
  1661.5 245.0 %reduce-scatter.28.cloned.1.call-done = f32[64,2816]{1,0:T(8,128)} async-done(((f32[2048,2816]{1,0:T(8,128)}), f32[64,2816]{1,0:T(8,128)}) %reduce-scatter.28.cloned.1.call-update) | async-done | bytes 720912 | tf_op jit(solution)/shard_map/reduce_scatter | solution.py:359
  1906.4 254.4 %reduce-scatter.30.cloned.1.call-done = f32[64,2816]{1,0:T(8,128)} async-done(((f32[2048,2816]{1,0:T(8,128)}), f32[64,2816]{1,0:T(8,128)}) %reduce-scatter.30.cloned.1.call-update) | async-done | bytes 720912 | tf_op jit(solution)/shard_map/reduce_scatter | solution.py:360
  2160.9 254.4 %reduce-scatter.32.cloned.1.call-done = f32[88,2048]{1,0:T(8,128)} async-done(((f32[2816,2048]{1,0:T(8,128)}), f32[88,2048]{1,0:T(8,128)}) %reduce-scatter.32.cloned.1.call-update) | async-done | bytes 720912 | tf_op jit(solution)/shard_map/reduce_scatter | solution.py:361
  2415.3 190.9 %reduce-scatter.26.cloned.1.call-done = f32[64,2048]{1,0:T(8,128)} async-done(((f32[2048,2048]{1,0:T(8,128)}), f32[64,2048]{1,0:T(8,128)}) %reduce-scatter.26.cloned.1.call-update) | async-done | bytes 524304 | tf_op jit(solution)/shard_map/reduce_scatter | solution.py:356
  2606.2 255.2 %reduce-scatter.20.cloned.1.call-done = f32[64,3072]{1,0:T(8,128)} async-done(((f32[2048,3072]{1,0:T(8,128)}), f32[64,3072]{1,0:T(8,128)}) %reduce-scatter.20.cloned.1.call-update) | async-done | bytes 786448 | tf_op jit(solution)/shard_map/reduce_scatter | solution.py:352
  (360 shorter events, 163.8 us)
Async XLA Ops:
  7.2 64.4 %all-gather.13.cloned.1.call-start = ((), (), s32[]{:S(2)}) async-start(), calls=%async_computation.17 | async-start | bytes 2703360 | tf_op jit(solution)/shard_map/all_gather | solution.py:92
  7.9 127.5 %all-gather.15.cloned.1.call-start = ((), (), s32[]{:S(2)}) async-start(), calls=%async_computation.18 | async-start | bytes 4325376 | tf_op jit(solution)/shard_map/all_gather | solution.py:94
  8.7 197.0 %all-gather.17.cloned.1.call-start = ((), (), s32[]{:S(2)}) async-start(), calls=%async_computation.19 | async-start | bytes 3145728 | tf_op jit(solution)/shard_map/all_gather | solution.py:130
  53.5 195.4 %copy-start.36 = (f32[2048]{0:T(1024)}, f32[2048]{0:T(1024)S(1)}, u32[]{:S(2)}) copy-start(f32[2048]{0:T(1024)S(1)} %convert_element_type.181) | copy-start | bytes 24580
  53.5 85.9 %copy-start.48 = (f32[512]{0:T(512)}, f32[512]{0:T(512)S(1)}, u32[]{:S(2)}) copy-start(f32[512]{0:T(512)S(1)} %convert_element_type.183) | copy-start | bytes 6148
  54.8 86.4 %copy-start.79 = (f32[128]{0:T(128)}, f32[128]{0:T(128)S(1)}, u32[]{:S(2)}) copy-start(f32[128]{0:T(128)S(1)} %fusion.64) | copy-start | bytes 1540
  54.8 194.2 %copy-start.58 = (f32[128]{0:T(128)}, f32[128]{0:T(128)S(1)}, u32[]{:S(2)}) copy-start(f32[128]{0:T(128)S(1)} %fusion.102) | copy-start | bytes 1540
  74.6 128.9 %copy-start.19 = (f32[128,576]{0,1:T(8,128)}, f32[128,576]{0,1:T(8,128)S(1)}, u32[]{:S(2)}) copy-start(f32[128,576]{0,1:T(8,128)S(1)} %fusion.116) | copy-start | bytes 884740
  74.7 67.2 %copy-start.81 = (f32[128]{0:T(128)}, f32[128]{0:T(128)S(1)}, u32[]{:S(2)}) copy-start(f32[128]{0:T(128)S(1)} %multiply_reduce_fusion.8) | copy-start | bytes 1540
  74.7 67.2 %copy-start.65 = (f32[128]{0:T(128)}, f32[128]{0:T(128)S(1)}, u32[]{:S(2)}) copy-start(f32[128]{0:T(128)S(1)} %fusion.103) | copy-start | bytes 1540
  139.4 51.2 %copy-start.13 = (bf16[128,2048]{1,0:T(8,128)(2,1)S(1)}, bf16[128,2048]{1,0:T(8,128)(2,1)}, u32[]{:S(2)}) copy-start(bf16[128,2048]{1,0:T(8,128)(2,1)} %param.35) | copy-start | bytes 1572868
  139.4 109.5 %all-gather.19.cloned.1.call-start = ((), (), s32[]{:S(2)}) async-start(), calls=%async_computation.20 | async-start | bytes 12976128 | tf_op jit(solution)/shard_map/all_gather | solution.py:91
  140.0 187.4 %all-gather.21.cloned.1.call-start = ((), (), s32[]{:S(2)}) async-start(), calls=%async_computation.21 | async-start | bytes 8650752 | tf_op jit(solution)/shard_map/all_gather | solution.py:95
  140.6 440.2 %all-gather.33.cloned.1.call-start = ((), (), s32[]{:S(2)}) async-start(), calls=%async_computation.27 | async-start | bytes 8650752 | tf_op jit(solution)/shard_map/all_gather | solution.py:201
  141.2 455.0 %all-gather.31.cloned.1.call-start = ((), (), s32[]{:S(2)}) async-start(), calls=%async_computation.26 | async-start | bytes 8650752 | tf_op jit(solution)/shard_map/all_gather | solution.py:200
  142.0 607.2 %all-gather.29.cloned.1.call-start = ((), (), s32[]{:S(2)}) async-start(), calls=%async_computation.25 | async-start | bytes 8650752 | tf_op jit(solution)/shard_map/all_gather | solution.py:199
  142.7 832.5 %all-gather.27.cloned.1.call-start = ((), (), s32[]{:S(2)}) async-start(), calls=%async_computation.24 | async-start | bytes 11894784 | tf_op jit(solution)/shard_map/all_gather | solution.py:100
  143.4 841.1 %all-gather.25.cloned.1.call-start = ((), (), s32[]{:S(2)}) async-start(), calls=%async_computation.23 | async-start | bytes 11894784 | tf_op jit(solution)/shard_map/all_gather | solution.py:99
  144.0 59.5 %copy-start.72 = (f32[32]{0:T(128)}, f32[32]{0:T(128)S(1)}, u32[]{:S(2)}) copy-start(f32[32]{0:T(128)S(1)} %multiply_exponential_fusion) | copy-start | bytes 388
  144.1 59.5 %copy-start.74 = (f32[128]{0:T(128)}, f32[128]{0:T(128)S(1)}, u32[]{:S(2)}) copy-start(f32[128]{0:T(128)S(1)} %fusion.109) | copy-start | bytes 1540
  150.4 181.9 %copy-start.46 = (f32[2048]{0:T(1024)}, f32[2048]{0:T(1024)S(1)}, u32[]{:S(2)}) copy-start(f32[2048]{0:T(1024)S(1)} %convert_element_type.192) | copy-start | bytes 24580
  190.6 142.7 %copy-start.38 = (bf16[2048,16]{0,1:T(8,128)(2,1)}, bf16[2048,16]{0,1:T(8,128)(2,1)S(1)}, u32[]{:S(2)}) copy-start(bf16[2048,16]{0,1:T(8,128)(2,1)S(1)} %reshape.500) | copy-start | bytes 196612
  203.8 53.8 %copy-start.44 = (f32[128,32]{0,1:T(8,128)}, f32[128,32]{0,1:T(8,128)S(1)}, u32[]{:S(2)}) copy-start(f32[128,32]{0,1:T(8,128)S(1)} %get-tuple-element.54) | copy-start | bytes 49156
  205.6 52.1 %copy-start.42 = (bf16[256,64]{0,1:T(8,128)(2,1)}, bf16[256,64]{0,1:T(8,128)(2,1)S(1)}, u32[]{:S(2)}) copy-start(bf16[256,64]{0,1:T(8,128)(2,1)S(1)} %all_gather.54) | copy-start | bytes 98308
  259.7 72.5 %copy-start.60 = (f32[16,128]{1,0:T(8,128)}, f32[16,128]{1,0:T(8,128)S(1)}, u32[]{:S(2)}) copy-start(f32[16,128]{1,0:T(8,128)S(1)} %fusion.40) | copy-start | bytes 24580
  260.9 71.3 %copy-start.23 = (bf16[16,128,128]{2,1,0:T(8,128)(2,1)}, bf16[16,128,128]{2,1,0:T(8,128)(2,1)S(1)}, u32[]{:S(2)}) copy-start(bf16[16,128,128]{2,1,0:T(8,128)(2,1)S(1)} %convolution_convert_fusion.3) | copy-start | bytes 1572868
  575.4 158.6 %all-to-all-start = ((bf16[16,96,2048]{2,1,0:T(8,128)(2,1)}), bf16[16,96,2048]{2,1,0:T(8,128)(2,1)}, u32[]{:S(2)}, u32[]{:S(2)}) async-start(bf16[16,96,2048]{2,1,0:T(8,128)(2,1)} %get-tuple-element.51), calls=%async_computation | async-start | bytes 12582912 | tf_op jit(solution)/shard_map/all_to_all | solution.py:197
  580.0 411.7 %all-gather.23.cloned.1.call-start = ((), (), s32[]{:S(2)}) async-start(), calls=%async_computation.22 | async-start | bytes 11894784 | tf_op jit(solution)/shard_map/all_gather | solution.py:98
  787.1 55.3 %slice-start.6 = ((s8[5767168]{0:T(1024)(128)(4,1)}), s8[1572864]{0:T(1024)(128)(4,1)S(1)}, s32[]{:S(2)}) async-start(s8[5767168]{0:T(1024)(128)(4,1)} %bitcast.241), calls=%async_computation.47 | async-start | bytes 3145728
  787.1 157.5 %all-to-all-start.1 = ((bf16[16,96,2048]{2,1,0:T(8,128)(2,1)}), bf16[16,96,2048]{2,1,0:T(8,128)(2,1)}, u32[]{:S(2)}, u32[]{:S(2)}) async-start(bf16[16,96,2048]{2,1,0:T(8,128)(2,1)} %fusion.23), calls=%async_computation.1 | async-start | bytes 12582912 | tf_op jit(solution)/shard_map/all_to_all | solution.py:215
  857.5 117.5 %copy-start.14 = (bf16[128,2048]{1,0:T(8,128)(2,1)S(1)}, bf16[128,2048]{1,0:T(8,128)(2,1)}, u32[]{:S(2)}) copy-start(bf16[128,2048]{1,0:T(8,128)(2,1)} %param.35) | copy-start | bytes 1572868
  857.5 117.6 %copy-start.64 = (s32[768]{0:T(1024)S(1)}, s32[768]{0:T(1024)}, u32[]{:S(2)}) copy-start(s32[768]{0:T(1024)} %copy-done.63) | copy-start | bytes 9220
  944.6 146.0 %all-to-all-start.3 = ((bf16[16,96,2048]{2,1,0:T(8,128)(2,1)}), bf16[16,96,2048]{2,1,0:T(8,128)(2,1)}, u32[]{:S(2)}, u32[]{:S(2)}) async-start(bf16[16,96,2048]{2,1,0:T(8,128)(2,1)} %add_convert_fusion), calls=%async_computation.3 | async-start | bytes 12582912 | tf_op jit(solution)/shard_map/all_to_all | solution.py:254
  974.7 213.4 %reduce-scatter.42.cloned.1.call-start = ((), (), s32[]{:S(2)}) async-start(), calls=%async_computation.39 | async-start | bytes 98304
  1136.8 52.5 %reduce-scatter.40.cloned.1.call-start = ((), (), s32[]{:S(2)}) async-start(), calls=%async_computation.38 | async-start | bytes 3145728
  1141.5 119.5 %reduce-scatter.34.cloned.1.call-start = ((), (), s32[]{:S(2)}) async-start(), calls=%async_computation.35 | async-start | bytes 8650752 | tf_op jit(solution)/shard_map/reduce_scatter | solution.py:263
  1157.1 108.6 %reduce-scatter.36.cloned.1.call-start = ((), (), s32[]{:S(2)}) async-start(), calls=%async_computation.36 | async-start | bytes 8650752 | tf_op jit(solution)/shard_map/reduce_scatter | solution.py:266
  1172.2 98.3 %reduce-scatter.38.cloned.1.call-start = ((), (), s32[]{:S(2)}) async-start(), calls=%async_computation.37 | async-start | bytes 8650752 | tf_op jit(solution)/shard_map/reduce_scatter | solution.py:269
  1186.7 185.2 %reduce-scatter.44.cloned.1.call-start = ((), (), s32[]{:S(2)}) async-start(), calls=%async_computation.40 | async-start | bytes 1081344
  1188.1 325.7 %reduce-scatter.22.cloned.1.call-start = ((), (), s32[]{:S(2)}) async-start(), calls=%async_computation.29 | async-start | bytes 5406720 | tf_op jit(solution)/shard_map/reduce_scatter | solution.py:353
  1197.5 463.9 %reduce-scatter.24.cloned.1.call-start = ((), (), s32[]{:S(2)}) async-start(), calls=%async_computation.30 | async-start | bytes 8650752 | tf_op jit(solution)/shard_map/reduce_scatter | solution.py:355
  1202.3 704.2 %reduce-scatter.28.cloned.1.call-start = ((), (), s32[]{:S(2)}) async-start(), calls=%async_computation.32 | async-start | bytes 23789568 | tf_op jit(solution)/shard_map/reduce_scatter | solution.py:359
  1215.1 945.7 %reduce-scatter.30.cloned.1.call-start = ((), (), s32[]{:S(2)}) async-start(), calls=%async_computation.33 | async-start | bytes 23789568 | tf_op jit(solution)/shard_map/reduce_scatter | solution.py:360
  1226.0 1189.3 %reduce-scatter.32.cloned.1.call-start = ((), (), s32[]{:S(2)}) async-start(), calls=%async_computation.34 | async-start | bytes 23789568 | tf_op jit(solution)/shard_map/reduce_scatter | solution.py:361
  1237.5 1368.8 %reduce-scatter.26.cloned.1.call-start = ((), (), s32[]{:S(2)}) async-start(), calls=%async_computation.31 | async-start | bytes 17301504 | tf_op jit(solution)/shard_map/reduce_scatter | solution.py:356
  1246.9 1614.5 %reduce-scatter.20.cloned.1.call-start = ((), (), s32[]{:S(2)}) async-start(), calls=%async_computation.28 | async-start | bytes 25952256 | tf_op jit(solution)/shard_map/reduce_scatter | solution.py:352
  1282.7 94.5 %copy-start.62 = (f32[2048]{0:T(1024)S(1)}, f32[2048]{0:T(1024)}, u32[]{:S(2)}) copy-start(f32[2048]{0:T(1024)} %get-tuple-element.18) | copy-start | bytes 24580
  1282.7 133.9 %copy-start.80 = (f32[128]{0:T(128)S(1)}, f32[128]{0:T(128)}, u32[]{:S(2)}) copy-start(f32[128]{0:T(128)} %copy-done.79) | copy-start | bytes 1540
  (71 other events, 570.7 us)
Sparse Core Ops, SparseCore 0:
  10.8 60.6 all-gather.12
  74.4 60.9 all-gather.14
  139.5 9.1 all-gather.16
  151.4 97.4 all-gather.18
  251.7 75.6 all-gather.20
  328.8 14.6 all-gather.32
  345.0 17.1 all-gather.30
  363.7 17.1 all-gather.28
  383.8 157.6 all-gather.26
  544.2 178.6 all-gather.24
  725.7 106.3 all-gather.22
  1136.9 30.4 reduce-scatter.41
  1169.6 10.7 reduce-scatter.39
  1183.2 15.0 reduce-scatter.33
  1201.0 15.0 reduce-scatter.35
  1218.3 15.0 reduce-scatter.37
  1235.5 136.3 reduce-scatter.43
  1374.8 138.9 reduce-scatter.21
  1516.8 144.6 reduce-scatter.23
  1664.3 242.0 reduce-scatter.27
  1909.4 251.4 reduce-scatter.29
  2163.9 251.3 reduce-scatter.31
  2418.3 187.9 reduce-scatter.25
  2614.2 247.1 reduce-scatter.19
where the time goes:
time: 2880 us; the launch traced here: 2870 us
  waiting for transfers between devices  1990 us (69%)
  blocking collectives  327 us (11%)
  matrix products  302 us (10%)
  local copies, waits for them, and re-layouts  104 us (4%)
  starting transfers between devices  75.1 us (3%)
  other arithmetic  52.3 us (2%)
    reduce_scatter x1, waiting for transfers between devices, body(): lax.psum_scatter(query_weight_grad, ('expert', 'fsdp'), scatter_dimension...  255 us
    reduce_scatter x1, waiting for transfers between devices, body(): lax.psum_scatter(shared_up_grad, ('expert', 'fsdp'), scatter_dimension=0,...  254 us
    reduce_scatter x1, waiting for transfers between devices, body(): lax.psum_scatter(shared_down_grad, ('expert', 'fsdp'), scatter_dimension=...  254 us
    reduce_scatter x1, waiting for transfers between devices, body(): lax.psum_scatter(shared_gate_grad, ('expert', 'fsdp'), scatter_dimension=...  245 us
    all_to_all x1, blocking collectives, body(): lax.all_to_all(send_grad, 'expert', split_axis=0, concat_axis=0, tiled=True)  206 us
    reduce_scatter x1, waiting for transfers between devices, body(): lax.psum_scatter(output_weight_grad, ('expert', 'fsdp'), scatter_dimensio...  191 us
    reduce_scatter x1, waiting for transfers between devices, body(): lax.psum_scatter(expand_weight_grad, ('expert', 'fsdp'), scatter_dimensio...  148 us
    all_to_all x1, waiting for transfers between devices, body(): lax.all_to_all(send_rows, 'expert', split_axis=0, concat_axis=0, tiled=True)  138 us
  transfers between devices with their start and end apart: 27, of which 15 were waited for; matrix products, arithmetic and copies ran while one was open for 14% of the time, Pallas kernels for 0%

commit v1 on v0

v1 whole, which is shorter than its diff:
```python
import math

import jax
import jax.numpy as jnp
from jax import lax
from jax.sharding import PartitionSpec as P

D = 2048
H = 16
DN = 128
DR = 64
DV = 128
KVR = 512
TOPK = 6
SEQ_DEV = 128

NORM_EPS = 1e-06
ROPE_THETA = 50000.0
GATE_SCALE = 2.446

BF16 = jnp.bfloat16
F32 = jnp.float32
BOTH = ("expert", "fsdp")

ORDER_QUERY = ((8, 4, 2, 1), (8, 1, 2, 4))
ORDER_OUTPUT = (1, 8, 4, 2)
ORDER_EXPAND = (8, 4, 2, 1)
ORDER_LATENT = (4, 8, 2, 1)
ORDER_SMALL = (1, 2, 4, 8)
ORDER_TOKENS = ((1, 8), (8, 1), (4, 2), (2, 4))
BACK_QUERY = ((2, 4, 8, 1), (4, 1, 2, 8))
BACK_OUTPUT = (1, 2, 4, 8)
BACK_EXPAND = (4, 2, 1, 8)
BACK_LATENT = (1, 2, 4, 8)


def rms_scale(values, gain_vec):
    return (
        values * lax.rsqrt(jnp.mean(values * values, axis=-1, keepdims=True) + NORM_EPS) * gain_vec
    )


def rotate(values, cos_table, sin_table):
    middle = values.shape[-1] // 2
    lower_half = values[..., :middle]
    upper_half = values[..., middle:]
    return jnp.concatenate(
        [
            lower_half * cos_table - upper_half * sin_table,
            upper_half * cos_table + lower_half * sin_table,
        ],
        axis=-1,
    )


def rope_tables(positions):
    steps_float = jnp.arange(DR // 2).astype(F32) * (2.0 / DR)
    inverse = jnp.exp(-steps_float * math.log(ROPE_THETA))
    turned = positions.astype(F32)[:, None] * inverse[None, :]
    return (jnp.cos(turned), jnp.sin(turned))


def product(left_side, right_side):
    return jnp.dot(left_side, right_side, preferred_element_type=F32)


def inner_rows(left_side, right_side):
    return lax.dot_general(
        left_side, right_side, (((0,), (0,)), ((), ())), preferred_element_type=F32
    )


def outer_cols(left_side, right_side):
    return lax.dot_general(
        left_side, right_side, (((1,), (1,)), ((), ())), preferred_element_type=F32
    )


def swiglu(gate_act, up_act):
    return jax.nn.silu(gate_act) * up_act


def after(value, *earlier):
    return lax.optimization_barrier((value, *earlier))[0]


class Chips:
    def __init__(self):
        self.n = lax.axis_size("expert")
        self.f = lax.axis_size("fsdp")
        self.chip = lax.axis_index("expert")
        self.core = lax.axis_index("fsdp")

    def bits(self, order):
        return tuple(m for m in order if (m if isinstance(m, int) else m[0]) < self.n)

    def exchange(self, value, mask):
        masks = (mask,) if isinstance(mask, int) else mask
        pairs = [
            (e * self.f + c, (e ^ masks[c % len(masks)]) * self.f + c)
            for e in range(self.n)
            for c in range(self.f)
        ]
        return lax.ppermute(value, BOTH, pairs)

    def other_core(self, value):
        return lax.ppermute(value, "fsdp", [(0, 1), (1, 0)])

    def gather_cores(self, value, axis=0):
        if self.f != 2:
            return lax.all_gather(value, "fsdp", axis=axis, tiled=True)
        other = self.other_core(value)
        first = self.core == 0
        return jnp.concatenate(
            [jnp.where(first, value, other), jnp.where(first, other, value)], axis=axis
        )

    def swap_cores(self, value, split, concat):
        if self.f != 2:
            return lax.all_to_all(value, "fsdp", split_axis=split, concat_axis=concat, tiled=True)
        size = value.shape[split] // 2
        keep = lax.dynamic_slice_in_dim(value, self.core * size, size, split)
        send = lax.dynamic_slice_in_dim(value, (1 - self.core) * size, size, split)
        other = self.other_core(send)
        first = self.core == 0
        return jnp.concatenate(
            [jnp.where(first, keep, other), jnp.where(first, other, keep)], axis=concat
        )

    def sum_cores(self, value):
        if self.f != 2:
            return lax.psum(value, "fsdp")
        return value + self.other_core(value)

    def scatter_cores(self, value):
        if self.f != 2:
            return lax.psum_scatter(value, "fsdp", scatter_dimension=0, tiled=True)
        size = value.shape[0] // 2
        keep = lax.dynamic_slice_in_dim(value, self.core * size, size, 0)
        send = lax.dynamic_slice_in_dim(value, (1 - self.core) * size, size, 0)
        return keep + self.other_core(send)

    def gather_chips(self, value, order):
        done = []
        for mask in self.bits(order):
            other = self.exchange(value, mask)
            place = sum(m > mask for m in done)
            high = (self.chip // mask) % 2 == 1
            value = jnp.stack(
                [jnp.where(high, other, value), jnp.where(high, value, other)], axis=place
            )
            done.append(mask)
        return value.reshape((self.n,) + value.shape[len(done) :])

    def halves(self, value, axis, mask):
        high = (self.chip // mask) % 2
        shape = value.shape
        split = value.reshape(
            shape[:axis] + (self.n // (2 * mask), 2, mask) + shape[axis + 1 :]
        )
        parts = [
            lax.dynamic_index_in_dim(split, bit, axis + 1, keepdims=False).reshape(
                shape[:axis] + (self.n // 2,) + shape[axis + 1 :]
            )
            for bit in (high, 1 - high)
        ]
        return parts

    def scatter_chips(self, value, order, done=()):
        left = [m for m in sorted(self.bits((8, 4, 2, 1)), reverse=True) if m not in done]
        for mask in self.bits(order):
            if mask in done:
                continue
            place = left.index(mask)
            high = (self.chip // mask) % 2
            rest = value.shape[1:]
            split = value.reshape((2,) * len(left) + rest)
            keep = lax.dynamic_index_in_dim(split, high, place, keepdims=False)
            send = lax.dynamic_index_in_dim(split, 1 - high, place, keepdims=False)
            left.remove(mask)
            other = self.exchange(send, mask)
            value = keep.astype(F32) + other.astype(F32)
            if left:
                value = value.astype(send.dtype)
            value = value.reshape((2 ** len(left),) + rest)
        return value[0]

    def weight_grad(self, rows, grads, order):
        mask = self.bits(order)[0]
        keep, send = self.halves(rows, 1, mask)
        count, width = keep.shape[1:]
        tokens = keep.shape[0]
        away = inner_rows(send.reshape(tokens, -1), grads).astype(BF16)
        other = self.exchange(away, mask)
        value = inner_rows(keep.reshape(tokens, -1), grads) + other.astype(F32)
        value = value.astype(BF16).reshape(count, width, -1)
        return self.scatter_chips(value, order, (mask,))

    def gather_tokens(self, value, order):
        order = self.bits(order)
        value = value[None]
        for masks in order[:-1]:
            value = jnp.concatenate([value, self.exchange(value, masks)], axis=0)
        return value, self.exchange(value, order[-1])

    def scatter_tokens(self, value, other, order):
        order = self.bits(order)
        value = value.astype(F32) + other.astype(F32)
        for masks in reversed(order[:-1]):
            half = value.shape[0] // 2
            value = value.astype(other.dtype)
            value = value[:half].astype(F32) + self.exchange(value[half:], masks).astype(F32)
        return value[0]


def body(
    tokens,
    segments,
    routes,
    norm_attn,
    query_proj,
    latent_proj,
    norm_latent,
    expand_proj,
    output_proj,
    norm_ffn,
    router,
    shared_gate,
    shared_up,
    shared_down,
    expert_gate,
    expert_up,
    expert_down,
    cotangent,
):
    chips = Chips()
    n, cores, chip, core = chips.n, chips.f, chips.chip, chips.core
    seq = SEQ_DEV * cores
    heads = H // cores
    shard = D // (n * cores)
    expert_count = n * expert_gate.shape[0]
    small_cut = (shard, 2 * shard, 2 * shard + norm_latent.shape[0])

    small = jnp.concatenate([norm_attn, norm_ffn, norm_latent, router.reshape(-1)])[None]
    small = chips.gather_chips(chips.gather_cores(small), ORDER_SMALL).reshape(n * cores, -1)
    gain_attn = small[:, : small_cut[0]].reshape(-1).astype(F32)
    gain_ffn = small[:, small_cut[0] : small_cut[1]].reshape(-1).astype(F32)
    gain_latent = small[:, small_cut[1] : small_cut[2]].reshape(-1).astype(F32)
    router_all = small[:, small_cut[2] :].reshape(D, -1)

    latent_own = chips.gather_chips(latent_proj, ORDER_LATENT)
    latent_weight = lax.all_gather(latent_own[:, None], "fsdp", axis=1, tiled=True).reshape(D, -1)
    query_own = chips.swap_cores(query_proj, 1, 0)
    query_cut = query_own.shape[1] // 2
    query_parts = [
        chips.gather_chips(part, order).reshape(D, -1)
        for part, order in zip((query_own[:, :query_cut], query_own[:, query_cut:]), ORDER_QUERY)
    ]
    expand_own = chips.swap_cores(expand_proj, 1, 0)
    expand_weight = chips.gather_chips(expand_own, ORDER_EXPAND).reshape(KVR, -1)
    output_own = chips.gather_chips(output_proj, ORDER_OUTPUT)
    output_weight = lax.all_gather(output_own[:, None], "fsdp", axis=1, tiled=True).reshape(-1, D)

    width = shared_gate.shape[1] // n
    shared_in = jnp.stack([shared_gate.reshape(shard, n, -1), shared_up.reshape(shard, n, -1)], 2)
    shared_in = lax.all_to_all(
        shared_in.transpose(1, 0, 2, 3).reshape(n * shard, 2 * width),
        "expert",
        split_axis=0,
        concat_axis=0,
        tiled=True,
    ).reshape(n, 1, shard, 2 * width)
    shared_in = lax.all_gather(shared_in, "fsdp", axis=1, tiled=True).reshape(D, 2 * width)
    shared_down_w = chips.gather_cores(shared_down)
    gate_full = lax.all_gather(expert_gate[0], "fsdp", axis=0, tiled=True)
    up_full = lax.all_gather(expert_up[0], "fsdp", axis=0, tiled=True)
    down_full = lax.all_gather(expert_down[0], "fsdp", axis=0, tiled=True)

    positions = jnp.arange(seq, dtype=jnp.int32)
    cos_table, sin_table = rope_tables(positions)
    inputs_f = tokens.astype(F32)
    normed_own = rms_scale(inputs_f, gain_attn).astype(BF16)
    normed = chips.gather_cores(normed_own)
    query_all = jnp.concatenate([product(normed, part) for part in query_parts], axis=1)
    query_all = query_all.reshape(seq, heads, DN + DR)
    query_nope = query_all[..., :DN].astype(BF16)
    query_rope = rotate(query_all[..., DN:], cos_table[:, None, :], sin_table[:, None, :]).astype(
        BF16
    )
    latent = product(normed, latent_weight)
    latent_norm = rms_scale(latent[:, :KVR], gain_latent).astype(BF16)
    key_rope = rotate(latent[:, KVR:], cos_table, sin_table).astype(BF16)
    expanded = product(latent_norm, expand_weight).astype(BF16).reshape(seq, heads, DN + DV)
    key_nope = expanded[..., :DN]
    values_all = expanded[..., DN:]
    allowed = (positions[:, None] >= positions[None, :]) & (segments[:, None] == segments[None, :])
    score_scale = (DN + DR) ** (-0.5)
    scores = jnp.einsum("thd,shd->hts", query_nope, key_nope, preferred_element_type=F32)
    scores = scores + jnp.einsum("thd,sd->hts", query_rope, key_rope, preferred_element_type=F32)
    scores = jnp.where(allowed[None], scores * score_scale, -1e30)
    shifted = jnp.exp(scores - jnp.max(scores, axis=-1, keepdims=True))
    probs = shifted / jnp.sum(shifted, axis=-1, keepdims=True)
    probs_low = probs.astype(BF16)
    attended = jnp.einsum("hts,shd->thd", probs_low, values_all, preferred_element_type=F32)
    attended = attended.reshape(seq, heads * DV).astype(BF16)
    attended = chips.gather_cores(attended, axis=1)
    attended_own = lax.dynamic_slice_in_dim(attended, core * SEQ_DEV, SEQ_DEV, 0)
    hidden = inputs_f + product(attended_own, output_weight)
    normed_ffn = rms_scale(hidden, gain_ffn).astype(BF16)

    parts = chips.gather_tokens(normed_ffn, ORDER_TOKENS)
    routes_all = jnp.concatenate(chips.gather_tokens(routes, ORDER_TOKENS), axis=0)
    cot_first, cot_last = chips.gather_tokens(cotangent, ORDER_TOKENS)
    logits = product(normed_ffn, router_all)
    route_hot = (
        routes[:, :, None] == jnp.arange(expert_count, dtype=jnp.int32)[None, None, :]
    ).astype(F32)

    def gate_values(logit_in):
        chosen = jnp.sum(route_hot * jax.nn.sigmoid(logit_in)[:, None, :], axis=2)
        return GATE_SCALE * chosen / jnp.sum(chosen, axis=1, keepdims=True)

    gate_weights, gate_pull = jax.vjp(gate_values, logits)
    gate_dense = jnp.sum(route_hot * gate_weights[:, :, None], axis=1)
    gate_all = jnp.concatenate(chips.gather_tokens(gate_dense, ORDER_TOKENS), axis=0)
    gate_here = lax.dynamic_index_in_dim(gate_all, chip, 2, keepdims=False)
    capacity = 2 * SEQ_DEV * TOPK // expert_count
    named = jnp.any(routes_all == chip, axis=2)
    rank = jnp.cumsum(named.astype(jnp.int32), axis=1) - 1
    slot_hot = (
        (rank[:, None, :] == jnp.arange(capacity, dtype=jnp.int32)[None, :, None])
        & named[:, None, :]
    ).astype(BF16)
    half = n // 2

    def pick(hot, rows):
        return (
            jnp.einsum("bct,btd->bcd", hot, rows, preferred_element_type=F32)
            .astype(BF16)
            .reshape(half * capacity, D)
        )

    def place(hot, rows):
        return jnp.einsum(
            "bct,bcd->btd", hot, rows.reshape(half, capacity, D), preferred_element_type=F32
        ).reshape(half * SEQ_DEV, D)

    def forward(rows, cot, hot, gate):
        source = pick(hot, rows)
        cot_slots = pick(hot, cot).astype(F32)
        gate_slots = jnp.sum(hot.astype(F32) * gate[:, None, :], axis=2).reshape(-1, 1)
        gate_act = product(source, gate_full)
        up_act = product(source, up_full)
        hidden_act = swiglu(gate_act, up_act).astype(BF16)
        slots_out = product(hidden_act, down_full).astype(BF16).astype(F32)
        grad_slots = jnp.sum(slots_out * cot_slots, axis=1).reshape(half, capacity, 1)
        grad_gate = jnp.sum(hot.astype(F32) * grad_slots, axis=1)
        flat = rows.reshape(-1, D)
        shared_act = product(flat, shared_in)
        shared_hidden = swiglu(shared_act[:, :width], shared_act[:, width:]).astype(BF16)
        out = place(hot, (slots_out * gate_slots).astype(BF16))
        out = (out + product(shared_hidden, shared_down_w)).astype(BF16)
        cot_flat = cot.reshape(-1, D)
        hidden_back = outer_cols((gate_slots * cot_slots).astype(BF16), down_full)
        shared_back = outer_cols(cot_flat, shared_down_w)
        kept = (
            source, (gate_slots * cot_slots).astype(BF16), gate_act, up_act, hidden_act, flat,
            cot_flat, shared_act, shared_hidden, hidden_back, shared_back,
        )
        return out, grad_gate, kept

    def backward(hot, kept):
        gate_act, up_act, shared_act, hidden_back, shared_back = (kept[i] for i in (2, 3, 7, 9, 10))
        _, pull = jax.vjp(swiglu, gate_act, up_act)
        gate_back, up_back = (v.astype(BF16) for v in pull(hidden_back))
        source_back = outer_cols(gate_back, gate_full) + outer_cols(up_back, up_full)
        _, shared_pull = jax.vjp(swiglu, shared_act[:, :width], shared_act[:, width:])
        acts_back = jnp.concatenate(shared_pull(shared_back), axis=1).astype(BF16)
        back = place(hot, source_back.astype(BF16)) + outer_cols(acts_back, shared_in)
        return back.astype(BF16), gate_back, up_back, acts_back

    out_first, gate_first, kept_first = forward(
        parts[0], cot_first, slot_hot[:half], gate_here[:half]
    )
    out_last, gate_last, kept_last = forward(parts[1], cot_last, slot_hot[half:], gate_here[half:])
    back_last, *acts_last = backward(slot_hot[half:], kept_last)
    sent_back = chips.exchange(back_last, chips.bits(ORDER_TOKENS)[-1])
    back_first, *acts_first = backward(slot_hot[:half], kept_first)
    shape = (half, SEQ_DEV, D)
    ffn_grad = chips.scatter_tokens(
        back_first.reshape(shape), sent_back.reshape(shape), ORDER_TOKENS
    )
    sent_out = chips.exchange(out_last, chips.bits(ORDER_TOKENS)[-1])
    block_sum = chips.scatter_tokens(out_first.reshape(shape), sent_out.reshape(shape), ORDER_TOKENS)
    block_out = (hidden + block_sum).astype(BF16)

    hot_expert = (jnp.arange(expert_count, dtype=jnp.int32) == chip).astype(F32)
    gate_first = gate_first[..., None] * hot_expert
    gate_last = gate_last[..., None] * hot_expert
    gate_sum = chips.scatter_tokens(
        gate_first, chips.exchange(gate_last, chips.bits(ORDER_TOKENS)[-1]), ORDER_TOKENS
    )
    gate_grad = jnp.sum(route_hot * gate_sum[:, None, :], axis=2)
    logit_grad = gate_pull(gate_grad)[0].astype(BF16)
    router_grad = inner_rows(normed_ffn, logit_grad)
    ffn_grad = ffn_grad + outer_cols(logit_grad, router_all)

    def joined(i):
        return jnp.concatenate([kept_first[i], kept_last[i]], axis=0)

    def joined_acts(i):
        return jnp.concatenate([acts_first[i], acts_last[i]], axis=0)

    def expert_grad(rows, grads):
        return lax.psum_scatter(
            inner_rows(rows, grads).astype(BF16), "fsdp", scatter_dimension=0, tiled=True
        ).astype(F32)[None]

    source, slots_grad, hidden_act = joined(0), joined(1), joined(4)
    gate_grad_w = expert_grad(source, joined_acts(0))
    up_grad_w = expert_grad(source, joined_acts(1))
    down_grad_w = expert_grad(hidden_act, slots_grad)
    shared_in_grad = inner_rows(joined(5), joined_acts(2)).astype(BF16)
    shared_in_grad = lax.all_to_all(
        shared_in_grad, BOTH, split_axis=0, concat_axis=0, tiled=True
    ).reshape(n, cores, shard, 2, width)
    shared_in_grad = jnp.sum(shared_in_grad.astype(F32), axis=1).transpose(2, 1, 0, 3)
    shared_in_grad = shared_in_grad.reshape(2, shard, n * width)
    shared_down_grad = chips.scatter_cores(inner_rows(joined(8), joined(6)))

    _, norm_pull = jax.vjp(rms_scale, hidden, gain_ffn)
    hidden_part, gain_ffn_grad = norm_pull(ffn_grad)
    hidden_grad = cotangent.astype(F32) + hidden_part
    attn_grad_own = hidden_grad.astype(BF16)
    attn_grad = chips.gather_cores(attn_grad_own)
    attended_grad = chips.swap_cores(
        outer_cols(attn_grad_own, output_weight).astype(BF16), 1, 0
    ).reshape(seq, heads, DV)
    attended_part = lax.dynamic_index_in_dim(
        attended.reshape(seq, n, cores, shard), core, 2, keepdims=False
    )
    output_grad = chips.weight_grad(attended_part, attn_grad, BACK_OUTPUT)
    prob_grad = jnp.einsum("thd,shd->hts", attended_grad, values_all, preferred_element_type=F32)
    weighted = jnp.sum(probs * prob_grad, axis=-1, keepdims=True)
    score_grad = (probs * (prob_grad - weighted)).astype(BF16)
    query_nope_grad = score_scale * jnp.einsum(
        "hts,shd->thd", score_grad, key_nope, preferred_element_type=F32
    )
    query_rope_grad = score_scale * jnp.einsum(
        "hts,sd->thd", score_grad, key_rope, preferred_element_type=F32
    )
    key_nope_grad = score_scale * jnp.einsum(
        "hts,thd->shd", score_grad, query_nope, preferred_element_type=F32
    )
    key_rope_grad = score_scale * jnp.einsum(
        "hts,thd->sd", score_grad, query_rope, preferred_element_type=F32
    )
    values_grad = jnp.einsum(
        "hts,thd->shd", probs_low, attended_grad, preferred_element_type=F32
    )
    expanded_grad = jnp.concatenate([key_nope_grad, values_grad], axis=2)
    expanded_grad = expanded_grad.reshape(seq, heads * (DN + DV)).astype(BF16)
    latent_back = chips.sum_cores(
        jnp.concatenate([outer_cols(expanded_grad, expand_weight), key_rope_grad], axis=1)
    )
    _, latent_pull = jax.vjp(rms_scale, latent[:, :KVR], gain_latent)
    latent_nope_grad, gain_latent_grad = latent_pull(latent_back[:, :KVR])
    gain_latent_grad = gain_latent_grad / cores
    latent_rope_grad = rotate(latent_back[:, KVR:], cos_table, -sin_table)
    latent_grad = jnp.concatenate([latent_nope_grad, latent_rope_grad], axis=1).astype(BF16)
    query_back = jnp.concatenate(
        [query_nope_grad, rotate(query_rope_grad, cos_table[:, None, :], -sin_table[:, None, :])],
        axis=2,
    )
    query_back = query_back.reshape(seq, heads * (DN + DR)).astype(BF16)

    normed_chips = normed.reshape(seq, n, D // n)
    query_grad = jnp.concatenate(
        [
            chips.weight_grad(normed_chips, part, order)
            for part, order in zip(
                (query_back[:, :query_cut], query_back[:, query_cut:]), BACK_QUERY
            )
        ],
        axis=1,
    )
    query_grad = chips.swap_cores(query_grad, 0, 1)
    expand_grad = chips.weight_grad(latent_norm.reshape(seq, n, KVR // n), expanded_grad, BACK_EXPAND)
    expand_grad = chips.swap_cores(expand_grad, 0, 1)
    normed_part = lax.dynamic_index_in_dim(
        normed.reshape(seq, n, cores, shard), core, 2, keepdims=False
    )
    latent_weight_grad = chips.weight_grad(normed_part, latent_grad, BACK_LATENT)

    normed_grad = outer_cols(query_back[:, :query_cut], query_parts[0]) + outer_cols(
        query_back[:, query_cut:], query_parts[1]
    )
    latent_grad_own = lax.dynamic_slice_in_dim(latent_grad, core * SEQ_DEV, SEQ_DEV, 0)
    normed_grad = chips.scatter_cores(normed_grad) + outer_cols(latent_grad_own, latent_weight)
    _, first_pull = jax.vjp(rms_scale, inputs_f, gain_attn)
    input_part, gain_attn_grad = first_pull(normed_grad)
    tokens_grad = (hidden_grad + input_part).astype(BF16)

    small_grad = jnp.concatenate(
        [
            gain_attn_grad.reshape(n * cores, -1),
            gain_ffn_grad.reshape(n * cores, -1),
            gain_latent_grad.reshape(n * cores, -1),
            router_grad.reshape(n * cores, -1),
        ],
        axis=1,
    )
    small_grad = chips.scatter_chips(small_grad.reshape(n, cores, -1), ORDER_SMALL[::-1])
    small_grad = chips.scatter_cores(small_grad).reshape(-1)
    return (
        block_out,
        tokens_grad,
        small_grad[: small_cut[0]],
        query_grad,
        latent_weight_grad,
        small_grad[small_cut[1] : small_cut[2]],
        expand_grad,
        output_grad,
        small_grad[small_cut[0] : small_cut[1]],
        small_grad[small_cut[2] :].reshape(shard, -1),
        shared_in_grad[0],
        shared_in_grad[1],
        shared_down_grad,
        gate_grad_w,
        up_grad_w,
        down_grad_w,
    )


def solution(mesh):
    rows = P(("expert", "fsdp"), None)
    flat = P(("expert", "fsdp"))
    experts = P("expert", "fsdp", None)
    return jax.shard_map(
        body,
        mesh=mesh,
        in_specs=(
            rows, P("expert"), rows, flat, rows, rows, flat, rows, rows, flat, rows, rows, rows,
            rows, experts, experts, experts, rows,
        ),
        out_specs=(
            rows, rows, flat, rows, rows, flat, rows, rows, flat, rows, rows, rows, rows, experts,
            experts, experts,
        ),
        check_vma=False,
    )
```

time: 2880 us -> 1170 us (0.41)
  waiting for transfers between devices: 1990 us -> 542 us
  blocking collectives: 327 us -> 0 us
  other arithmetic: 52.3 us -> 117 us
  starting transfers between devices: 75.1 us -> 113 us
  matrix products: 302 us -> 265 us
    reduce_scatter x10 -> x3, waiting for transfers between devices: 1440 us -> 0.02 us  [expert_grad(): lax.psum_scatter(inner_rows(rows, grads).astype(BF16), 'fsdp', scatter_di...]
    ppermute x0 -> x90, waiting for transfers between devices: none -> 541 us  [the longest x76 538 us: exchange(): return lax.ppermute(value, BOTH, pairs)]
    all_to_all x3 -> x2, waiting for transfers between devices: 277 us -> 0.01 us  [the longest x1 0.01 us: body(): lax.all_to_all(shared_in_grad, BOTH, split_axis=0, concat_axis=0, tiled=T...]
    all_to_all x1 -> x0, blocking collectives: 206 us -> none  [body(): lax.all_to_all(send_grad, 'expert', split_axis=0, concat_axis=0, tiled=True)]
    all_gather x11 -> x6, waiting for transfers between devices: 182 us -> 0.05 us  [the longest x1 0.02 us: body(): lax.all_gather(output_own[:, None], 'fsdp', axis=1, tiled=True)]
    ppermute x0 -> x90, starting transfers between devices: none -> 102 us  [the longest x76 92.1 us: exchange(): return lax.ppermute(value, BOTH, pairs)]
    unnamed x27 -> x9, waiting for transfers between devices: 90.4 us -> 1.32 us
    unnamed x2 -> x0, blocking collectives: 80 us -> none
  transfers between devices with their start and end apart: 27 -> 101, of which waited for: 15 -> 55; matrix products, arithmetic and copies ran while one was open for 14% -> 41% of each run, Pallas kernels for 0% -> 0%
where the time goes in v1:
time: 1170 us; the launch traced here: 1160 us
  waiting for transfers between devices  542 us (46%)
  matrix products  265 us (23%)
  other arithmetic  117 us (10%)
  starting transfers between devices  113 us (10%)
  local copies, waits for them, and re-layouts  106 us (9%)
  between operations  17.3 us (1%)
    ppermute x76, waiting for transfers between devices, exchange(): return lax.ppermute(value, BOTH, pairs)  538 us
    ppermute x76, starting transfers between devices, exchange(): return lax.ppermute(value, BOTH, pairs)  92.1 us
    dot_general x16, matrix products, outer_cols(): lax.dot_general(left_side, right_side, (((1,), (1,)), ((), ())), preferre...  80.9 us
    dot_general x16, matrix products, product(): return jnp.dot(left_side, right_side, preferred_element_type=F32)  75.1 us
    dot_general x16, matrix products, inner_rows(): lax.dot_general(left_side, right_side, (((0,), (0,)), ((), ())), preferre...  69.2 us
  transfers between devices with their start and end apart: 101, of which 55 were waited for; matrix products, arithmetic and copies ran while one was open for 41% of the time, Pallas kernels for 0%

profile of v1, /device:TPU:0, one launch (start us, length us, event | category | flops | bytes accessed | tf_op | source)
XLA Modules:
  0.0 1160.3 jit_solution(5187885800912314543)
XLA Ops:
  22.3 10.6 collective-permute-done.6
  36.2 11.5 collective-permute-done.26
  51.9 7.1 collective-permute-done.8
  60.5 12.2 %collective-permute-done.27 = bf16[2,2,64,2048]{3,2,1,0:T(8,128)(2,1)} collective-permute-done((bf16[2,2,64,2048]{3,2,1,0:T(8,128)(2,1)S(1)}, bf16[2,2,64,2048]{3,2,1,0:T(8,128)(2,1)}, u32[]{:S(2)}, u32[]{:S(2)}) %collective-permute-start.27) | collective-permute-done | bytes 1048608 | tf_op jit(solution)/shard_map/ppermute | solution.py:104
  78.5 43.5 %collective-permute-done.28 = bf16[2,2,2,64,2048]{4,3,2,1,0:T(8,128)(2,1)} collective-permute-done((bf16[2,2,2,64,2048]{4,3,2,1,0:T(8,128)(2,1)}, bf16[2,2,2,64,2048]{4,3,2,1,0:T(8,128)(2,1)}, u32[]{:S(2)}, u32[]{:S(2)}) %collective-permute-start.28) | collective-permute-done | bytes 2097184 | tf_op jit(solution)/shard_map/ppermute | solution.py:104
  140.5 7.0 all-to-all-start
  152.4 10.1 collective-permute-done.1
  180.6 7.4 collective-permute-start.5
  191.3 8.7 collective-permute-done.16
  200.2 11.5 collective-permute-done.20
  215.1 7.8 collective-permute-done.21
  229.7 15.6 %collective-permute-done.22 = bf16[2,2,128,768]{3,2,0,1:T(8,128)(2,1)S(1)} collective-permute-done((bf16[2,2,128,768]{3,2,0,1:T(8,128)(2,1)S(1)}, bf16[2,2,128,768]{3,2,0,1:T(8,128)(2,1)S(1)}, u32[]{:S(2)}, u32[]{:S(2)}) %collective-permute-start.22) | collective-permute-done | bytes 786464 | tf_op jit(solution)/shard_map/ppermute | solution.py:104
  248.3 12.5 %collective-permute-done.18 = bf16[2,2,128,768]{3,2,1,0:T(8,128)(2,1)S(1)} collective-permute-done((bf16[2,2,128,768]{3,2,1,0:T(8,128)(2,1)S(1)}, bf16[2,2,128,768]{3,2,1,0:T(8,128)(2,1)S(1)}, u32[]{:S(2)}, u32[]{:S(2)}) %collective-permute-start.18) | collective-permute-done | bytes 786464 | tf_op jit(solution)/shard_map/ppermute | solution.py:104
  273.1 10.5 collective-permute-done.23
  284.4 17.1 %collective-permute-done.19 = bf16[2,2,2,128,768]{4,3,2,1,0:T(8,128)(2,1)S(1)} collective-permute-done((bf16[2,2,2,128,768]{4,3,2,1,0:T(8,128)(2,1)S(1)}, bf16[2,2,2,128,768]{4,3,2,1,0:T(8,128)(2,1)S(1)}, u32[]{:S(2)}, u32[]{:S(2)}) %collective-permute-start.19) | collective-permute-done | bytes 1572896 | tf_op jit(solution)/shard_map/ppermute | solution.py:104
  336.0 41.8 %collective-permute-done.32 = s32[8,128,6]{1,2,0:T(8,128)S(1)} collective-permute-done((s32[8,128,6]{1,2,0:T(8,128)S(1)}, s32[8,128,6]{1,2,0:T(8,128)S(1)}, u32[]{:S(2)}, u32[]{:S(2)}) %collective-permute-start.32) | collective-permute-done | bytes 24608 | tf_op jit(solution)/shard_map/ppermute | solution.py:104
  379.3 8.6 copy.322
  409.7 20.7 %collective-permute-done.34 = bf16[2,128,2048]{2,1,0:T(8,128)(2,1)S(1)} collective-permute-done((bf16[2,128,2048]{2,1,0:T(8,128)(2,1)S(1)}, bf16[2,128,2048]{2,1,0:T(8,128)(2,1)S(1)}, u32[]{:S(2)}, u32[]{:S(2)}) %collective-permute-start.34) | collective-permute-done | bytes 1048608 | tf_op jit(solution)/shard_map/ppermute | solution.py:104
  443.1 13.1 %collective-permute-done.37 = f32[2,128,16]{1,2,0:T(8,128)S(1)} collective-permute-done((f32[2,128,16]{1,2,0:T(8,128)S(1)}, f32[2,128,16]{1,2,0:T(8,128)S(1)}, u32[]{:S(2)}, u32[]{:S(2)}) %collective-permute-start.37) | collective-permute-done | bytes 16416 | tf_op jit(solution)/shard_map/ppermute | solution.py:104
  473.7 9.7 fusion.44
  483.3 10.9 multiply_convert_fusion.3
  494.2 9.6 fusion.16
  505.2 12.1 %collective-permute-done.41 = bf16[8,128,2048]{2,1,0:T(8,128)(2,1)} collective-permute-done((bf16[8,128,2048]{2,1,0:T(8,128)(2,1)}, bf16[8,128,2048]{2,1,0:T(8,128)(2,1)}, u32[]{:S(2)}, u32[]{:S(2)}) %collective-permute-start.41) | collective-permute-done | bytes 4194336 | tf_op jit(solution)/shard_map/ppermute | solution.py:104
  520.7 8.7 fusion.42
  529.5 6.7 multiply_convert_fusion.2
  536.2 7.7 fusion.18
  548.7 6.7 fusion.17
  559.4 10.7 fusion.51
  570.2 9.6 fusion.48
  579.7 14.1 %convolution_convert_fusion.2 = bf16[2048,1408]{1,0:T(8,128)(2,1)} fusion(bf16[768,1408]{1,0:T(8,128)(2,1)} %get-tuple-element.128, bf16[768,1408]{1,0:T(8,128)(2,1)} %get-tuple-element.126, bf16[768,2048]{1,0:T(8,128)(2,1)S(1)} %bitcast.573, bf16[768,2048]{1,0:T(8,128)(2,1)S(1)} %bitcast.569), kind=kOutput, calls=%fused_computation.27 | convolution fusion | flops 8882487296 | bytes 16384000 | tf_op jit(solution)/shard_map/dot_general | solution.py:68
  656.6 13.0 %convolution_convert_fusion.1 = bf16[2048,1408]{1,0:T(8,128)(2,1)} fusion(bf16[768,1408]{1,0:T(8,128)(2,1)S(1)} %copy-done.166, bf16[768,1408]{1,0:T(8,128)(2,1)S(1)} %copy-done.163, bf16[768,2048]{1,0:T(8,128)(2,1)S(1)} %bitcast.574, bf16[768,2048]{1,0:T(8,128)(2,1)S(1)} %bitcast.570), kind=kOutput, calls=%fused_computation.26 | convolution fusion | flops 8882487296 | bytes 16384000 | tf_op jit(solution)/shard_map/dot_general | solution.py:68
  669.6 8.1 fusion.9
  679.1 8.8 fusion.75
  687.9 11.0 convolution_convert_fusion
  702.3 7.2 fusion.32
  709.6 7.1 add_convert_fusion.3
  783.2 37.4 %collective-permute-done.43 = bf16[4,128,2048]{2,1,0:T(8,128)(2,1)} collective-permute-done((bf16[4,128,2048]{2,1,0:T(8,128)(2,1)}, bf16[4,128,2048]{2,1,0:T(8,128)(2,1)}, u32[]{:S(2)}, u32[]{:S(2)}) %collective-permute-start.43) | collective-permute-done | bytes 2097184 | tf_op jit(solution)/shard_map/ppermute | solution.py:104
  838.4 7.1 reduce_sum.283
  847.7 24.8 %collective-permute-done.44 = bf16[2,128,2048]{2,1,0:T(8,128)(2,1)} collective-permute-done((bf16[2,128,2048]{2,1,0:T(8,128)(2,1)}, bf16[2,128,2048]{2,1,0:T(8,128)(2,1)}, u32[]{:S(2)}, u32[]{:S(2)}) %collective-permute-start.44) | collective-permute-done | bytes 1048608 | tf_op jit(solution)/shard_map/ppermute | solution.py:104
  875.2 8.2 collective-permute-done.45
  926.0 10.4 collective-permute-done.79
  940.1 35.6 %collective-permute-done.75 = bf16[512,576]{0,1:T(8,128)(2,1)S(1)} collective-permute-done((bf16[512,576]{0,1:T(8,128)(2,1)S(1)}, bf16[512,576]{0,1:T(8,128)(2,1)S(1)}, u32[]{:S(2)}, u32[]{:S(2)}) %collective-permute-start.75) | collective-permute-done | bytes 589856 | tf_op jit(solution)/shard_map/ppermute | solution.py:104
  1003.4 20.2 %collective-permute-done.77 = bf16[2,64,576]{2,1,0:T(8,128)(2,1)} collective-permute-done((bf16[2,64,576]{2,1,0:T(8,128)(2,1)}, bf16[2,64,576]{2,1,0:T(8,128)(2,1)}, u32[]{:S(2)}, u32[]{:S(2)}) %collective-permute-start.77) | collective-permute-done | bytes 147488 | tf_op jit(solution)/shard_map/ppermute | solution.py:104
  1052.6 7.8 collective-permute-done.82
  1070.6 13.3 %collective-permute-done.71 = bf16[2,2,128,768]{3,2,0,1:T(8,128)(2,1)S(1)} collective-permute-done((bf16[2,2,128,768]{3,2,0,1:T(8,128)(2,1)S(1)}, bf16[2,2,128,768]{3,2,0,1:T(8,128)(2,1)S(1)}, u32[]{:S(2)}, u32[]{:S(2)}) %collective-permute-start.71) | collective-permute-done | bytes 786464 | tf_op jit(solution)/shard_map/ppermute | solution.py:104
  1089.5 6.8 collective-permute-done.72
  1097.0 13.8 %collective-permute-done.68 = bf16[2,128,768]{2,1,0:T(8,128)(2,1)S(1)} collective-permute-done((bf16[2,128,768]{2,1,0:T(8,128)(2,1)S(1)}, bf16[2,128,768]{2,1,0:T(8,128)(2,1)S(1)}, u32[]{:S(2)}, u32[]{:S(2)}) %collective-permute-start.68) | collective-permute-done | bytes 393248 | tf_op jit(solution)/shard_map/ppermute | solution.py:104
  1140.9 11.8 %collective-permute-done.88 = bf16[64,2048]{1,0:T(8,128)(2,1)S(1)} collective-permute-done((bf16[64,2048]{1,0:T(8,128)(2,1)S(1)}, bf16[64,2048]{1,0:T(8,128)(2,1)S(1)}, u32[]{:S(2)}, u32[]{:S(2)}) %collective-permute-start.88) | collective-permute-done | bytes 262176 | tf_op jit(solution)/shard_map/ppermute | solution.py:104
  (876 shorter events, 506.3 us)
Async XLA Ops:
  7.2 300.0 %all-gather.11.cloned.1.call-start = ((), (), s32[]{:S(2)}) async-start(), calls=%async_computation.5 | async-start | bytes 3932160 | tf_op jit(solution)/shard_map/all_gather | solution.py:252
  17.8 29.9 %collective-permute-start.26 = (bf16[2,64,2048]{2,1,0:T(8,128)(2,1)S(1)}, bf16[2,64,2048]{2,1,0:T(8,128)(2,1)S(1)}, u32[]{:S(2)}, u32[]{:S(2)}) collective-permute-start(bf16[2,64,2048]{2,1,0:T(8,128)(2,1)S(1)} %pad_maximum_fusion.34), channel_id=1, source_target_pairs={{0,16},{1,17},{2,18},{3,19},{4,20},{5,21},{6,22},{7,23},{8,24},{9,... | collective-permute-start | bytes 1572872 | tf_op jit(solution)/shard_map/ppermute | solution.py:104
  75.6 46.5 %collective-permute-start.28 = (bf16[2,2,2,64,2048]{4,3,2,1,0:T(8,128)(2,1)}, bf16[2,2,2,64,2048]{4,3,2,1,0:T(8,128)(2,1)}, u32[]{:S(2)}, u32[]{:S(2)}) collective-permute-start(bf16[2,2,2,64,2048]{4,3,2,1,0:T(8,128)(2,1)} %pad_maximum_fusion.9), channel_id=1, source_target_pairs={{0,4},{1,5},{2,6},{3,7},{4,0},{5,1},{6,2},{7,3},{8,12},{9,13},{10,... | collective-permute-start | bytes 6291464 | tf_op jit(solution)/shard_map/ppermute | solution.py:104
  78.5 300.8 %all-gather.13.cloned.1.call-start = ((), (), s32[]{:S(2)}) async-start(), calls=%async_computation.6 | async-start | bytes 12582912 | tf_op jit(solution)/shard_map/all_gather | solution.py:262
  126.4 347.2 %all-gather.15.cloned.1.call-start = ((), (), s32[]{:S(2)}) async-start(), calls=%async_computation.10 | async-start | bytes 8650752 | tf_op jit(solution)/shard_map/all_gather | solution.py:275
  127.2 356.2 %all-gather.17.cloned.1.call-start = ((), (), s32[]{:S(2)}) async-start(), calls=%async_computation.11 | async-start | bytes 8650752 | tf_op jit(solution)/shard_map/all_gather | solution.py:276
  127.8 36.3 %collective-permute-start.29 = (s32[1,128,6]{1,2,0:T(8,128)S(1)}, s32[1,128,6]{1,2,0:T(8,128)S(1)}, u32[]{:S(2)}, u32[]{:S(2)}) collective-permute-start(s32[1,128,6]{1,2,0:T(8,128)S(1)} %bitcast.543), channel_id=1, source_target_pairs={{0,2},{1,17},{2,0},{3,19},{4,6},{5,21},{6,4},{7,23},{8,10},{9,25},... | collective-permute-start | bytes 9224 | tf_op jit(solution)/shard_map/ppermute | solution.py:104
  129.6 42.3 %collective-permute-start.10 = (bf16[16,2048]{1,0:T(8,128)(2,1)S(1)}, bf16[16,2048]{1,0:T(8,128)(2,1)}, u32[]{:S(2)}, u32[]{:S(2)}) collective-permute-start(bf16[16,2048]{1,0:T(8,128)(2,1)S(1)} %constant_dynamic-slice_fusion.29), channel_id=1, source_target_pairs={{0,1},{1,0},{2,3},{3,2},{4,5},{5,4},{6,7},{7,6},{8,9},{9,8},{10,11... | collective-permute-start | bytes 196616 | tf_op jit(solution)/shard_map/ppermute | solution.py:107
  130.2 57.9 %collective-permute-start.15 = (bf16[64,1536]{1,0:T(8,128)(2,1)S(1)}, bf16[64,1536]{1,0:T(8,128)(2,1)}, u32[]{:S(2)}, u32[]{:S(2)}) collective-permute-start(bf16[64,1536]{1,0:T(8,128)(2,1)S(1)} %constant_dynamic-slice_fusion.28), channel_id=1, source_target_pairs={{0,1},{1,0},{2,3},{3,2},{4,5},{5,4},{6,7},{7,6},{8,9},{9,8},{10,11... | collective-permute-start | bytes 589832 | tf_op jit(solution)/shard_map/ppermute | solution.py:107
  140.5 256.6 %all-to-all-start = ((bf16[16,64,352]{2,1,0:T(8,128)(2,1)}), bf16[16,64,352]{2,1,0:T(8,128)(2,1)}, u32[]{:S(2)}, u32[]{:S(2)}) async-start(bf16[16,64,352]{2,1,0:T(8,128)(2,1)} %all_to_all.12), calls=%async_computation | async-start | bytes 1572864 | tf_op jit(solution)/shard_map/all_to_all | solution.py:266
  147.5 346.7 %all-gather.19.cloned.1.call-start = ((), (), s32[]{:S(2)}) async-start(), calls=%async_computation.12 | async-start | bytes 8650752 | tf_op jit(solution)/shard_map/all_gather | solution.py:277
  147.5 65.9 %collective-permute-start.46 = (bf16[1,128,2048]{2,1,0:T(8,128)(2,1)S(1)}, bf16[1,128,2048]{2,1,0:T(8,128)(2,1)S(1)}, u32[]{:S(2)}, u32[]{:S(2)}) collective-permute-start(bf16[1,128,2048]{2,1,0:T(8,128)(2,1)S(1)} %bitcast.510), channel_id=1, source_target_pairs={{0,2},{1,17},{2,0},{3,19},{4,6},{5,21},{6,4},{7,23},{8,10},{9,25},... | collective-permute-start | bytes 1572872 | tf_op jit(solution)/shard_map/ppermute | solution.py:104
  149.5 464.4 %all-gather.21.cloned.1.call-start = ((), (), s32[]{:S(2)}) async-start(), calls=%async_computation.13 | async-start | bytes 2359296 | tf_op jit(solution)/shard_map/all_gather | solution.py:273
  164.7 165.5 %collective-permute-start.30 = (s32[2,128,6]{1,2,0:T(8,128)}, s32[2,128,6]{1,2,0:T(8,128)}, u32[]{:S(2)}, u32[]{:S(2)}) collective-permute-start(s32[2,128,6]{1,2,0:T(8,128)} %pad_add_fusion.2), channel_id=1, source_target_pairs={{0,16},{1,3},{2,18},{3,1},{4,20},{5,7},{6,22},{7,5},{8,24},{9,11},... | collective-permute-start | bytes 18440 | tf_op jit(solution)/shard_map/ppermute | solution.py:104
  180.6 66.4 %collective-permute-start.5 = (bf16[128,2048]{1,0:T(8,128)(2,1)}, bf16[128,2048]{1,0:T(8,128)(2,1)S(1)}, u32[]{:S(2)}, u32[]{:S(2)}) collective-permute-start(bf16[128,2048]{1,0:T(8,128)(2,1)} %fusion.102), channel_id=1, source_target_pairs={{0,1},{1,0},{2,3},{3,2},{4,5},{5,4},{6,7},{7,6},{8,9},{9,8},{10,11... | collective-permute-start | bytes 1572872 | tf_op jit(solution)/shard_map/ppermute | solution.py:107
  222.9 38.8 %collective-permute-start.47 = (bf16[2,128,2048]{2,1,0:T(8,128)(2,1)S(1)}, bf16[2,128,2048]{2,1,0:T(8,128)(2,1)S(1)}, u32[]{:S(2)}, u32[]{:S(2)}) collective-permute-start(bf16[2,128,2048]{2,1,0:T(8,128)(2,1)S(1)} %pad_maximum_fusion.21), channel_id=1, source_target_pairs={{0,16},{1,3},{2,18},{3,1},{4,20},{5,7},{6,22},{7,5},{8,24},{9,11},... | collective-permute-start | bytes 3145736 | tf_op jit(solution)/shard_map/ppermute | solution.py:104
  228.0 32.8 %collective-permute-start.18 = (bf16[2,2,128,768]{3,2,1,0:T(8,128)(2,1)S(1)}, bf16[2,2,128,768]{3,2,1,0:T(8,128)(2,1)S(1)}, u32[]{:S(2)}, u32[]{:S(2)}) collective-permute-start(bf16[2,2,128,768]{3,2,1,0:T(8,128)(2,1)S(1)} %pad_maximum_fusion.24), channel_id=1, source_target_pairs={{0,4},{1,5},{2,6},{3,7},{4,0},{5,1},{6,2},{7,3},{8,12},{9,13},{10,... | collective-permute-start | bytes 2359304 | tf_op jit(solution)/shard_map/ppermute | solution.py:104
  247.0 36.5 %collective-permute-start.23 = (bf16[2,2,2,128,768]{4,3,0,2,1:T(8,128)(2,1)S(1)}, bf16[2,2,2,128,768]{4,3,0,2,1:T(8,128)(2,1)S(1)}, u32[]{:S(2)}, u32[]{:S(2)}) collective-permute-start(bf16[2,2,2,128,768]{4,3,0,2,1:T(8,128)(2,1)S(1)} %pad_maximum_fusion.13), channel_id=1, source_target_pairs={{0,8},{1,9},{2,10},{3,11},{4,12},{5,13},{6,14},{7,15},{8,0},{9,1},... | collective-permute-start | bytes 4718600 | tf_op jit(solution)/shard_map/ppermute | solution.py:104
  261.1 40.4 %collective-permute-start.19 = (bf16[2,2,2,128,768]{4,3,2,1,0:T(8,128)(2,1)S(1)}, bf16[2,2,2,128,768]{4,3,2,1,0:T(8,128)(2,1)S(1)}, u32[]{:S(2)}, u32[]{:S(2)}) collective-permute-start(bf16[2,2,2,128,768]{4,3,2,1,0:T(8,128)(2,1)S(1)} %pad_maximum_fusion.12), channel_id=1, source_target_pairs={{0,2},{1,3},{2,0},{3,1},{4,6},{5,7},{6,4},{7,5},{8,10},{9,11},{10,... | collective-permute-start | bytes 4718600 | tf_op jit(solution)/shard_map/ppermute | solution.py:104
  263.4 61.7 %collective-permute-start.48 = (bf16[4,128,2048]{2,1,0:T(8,128)(2,1)}, bf16[4,128,2048]{2,1,0:T(8,128)(2,1)}, u32[]{:S(2)}, u32[]{:S(2)}) collective-permute-start(bf16[4,128,2048]{2,1,0:T(8,128)(2,1)} %pad_maximum_fusion.11), channel_id=1, source_target_pairs={{0,8},{1,5},{2,10},{3,7},{4,12},{5,1},{6,14},{7,3},{8,0},{9,13},{1... | collective-permute-start | bytes 6291464 | tf_op jit(solution)/shard_map/ppermute | solution.py:104
  325.0 53.0 %collective-permute-start.24 = (bf16[256,1024]{0,1:T(8,128)(2,1)S(1)}, bf16[256,1024]{0,1:T(8,128)(2,1)}, u32[]{:S(2)}, u32[]{:S(2)}) collective-permute-start(bf16[256,1024]{0,1:T(8,128)(2,1)S(1)} %bitcast.538), channel_id=1, source_target_pairs={{0,1},{1,0},{2,3},{3,2},{4,5},{5,4},{6,7},{7,6},{8,9},{9,8},{10,11... | collective-permute-start | bytes 1572872 | tf_op jit(solution)/shard_map/ppermute | solution.py:107
  328.6 103.1 %collective-permute-start.49 = (bf16[8,128,2048]{2,1,0:T(8,128)(2,1)}, bf16[8,128,2048]{2,1,0:T(8,128)(2,1)}, u32[]{:S(2)}, u32[]{:S(2)}) collective-permute-start(bf16[8,128,2048]{2,1,0:T(8,128)(2,1)} %pad_maximum_fusion.3), channel_id=1, source_target_pairs={{0,4},{1,9},{2,6},{3,11},{4,0},{5,13},{6,2},{7,15},{8,12},{9,1},{1... | collective-permute-start | bytes 12582920 | tf_op jit(solution)/shard_map/ppermute | solution.py:104
  335.5 42.4 %collective-permute-start.32 = (s32[8,128,6]{1,2,0:T(8,128)S(1)}, s32[8,128,6]{1,2,0:T(8,128)S(1)}, u32[]{:S(2)}, u32[]{:S(2)}) collective-permute-start(s32[8,128,6]{1,2,0:T(8,128)S(1)} %pad_add_fusion), channel_id=1, source_target_pairs={{0,4},{1,9},{2,6},{3,11},{4,0},{5,13},{6,2},{7,15},{8,12},{9,1},{1... | collective-permute-start | bytes 73736 | tf_op jit(solution)/shard_map/ppermute | solution.py:104
  397.1 715.6 %reduce-scatter.4.cloned.1.call-start = ((), (), s32[]{:S(2)}) async-start(), calls=%async_computation.7 | async-start | bytes 8650752 | tf_op jit(solution)/shard_map/reduce_scatter | solution.py:415
  431.7 33.6 %collective-permute-start.35 = (bf16[4,128,2048]{2,1,0:T(8,128)(2,1)S(1)}, bf16[4,128,2048]{2,1,0:T(8,128)(2,1)S(1)}, u32[]{:S(2)}, u32[]{:S(2)}) collective-permute-start(bf16[4,128,2048]{2,1,0:T(8,128)(2,1)S(1)} %pad_maximum_fusion.10), channel_id=1, source_target_pairs={{0,8},{1,5},{2,10},{3,7},{4,12},{5,1},{6,14},{7,3},{8,0},{9,13},{1... | collective-permute-start | bytes 6291464 | tf_op jit(solution)/shard_map/ppermute | solution.py:104
  468.5 48.8 %collective-permute-start.41 = (bf16[8,128,2048]{2,1,0:T(8,128)(2,1)}, bf16[8,128,2048]{2,1,0:T(8,128)(2,1)}, u32[]{:S(2)}, u32[]{:S(2)}) collective-permute-start(bf16[8,128,2048]{2,1,0:T(8,128)(2,1)} %pad_maximum_fusion.2), channel_id=1, source_target_pairs={{0,4},{1,9},{2,6},{3,11},{4,0},{5,13},{6,2},{7,15},{8,12},{9,1},{1... | collective-permute-start | bytes 12582920 | tf_op jit(solution)/shard_map/ppermute | solution.py:104
  593.9 523.5 %reduce-scatter.6.cloned.1.call-start = ((), (), s32[]{:S(2)}) async-start(), calls=%async_computation.8 | async-start | bytes 8650752 | tf_op jit(solution)/shard_map/reduce_scatter | solution.py:415
  623.2 94.8 %collective-permute-start.54 = (f32[8,128,16]{1,2,0:T(8,128)S(1)}, f32[8,128,16]{1,2,0:T(8,128)S(1)}, u32[]{:S(2)}, u32[]{:S(2)}) collective-permute-start(f32[8,128,16]{1,2,0:T(8,128)S(1)} %broadcast_multiply_fusion), channel_id=1, source_target_pairs={{0,4},{1,9},{2,6},{3,11},{4,0},{5,13},{6,2},{7,15},{8,12},{9,1},{1... | collective-permute-start | bytes 196616 | tf_op jit(solution)/shard_map/ppermute | solution.py:104
  638.1 103.4 %collective-permute-start.42 = (bf16[1024,2048]{1,0:T(8,128)(2,1)}, bf16[1024,2048]{1,0:T(8,128)(2,1)}, u32[]{:S(2)}, u32[]{:S(2)}) collective-permute-start(bf16[1024,2048]{1,0:T(8,128)(2,1)} %fusion.11), channel_id=1, source_target_pairs={{0,4},{1,9},{2,6},{3,11},{4,0},{5,13},{6,2},{7,15},{8,12},{9,1},{1... | collective-permute-start | bytes 12582920 | tf_op jit(solution)/shard_map/ppermute | solution.py:104
  677.7 54.5 %collective-permute-start.50 = (bf16[1024,2048]{1,0:T(8,128)(2,1)}, bf16[1024,2048]{1,0:T(8,128)(2,1)}, u32[]{:S(2)}, u32[]{:S(2)}) collective-permute-start(bf16[1024,2048]{1,0:T(8,128)(2,1)} %fusion.9), channel_id=1, source_target_pairs={{0,4},{1,9},{2,6},{3,11},{4,0},{5,13},{6,2},{7,15},{8,12},{9,1},{1... | collective-permute-start | bytes 12582920 | tf_op jit(solution)/shard_map/ppermute | solution.py:104
  722.7 36.9 %collective-permute-start.56 = (f32[2,128,16]{1,2,0:T(8,128)S(1)}, f32[2,128,16]{1,2,0:T(8,128)}, u32[]{:S(2)}, u32[]{:S(2)}) collective-permute-start(f32[2,128,16]{1,2,0:T(8,128)S(1)} %slice.299), channel_id=1, source_target_pairs={{0,16},{1,3},{2,18},{3,1},{4,20},{5,7},{6,22},{7,5},{8,24},{9,11},... | collective-permute-start | bytes 49160 | tf_op jit(solution)/shard_map/ppermute | solution.py:104
  739.2 34.6 %collective-permute-start.51 = (bf16[4,128,2048]{2,1,0:T(8,128)(2,1)}, bf16[4,128,2048]{2,1,0:T(8,128)(2,1)S(1)}, u32[]{:S(2)}, u32[]{:S(2)}) collective-permute-start(bf16[4,128,2048]{2,1,0:T(8,128)(2,1)} %bitcast.102), channel_id=1, source_target_pairs={{0,8},{1,5},{2,10},{3,7},{4,12},{5,1},{6,14},{7,3},{8,0},{9,13},{1... | collective-permute-start | bytes 6291464 | tf_op jit(solution)/shard_map/ppermute | solution.py:104
  748.0 72.7 %collective-permute-start.43 = (bf16[4,128,2048]{2,1,0:T(8,128)(2,1)}, bf16[4,128,2048]{2,1,0:T(8,128)(2,1)}, u32[]{:S(2)}, u32[]{:S(2)}) collective-permute-start(bf16[4,128,2048]{2,1,0:T(8,128)(2,1)} %bitcast.90), channel_id=1, source_target_pairs={{0,8},{1,5},{2,10},{3,7},{4,12},{5,1},{6,14},{7,3},{8,0},{9,13},{1... | collective-permute-start | bytes 6291464 | tf_op jit(solution)/shard_map/ppermute | solution.py:104
  755.9 75.9 %all-to-all-start.1 = ((bf16[32,64,352]{2,1,0:T(8,128)(2,1)}), bf16[32,64,352]{2,1,0:T(8,128)(2,1)}, u32[]{:S(2)}, u32[]{:S(2)}) async-start(bf16[32,64,352]{2,1,0:T(8,128)(2,1)} %bitcast.171), calls=%async_computation.1 | async-start | bytes 3145728 | tf_op jit(solution)/shard_map/all_to_all | solution.py:424
  759.5 368.1 %reduce-scatter.8.cloned.1.call-start = ((), (), s32[]{:S(2)}) async-start(), calls=%async_computation.9 | async-start | bytes 8650752 | tf_op jit(solution)/shard_map/reduce_scatter | solution.py:415
  763.5 66.0 %collective-permute-start.89 = (f32[88,2048]{1,0:T(8,128)}, f32[88,2048]{1,0:T(8,128)}, u32[]{:S(2)}, u32[]{:S(2)}) collective-permute-start(f32[88,2048]{1,0:T(8,128)} %constant_dynamic-slice_fusion.1), channel_id=1, source_target_pairs={{0,1},{1,0},{2,3},{3,2},{4,5},{5,4},{6,7},{7,6},{8,9},{9,8},{10,11... | collective-permute-start | bytes 2162696 | tf_op jit(solution)/shard_map/ppermute | solution.py:107
  779.6 66.0 %collective-permute-start.52 = (bf16[2,128,2048]{2,1,0:T(8,128)(2,1)}, bf16[2,128,2048]{2,1,0:T(8,128)(2,1)}, u32[]{:S(2)}, u32[]{:S(2)}) collective-permute-start(bf16[2,128,2048]{2,1,0:T(8,128)(2,1)} %slice.293), channel_id=1, source_target_pairs={{0,16},{1,3},{2,18},{3,1},{4,20},{5,7},{6,22},{7,5},{8,24},{9,11},... | collective-permute-start | bytes 3145736 | tf_op jit(solution)/shard_map/ppermute | solution.py:104
  825.6 46.9 %collective-permute-start.44 = (bf16[2,128,2048]{2,1,0:T(8,128)(2,1)}, bf16[2,128,2048]{2,1,0:T(8,128)(2,1)}, u32[]{:S(2)}, u32[]{:S(2)}) collective-permute-start(bf16[2,128,2048]{2,1,0:T(8,128)(2,1)} %slice.287), channel_id=1, source_target_pairs={{0,16},{1,3},{2,18},{3,1},{4,20},{5,7},{6,22},{7,5},{8,24},{9,11},... | collective-permute-start | bytes 3145736 | tf_op jit(solution)/shard_map/ppermute | solution.py:104
  847.4 27.2 %collective-permute-start.53 = (bf16[1,128,2048]{2,1,0:T(8,128)(2,1)S(1)}, bf16[1,128,2048]{2,1,0:T(8,128)(2,1)S(1)}, u32[]{:S(2)}, u32[]{:S(2)}) collective-permute-start(bf16[1,128,2048]{2,1,0:T(8,128)(2,1)S(1)} %slice.295), channel_id=1, source_target_pairs={{0,2},{1,17},{2,0},{3,19},{4,6},{5,21},{6,4},{7,23},{8,10},{9,25},... | collective-permute-start | bytes 1572872 | tf_op jit(solution)/shard_map/ppermute | solution.py:104
  914.8 153.4 %collective-permute-start.85 = (bf16[512,2048]{1,0:T(8,128)(2,1)}, bf16[512,2048]{1,0:T(8,128)(2,1)}, u32[]{:S(2)}, u32[]{:S(2)}) collective-permute-start(bf16[512,2048]{1,0:T(8,128)(2,1)} %convolution_convert_fusion.7), channel_id=1, source_target_pairs={{0,2},{1,3},{2,0},{3,1},{4,6},{5,7},{6,4},{7,5},{8,10},{9,11},{10,... | collective-permute-start | bytes 6291464 | tf_op jit(solution)/shard_map/ppermute | solution.py:104
  916.3 59.3 %collective-permute-start.75 = (bf16[512,576]{0,1:T(8,128)(2,1)S(1)}, bf16[512,576]{0,1:T(8,128)(2,1)S(1)}, u32[]{:S(2)}, u32[]{:S(2)}) collective-permute-start(bf16[512,576]{0,1:T(8,128)(2,1)S(1)} %convolution_convert_fusion.13), channel_id=1, source_target_pairs={{0,2},{1,3},{2,0},{3,1},{4,6},{5,7},{6,4},{7,5},{8,10},{9,11},{10,... | collective-permute-start | bytes 1769480 | tf_op jit(solution)/shard_map/ppermute | solution.py:104
  938.6 55.3 %collective-permute-start.80 = (bf16[2,2,32,2048]{3,2,0,1:T(8,128)(2,1)}, bf16[2,2,32,2048]{3,2,0,1:T(8,128)(2,1)}, u32[]{:S(2)}, u32[]{:S(2)}) collective-permute-start(bf16[2,2,32,2048]{3,2,0,1:T(8,128)(2,1)} %bitcast.482), channel_id=1, source_target_pairs={{0,4},{1,5},{2,6},{3,7},{4,0},{5,1},{6,2},{7,3},{8,12},{9,13},{10,... | collective-permute-start | bytes 1572872 | tf_op jit(solution)/shard_map/ppermute | solution.py:104
  983.0 78.9 %collective-permute-start.70 = (bf16[1024,768]{1,0:T(8,128)(2,1)}, bf16[1024,768]{1,0:T(8,128)(2,1)}, u32[]{:S(2)}, u32[]{:S(2)}) collective-permute-start(bf16[1024,768]{1,0:T(8,128)(2,1)} %convolution_convert_fusion.11), channel_id=1, source_target_pairs={{0,8},{1,9},{2,10},{3,11},{4,12},{5,13},{6,14},{7,15},{8,0},{9,1},... | collective-permute-start | bytes 4718600 | tf_op jit(solution)/shard_map/ppermute | solution.py:104
  990.4 74.9 %collective-permute-start.66 = (bf16[1024,768]{1,0:T(8,128)(2,1)}, bf16[1024,768]{1,0:T(8,128)(2,1)}, u32[]{:S(2)}, u32[]{:S(2)}) collective-permute-start(bf16[1024,768]{1,0:T(8,128)(2,1)} %convolution_convert_fusion.12), channel_id=1, source_target_pairs={{0,4},{1,5},{2,6},{3,7},{4,0},{5,1},{6,2},{7,3},{8,12},{9,13},{10,... | collective-permute-start | bytes 4718600 | tf_op jit(solution)/shard_map/ppermute | solution.py:104
  993.8 29.8 %collective-permute-start.77 = (bf16[2,64,576]{2,1,0:T(8,128)(2,1)}, bf16[2,64,576]{2,1,0:T(8,128)(2,1)}, u32[]{:S(2)}, u32[]{:S(2)}) collective-permute-start(bf16[2,64,576]{2,1,0:T(8,128)(2,1)} %dynamic-slice_bitcast_fusion.9), channel_id=1, source_target_pairs={{0,8},{1,9},{2,10},{3,11},{4,12},{5,13},{6,14},{7,15},{8,0},{9,1},... | collective-permute-start | bytes 442376 | tf_op jit(solution)/shard_map/ppermute | solution.py:104
  998.1 52.2 %collective-permute-start.81 = (bf16[2,32,2048]{2,1,0:T(8,128)(2,1)}, bf16[2,32,2048]{2,1,0:T(8,128)(2,1)}, u32[]{:S(2)}, u32[]{:S(2)}) collective-permute-start(bf16[2,32,2048]{2,1,0:T(8,128)(2,1)} %dynamic-slice_bitcast_fusion.6), channel_id=1, source_target_pairs={{0,2},{1,3},{2,0},{3,1},{4,6},{5,7},{6,4},{7,5},{8,10},{9,11},{10,... | collective-permute-start | bytes 786440 | tf_op jit(solution)/shard_map/ppermute | solution.py:104
  1088.9 33.2 %collective-permute-start.86 = (bf16[2,2,64,2048]{3,2,0,1:T(8,128)(2,1)}, bf16[2,2,64,2048]{3,2,0,1:T(8,128)(2,1)S(1)}, u32[]{:S(2)}, u32[]{:S(2)}) collective-permute-start(bf16[2,2,64,2048]{3,2,0,1:T(8,128)(2,1)} %bitcast.480), channel_id=1, source_target_pairs={{0,4},{1,5},{2,6},{3,7},{4,0},{5,1},{6,2},{7,3},{8,12},{9,13},{10,... | collective-permute-start | bytes 3145736 | tf_op jit(solution)/shard_map/ppermute | solution.py:104
  1097.0 28.5 %collective-permute-start.73 = (bf16[128,768]{1,0:T(8,128)(2,1)}, bf16[128,768]{1,0:T(8,128)(2,1)}, u32[]{:S(2)}, u32[]{:S(2)}) collective-permute-start(bf16[128,768]{1,0:T(8,128)(2,1)} %dynamic-slice_bitcast_fusion.7), channel_id=1, source_target_pairs={{0,16},{1,17},{2,18},{3,19},{4,20},{5,21},{6,22},{7,23},{8,24},{9,... | collective-permute-start | bytes 589832 | tf_op jit(solution)/shard_map/ppermute | solution.py:104
  (236 other events, 2542.5 us)
Sparse Core Ops, SparseCore 0:
  78.6 11.5 all-gather.10
  126.5 21.9 all-gather.12
  150.0 17.1 all-gather.14
  168.6 17.1 all-gather.16
  187.2 17.1 all-gather.18
  397.2 9.4 all-gather.20
  594.0 13.9 reduce-scatter.3
  669.7 13.7 reduce-scatter.5
  764.5 13.2 reduce-scatter.7

commit v2 on v1

v2 whole, which is shorter than its diff:
```python
import math

import jax
import jax.numpy as jnp
from jax import lax
from jax.experimental import pallas as pl
from jax.experimental.pallas import tpu as pltpu
from jax.sharding import PartitionSpec as P

D = 2048
H = 16
DN = 128
DR = 64
DV = 128
KVR = 512
TOPK = 6
SEQ_DEV = 128

NORM_EPS = 1e-06
ROPE_THETA = 50000.0
GATE_SCALE = 2.446

BF16 = jnp.bfloat16
F32 = jnp.float32
BOTH = ("expert", "fsdp")

ORDER_QUERY = ((8, 4, 1, 2), (8, 2, 4, 1))
ORDER_EXPAND = (8, 1, 2, 4)
ORDER_LATENT = (8, 1, 2, 4)
ORDER_SMALL = (1, 2, 4, 8)
ORDER_OUTPUT = ((8, 1, 4, 2), (8, 2, 1, 4))
TOKEN_GROUPS = (48, 48, 32)
ORDER_TOKENS = ((8, 2, 1, 4), (8, 1, 4, 2), (8, 4, 2, 1))
BACK_QUERY = ((1, 4, 2, 8), (4, 2, 1, 8))
BACK_EXPAND = (2, 1, 4, 8)
BACK_LATENT = (2, 1, 4, 8)
BACK_OUTPUT = ((4, 1, 2, 8), (2, 4, 1, 8))


def rms_scale(values, gain_vec):
    return (
        values * lax.rsqrt(jnp.mean(values * values, axis=-1, keepdims=True) + NORM_EPS) * gain_vec
    )


def rotate(values, cos_table, sin_table):
    middle = values.shape[-1] // 2
    lower_half = values[..., :middle]
    upper_half = values[..., middle:]
    return jnp.concatenate(
        [
            lower_half * cos_table - upper_half * sin_table,
            upper_half * cos_table + lower_half * sin_table,
        ],
        axis=-1,
    )


def rope_tables(positions):
    steps_float = jnp.arange(DR // 2).astype(F32) * (2.0 / DR)
    inverse = jnp.exp(-steps_float * math.log(ROPE_THETA))
    turned = positions.astype(F32)[:, None] * inverse[None, :]
    return (jnp.cos(turned), jnp.sin(turned))


def product(left_side, right_side):
    return jnp.dot(left_side, right_side, preferred_element_type=F32)


def inner_rows(left_side, right_side):
    return lax.dot_general(
        left_side, right_side, (((0,), (0,)), ((), ())), preferred_element_type=F32
    )


def outer_cols(left_side, right_side):
    return lax.dot_general(
        left_side, right_side, (((1,), (1,)), ((), ())), preferred_element_type=F32
    )


def together(*values):
    return lax.optimization_barrier(values)


def swiglu(gate_act, up_act):
    return jax.nn.silu(gate_act) * up_act


WIDE = 512
LANES = 128
VMEM_BYTES = 60 * 2**20


def whole_in_vmem():
    return pl.BlockSpec(memory_space=pltpu.VMEM)


def spans(size):
    return [(start, min(WIDE, size - start)) for start in range(0, size, WIDE)]


def weight_copies(in_hbm, down_hbm, in_refs, down_ref, sems):
    ff = in_hbm[0].shape[1]
    count = 0
    by_span = [[] for _ in spans(down_ref.shape[0])]

    def copy(source, target):
        nonlocal count
        count += 1
        return pltpu.make_async_copy(source, target, sems.at[count - 1])

    for extra, joined in zip(in_hbm[1::2], in_refs):
        by_span[-1].append(copy(extra, joined.at[:, pl.ds(ff, extra.shape[1])]))
    for k, (start, size) in enumerate(spans(ff)):
        for expert, joined in zip(in_hbm[0::2], in_refs):
            there = pl.ds(start, size)
            by_span[k].append(copy(expert.at[:, there], joined.at[:, there]))
    down = [
        copy(down_hbm[0], down_ref.at[pl.ds(0, ff), :]),
        copy(down_hbm[1], down_ref.at[pl.ds(ff, down_hbm[1].shape[0]), :]),
    ]
    return by_span, down


def gated(gate, start, size, ff):
    units = lax.broadcasted_iota(jnp.int32, (1, size), 1) + start
    return jnp.where(units < ff, gate, 1.0)


def row_groups(refs):
    start = 0
    for ref in refs:
        yield ref, pl.ds(start, ref.shape[0])
        start += ref.shape[0]


def forward_kernel(*refs):
    groups = len(TOKEN_GROUPS)
    rows_refs = refs[:groups]
    member_ref, own_ref, gate_w, gate_x, up_w, up_x, down_w, down_x = refs[groups : groups + 8]
    out_refs = refs[groups + 8 : 2 * groups + 8]
    logits_ref, gate_act_ref, up_act_ref, hidden_ref = refs[2 * groups + 8 : 2 * groups + 12]
    gate_all, up_all, down_all, sems = refs[2 * groups + 12 :]
    by_span, down = weight_copies(
        (gate_w, gate_x, up_w, up_x), (down_w, down_x), (gate_all, up_all), down_all, sems
    )
    for copy in by_span[-1] + sum(by_span[:-1], []) + down:
        copy.start()
    ff, units = gate_w.shape[1], down_all.shape[0]
    width = down_all.shape[1]
    order = list(zip(spans(units), by_span))
    order = order[-1:] + order[:-1]
    for rows_ref, here in row_groups(rows_refs):
        first = here.start == 0
        for k, ((start, size), copies) in enumerate(order):
            there = pl.ds(start, size)
            if first:
                for copy in copies:
                    copy.wait()
            gate_act = product(rows_ref[...], gate_all[:, there])
            up_act = product(rows_ref[...], up_all[:, there])
            if k == 0:
                logits_ref[here, :] = gate_act
                chosen = member_ref[here, :] / (1.0 + jnp.exp(-gate_act))
                own = jnp.sum(chosen * own_ref[...], axis=1, keepdims=True)
                gate = GATE_SCALE * own / jnp.sum(chosen, axis=1, keepdims=True)
            gate_act_ref[here, there] = gate_act.astype(BF16)
            up_act_ref[here, there] = up_act.astype(BF16)
            hidden = swiglu(gate_act, up_act) * gated(gate, start, size, ff)
            hidden_ref[here, there] = hidden.astype(BF16)
    for copy in down:
        copy.wait()
    for out_ref, here in row_groups(out_refs):
        for start, size in spans(width):
            there = pl.ds(start, size)
            out_ref[:, there] = product(hidden_ref[here, :], down_all[:, there]).astype(BF16)


def backward_kernel(*refs):
    groups = len(TOKEN_GROUPS)
    cot_refs = refs[:groups]
    member_ref, own_ref, logits_ref, gate_act_ref, up_act_ref = refs[groups : groups + 5]
    gate_w, gate_x, up_w, up_x, down_w, down_x = refs[groups + 5 : groups + 11]
    back_refs = refs[groups + 11 : 2 * groups + 11]
    gate_back_ref, up_back_ref, gate_all, up_all, down_all, sems = refs[2 * groups + 11 :]
    by_span, down = weight_copies(
        (gate_w, gate_x, up_w, up_x), (down_w, down_x), (gate_all, up_all), down_all, sems
    )
    for copy in down + sum(by_span, []):
        copy.start()
    ff, units = gate_w.shape[1], down_all.shape[0]
    width = down_all.shape[1]
    for copy in down:
        copy.wait()
    for cot_ref, here in row_groups(cot_refs):
        sigmoid = 1.0 / (1.0 + jnp.exp(-logits_ref[here, :]))
        chosen = member_ref[here, :] * sigmoid
        own = jnp.sum(chosen * own_ref[...], axis=1, keepdims=True)
        all_chosen = jnp.sum(chosen, axis=1, keepdims=True)
        gate = GATE_SCALE * own / all_chosen
        gate_grad = jnp.zeros_like(gate)
        for start, size in spans(units):
            there = pl.ds(start, size)
            last = start + size == units
            hidden_back = outer_cols(cot_ref[...], down_all[there, :])
            gate_act = gate_act_ref[here, there].astype(F32)
            up_act = up_act_ref[here, there].astype(F32)
            sig = 1.0 / (1.0 + jnp.exp(-gate_act))
            silu = gate_act * sig
            column = lax.broadcasted_iota(jnp.int32, (1, size), 1) + start
            term = jnp.where(column < ff, silu * up_act * hidden_back, 0.0)
            gate_grad = gate_grad + jnp.sum(term, axis=1, keepdims=True)
            scaled = hidden_back * gated(gate, start, size, ff)
            up_back_ref[here, there] = (scaled * silu).astype(BF16)
            gate_back = scaled * up_act * (sig + silu * (1.0 - sig))
            if last:
                named = jnp.sum(member_ref[here, :] * own_ref[...], axis=1, keepdims=True)
                logit_back = GATE_SCALE * named * gate_grad * chosen * (1.0 - sigmoid)
                logit_back = logit_back * (own_ref[...] - own / all_chosen) / all_chosen
                gate_back = jnp.where(member_ref[here, :] > 0.0, logit_back, gate_back)
            gate_back_ref[here, there] = gate_back.astype(BF16)
    for copy in sum(by_span, []):
        copy.wait()
    for back_ref, here in row_groups(back_refs):
        for start, size in spans(width):
            there = pl.ds(start, size)
            back = outer_cols(gate_back_ref[here, :], gate_all[there, :])
            back = back + outer_cols(up_back_ref[here, :], up_all[there, :])
            back_ref[:, there] = back.astype(BF16)


def expert_call(kernel, out_shapes, arrays, weights):
    width, ff = weights[0].shape
    units = ff + weights[1].shape[1]
    tokens = sum(rows.shape[0] for rows in arrays[: len(TOKEN_GROUPS)])
    return pl.pallas_call(
        kernel,
        out_shape=out_shapes,
        in_specs=[whole_in_vmem() for _ in arrays]
        + [pl.BlockSpec(memory_space=pl.ANY) for _ in weights],
        out_specs=[whole_in_vmem() for _ in out_shapes],
        scratch_shapes=[
            pltpu.VMEM((width, units), BF16),
            pltpu.VMEM((width, units), BF16),
            pltpu.VMEM((units, width), BF16),
            pltpu.SemaphoreType.DMA((2 * len(spans(ff)) + 4,)),
        ],
        compiler_params=pltpu.CompilerParams(vmem_limit_bytes=VMEM_BYTES),
        cost_estimate=pl.CostEstimate(
            flops=6 * tokens * width * units,
            bytes_accessed=6 * width * units + 12 * tokens * width,
            transcendentals=tokens * units,
        ),
    )(*arrays, *weights)


def expert_forward(rows, member, own, weights):
    tokens = member.shape[0]
    units = weights[0].shape[1] + weights[1].shape[1]
    shapes = [jax.ShapeDtypeStruct(v.shape, BF16) for v in rows]
    shapes.append(jax.ShapeDtypeStruct(member.shape, F32))
    shapes += [jax.ShapeDtypeStruct((tokens, units), BF16)] * 3
    results = expert_call(forward_kernel, shapes, (*rows, member, own), weights)
    return results[: len(rows)], results[len(rows) :]


def expert_backward(cot, member, own, logits, gate_act, up_act, weights):
    shapes = [jax.ShapeDtypeStruct(v.shape, BF16) for v in cot]
    shapes += [jax.ShapeDtypeStruct(gate_act.shape, BF16)] * 2
    results = expert_call(
        backward_kernel, shapes, (*cot, member, own, logits, gate_act, up_act), weights
    )
    return results[: len(cot)], results[len(cot) :]


def in_weights_kernel(*refs):
    groups = 2 * len(TOKEN_GROUPS)
    rows, grads, outs = refs[:groups], refs[groups : groups + 4], refs[groups + 4 : groups + 8]
    turned = refs[-1]
    for ref, here in row_groups(rows):
        turned[:, here] = ref[...].T
    tokens = grads[0].shape[0]
    ff = outs[0].shape[1]
    for first, last, joined in ((grads[0], grads[1], outs[:2]), (grads[2], grads[3], outs[2:])):
        for out, begin in zip(joined, (0, ff)):
            for start, size in spans(out.shape[1]):
                there = pl.ds(begin + start, size)
                value = product(turned[:, pl.ds(0, tokens)], first[:, there])
                value = value + product(turned[:, pl.ds(tokens, tokens)], last[:, there])
                out[:, pl.ds(start, size)] = value.astype(out.dtype)


def in_weights(rows, gate_back, up_back, ff):
    tokens, units = gate_back[0].shape
    width = rows[0].shape[1]
    whole = pl.BlockSpec((tokens, units), lambda i: (0, 0), pipeline_mode=pl.Buffered(1))
    outs = [((width, ff), BF16), ((width, units - ff), F32)] * 2
    return pl.pallas_call(
        in_weights_kernel,
        grid=(width // WIDE,),
        out_shape=[jax.ShapeDtypeStruct(*out) for out in outs],
        in_specs=[pl.BlockSpec((v.shape[0], WIDE), lambda i: (0, i)) for v in rows] + [whole] * 4,
        out_specs=[pl.BlockSpec((WIDE, shape[1]), lambda i: (i, 0)) for shape, _ in outs],
        scratch_shapes=[pltpu.VMEM((WIDE, 2 * tokens), BF16)],
        compiler_params=pltpu.CompilerParams(vmem_limit_bytes=VMEM_BYTES),
        cost_estimate=pl.CostEstimate(
            flops=8 * tokens * width * units,
            bytes_accessed=4 * tokens * (width + 2 * units) + 4 * width * units,
            transcendentals=0,
        ),
    )(*rows, *gate_back, *up_back)


def down_weights_kernel(hidden_first, hidden_last, *refs):
    groups = 2 * len(TOKEN_GROUPS)
    cot, (out, extra_out), turned = refs[:groups], refs[groups : groups + 2], refs[-1]
    tokens = hidden_first.shape[0]

    @pl.when(pl.program_id(0) == 0)
    def _():
        turned[:, pl.ds(0, tokens)] = hidden_first[...].T
        turned[:, pl.ds(tokens, tokens)] = hidden_last[...].T

    for ref, begin in ((out, 0), (extra_out, out.shape[0])):
        for start, size in spans(ref.shape[0]):
            there = pl.ds(begin + start, size)
            value = sum(product(turned[there, here], group[...]) for group, here in row_groups(cot))
            ref[pl.ds(start, size), :] = value.astype(ref.dtype)


def down_weights(hidden, cot, ff):
    tokens, units = hidden[0].shape
    width = cot[0].shape[1]
    whole = pl.BlockSpec((tokens, units), lambda i: (0, 0), pipeline_mode=pl.Buffered(1))
    outs = [((ff, width), BF16), ((units - ff, width), F32)]
    return pl.pallas_call(
        down_weights_kernel,
        grid=(width // WIDE,),
        out_shape=[jax.ShapeDtypeStruct(*out) for out in outs],
        in_specs=[whole] * 2 + [pl.BlockSpec((v.shape[0], WIDE), lambda i: (0, i)) for v in cot],
        out_specs=[pl.BlockSpec((shape[0], WIDE), lambda i: (0, i)) for shape, _ in outs],
        scratch_shapes=[pltpu.VMEM((units, 2 * tokens), BF16)],
        compiler_params=pltpu.CompilerParams(vmem_limit_bytes=VMEM_BYTES),
        cost_estimate=pl.CostEstimate(
            flops=4 * tokens * width * units,
            bytes_accessed=4 * tokens * (width + units) + 2 * width * units,
            transcendentals=0,
        ),
    )(*hidden, *cot)


class Chips:
    def __init__(self):
        self.n = lax.axis_size("expert")
        self.f = lax.axis_size("fsdp")
        self.chip = lax.axis_index("expert")
        self.core = lax.axis_index("fsdp")

    def bits(self, order):
        return tuple(m for m in order if (m if isinstance(m, int) else m[0]) < self.n)

    def exchange(self, value, mask):
        masks = (mask,) if isinstance(mask, int) else mask
        pairs = [
            (e * self.f + c, (e ^ masks[c % len(masks)]) * self.f + c)
            for e in range(self.n)
            for c in range(self.f)
        ]
        return lax.ppermute(value, BOTH, pairs)

    def other_core(self, value):
        return lax.ppermute(value, "fsdp", [(0, 1), (1, 0)])

    def gather_cores(self, value, axis=0):
        if self.f != 2:
            return lax.all_gather(value, "fsdp", axis=axis, tiled=True)
        other = self.other_core(value)
        first = self.core == 0
        return jnp.concatenate(
            [jnp.where(first, value, other), jnp.where(first, other, value)], axis=axis
        )

    def swap_cores(self, value, split, concat):
        if self.f != 2:
            return lax.all_to_all(value, "fsdp", split_axis=split, concat_axis=concat, tiled=True)
        size = value.shape[split] // 2
        first = self.core == 0
        low = lax.slice_in_dim(value, 0, size, axis=split)
        high = lax.slice_in_dim(value, size, 2 * size, axis=split)
        keep = jnp.where(first, low, high)
        other = self.other_core(jnp.where(first, high, low))
        return jnp.concatenate(
            [jnp.where(first, keep, other), jnp.where(first, other, keep)], axis=concat
        )

    def sum_cores(self, value):
        if self.f != 2:
            return lax.psum(value, "fsdp")
        return value + self.other_core(value)

    def scatter_cores(self, value, axis=0):
        if self.f != 2:
            return lax.psum_scatter(value, "fsdp", scatter_dimension=axis, tiled=True)
        size = value.shape[axis] // 2
        first = self.core == 0
        low = lax.slice_in_dim(value, 0, size, axis=axis)
        high = lax.slice_in_dim(value, size, 2 * size, axis=axis)
        return jnp.where(first, low, high) + self.other_core(jnp.where(first, high, low))

    def lockstep(self, *streams):
        results = [None] * len(streams)
        waiting = {}

        def advance(i, other):
            try:
                waiting[i] = streams[i].send(other)
            except StopIteration as stop:
                waiting.pop(i, None)
                results[i] = stop.value

        for i in range(len(streams)):
            advance(i, None)
        while waiting:
            names = list(waiting)
            over = [i for i in range(len(streams)) if i not in waiting]
            values, kept = together([waiting[i][0] for i in names], [results[i] for i in over])
            for i, result in zip(over, kept):
                results[i] = result
            masks = [waiting[i][1] for i in names]
            others = [v if m is None else self.exchange(v, m) for v, m in zip(values, masks)]
            for i, other in zip(names, others):
                advance(i, other)
        return together(*results)

    def gather_chips(self, value, order):
        done = []
        for mask in self.bits(order):
            other = yield value, mask
            place = sum(m > mask for m in done)
            high = (self.chip // mask) % 2 == 1
            value = jnp.stack(
                [jnp.where(high, other, value), jnp.where(high, value, other)], axis=place
            )
            done.append(mask)
        return value.reshape((self.n,) + value.shape[len(done) :])

    def halves(self, value, mask, width):
        high = (self.chip // mask) % 2 == 1
        run = mask * width
        low_runs = [value[:, i : i + run] for i in range(0, self.n * width, 2 * run)]
        high_runs = [value[:, i : i + run] for i in range(run, self.n * width, 2 * run)]
        pairs = list(zip(low_runs, high_runs))
        keep = [jnp.where(high, h, l) for l, h in pairs]
        send = [jnp.where(high, l, h) for l, h in pairs]
        return jnp.concatenate(keep, axis=1), jnp.concatenate(send, axis=1)

    def scatter_chips(self, value, order, done=()):
        left = [m for m in sorted(self.bits((8, 4, 2, 1)), reverse=True) if m not in done]
        for mask in self.bits(order):
            if mask in done:
                continue
            place = left.index(mask)
            high = (self.chip // mask) % 2
            rest = value.shape[1:]
            split = value.reshape((2,) * len(left) + rest)
            keep = lax.dynamic_index_in_dim(split, high, place, keepdims=False)
            send = lax.dynamic_index_in_dim(split, 1 - high, place, keepdims=False)
            left.remove(mask)
            other = yield send, mask
            value = keep.astype(F32) + other.astype(F32)
            if left:
                value = value.astype(send.dtype)
            value = value.reshape((2 ** len(left),) + rest)
        return value[0]

    def weight_grad(self, rows, grads, order):
        mask = self.bits(order)[0]
        width = rows.shape[1] // self.n
        keep, send = self.halves(rows, mask, width)
        away = inner_rows(send, grads).astype(BF16)
        other = yield away, mask
        value = inner_rows(keep, grads) + other.astype(F32)
        value = value.astype(BF16).reshape(self.n // 2, width, -1)
        return (yield from self.scatter_chips(value, order, (mask,)))

    def gather_groups(self, value, idle=0):
        start = 0
        for size, order in zip(TOKEN_GROUPS, ORDER_TOKENS):
            yield self.gather_tokens(value[start : start + size], order, idle)
            start += size

    def gather_tokens(self, value, order, idle):
        for _ in range(idle):
            yield (), None
        value = value[None]
        for mask in self.bits(order)[:-1]:
            other = yield value, mask
            value = jnp.concatenate([value, other], axis=0)
        return value

    def last_groups(self, groups):
        for value, order in zip(groups, ORDER_TOKENS):
            yield self.last_exchange(value, self.bits(order)[-1])

    def last_exchange(self, value, mask):
        return (yield value, mask)

    def scatter_groups(self, groups, others):
        for value, other, order in zip(groups, others, ORDER_TOKENS):
            yield self.scatter_tokens(value, other, order)

    def scatter_tokens(self, value, other, order):
        order = self.bits(order)
        value = value.astype(F32) + other.astype(F32)
        for masks in reversed(order[:-1]):
            half = value.shape[0] // 2
            value = value.astype(other.dtype)
            received = yield value[half:], masks
            value = value[:half].astype(F32) + received.astype(F32)
        return value[0]


def body(
    tokens,
    segments,
    routes,
    norm_attn,
    query_proj,
    latent_proj,
    norm_latent,
    expand_proj,
    output_proj,
    norm_ffn,
    router,
    shared_gate,
    shared_up,
    shared_down,
    expert_gate,
    expert_up,
    expert_down,
    cotangent,
):
    chips = Chips()
    n, cores, chip, core = chips.n, chips.f, chips.chip, chips.core
    seq = SEQ_DEV * cores
    heads = H // cores
    shard = D // (n * cores)
    expert_count = n * expert_gate.shape[0]
    small_cut = (shard, 2 * shard, 2 * shard + norm_latent.shape[0])

    small = jnp.concatenate([norm_attn, norm_ffn, norm_latent, router.reshape(-1)])[None]
    query_own = chips.swap_cores(query_proj, 1, 0)
    query_cut = query_own.shape[1] // 2
    expand_own = chips.swap_cores(expand_proj, 1, 0)
    width = shared_gate.shape[1] // n

    def shared_weights():
        weights = (shared_gate, shared_up)
        for _ in range(4):
            weights = yield weights, None
        shared_gate_in, shared_up_in = weights
        shared_in = jnp.stack(
            [shared_gate_in.reshape(shard, n, -1), shared_up_in.reshape(shard, n, -1)], 2
        )
        shared_in = lax.all_to_all(
            shared_in.transpose(1, 0, 2, 3).reshape(n * shard, 2 * width),
            "expert",
            split_axis=0,
            concat_axis=0,
            tiled=True,
        ).reshape(n, 1, shard, 2 * width)
        return shared_in

    small, query_first, query_last, expand_weight, latent_own, routes_all, shared_in = chips.lockstep(
        chips.gather_chips(chips.gather_cores(small), ORDER_SMALL),
        chips.gather_chips(query_own[:, :query_cut], ORDER_QUERY[0]),
        chips.gather_chips(query_own[:, query_cut:], ORDER_QUERY[1]),
        chips.gather_chips(expand_own, ORDER_EXPAND),
        chips.gather_chips(latent_proj, ORDER_LATENT),
        chips.gather_chips(routes, ORDER_SMALL),
        shared_weights(),
    )
    shared_in = lax.all_gather(shared_in, "fsdp", axis=1, tiled=True).reshape(D, 2 * width)
    output_own = chips.swap_cores(output_proj, 1, 0)
    output_cut = output_own.shape[1] // 2
    small, query_first, query_last, expand_weight, latent_own, output_own, cot_in, routes_all = together(
        small, query_first, query_last, expand_weight, latent_own, output_own, cotangent, routes_all
    )
    small = small.reshape(n * cores, -1)
    gain_attn = small[:, : small_cut[0]].reshape(-1).astype(F32)
    gain_ffn = small[:, small_cut[0] : small_cut[1]].reshape(-1).astype(F32)
    gain_latent = small[:, small_cut[1] : small_cut[2]].reshape(-1).astype(F32)
    router_all = small[:, small_cut[2] :].reshape(D, -1)
    extra = -(-(width + expert_count) // LANES) * LANES
    router_at = extra - LANES
    gate_extra = jnp.concatenate([shared_in[:, :width], router_all], axis=1)
    gate_extra = jnp.pad(gate_extra, ((0, 0), (0, extra - width - expert_count)))
    up_extra = jnp.pad(shared_in[:, width:], ((0, 0), (0, extra - width)))
    member_pad = (width - router_at, extra - width - expert_count)
    query_parts = [query_first.reshape(D, -1), query_last.reshape(D, -1)]
    expand_weight = expand_weight.reshape(KVR, -1)
    latent_weight = chips.gather_cores(latent_own[:, None], axis=1).reshape(D, -1)
    down_extra = jnp.pad(chips.gather_cores(shared_down), ((0, extra - width), (0, 0)))
    gate_full, up_full, down_full = (
        lax.all_gather(w[0], "fsdp", axis=0, tiled=True)
        for w in (expert_gate, expert_up, expert_down)
    )
    weights = (gate_full, gate_extra, up_full, up_extra, down_full, down_extra)
    ff = gate_full.shape[1]

    positions = jnp.arange(seq, dtype=jnp.int32)
    cos_table, sin_table = rope_tables(positions)
    inputs_f = tokens.astype(F32)
    score_scale = (DN + DR) ** (-0.5)

    def attention():
        yield (), None
        normed_own = rms_scale(inputs_f, gain_attn).astype(BF16)
        normed = chips.gather_cores(normed_own)
        latent = product(normed, latent_weight)
        query_all = jnp.concatenate([product(normed, part) for part in query_parts], axis=1)
        query_all = query_all.reshape(seq, heads, DN + DR)
        query_nope = query_all[..., :DN].astype(BF16)
        query_rope = rotate(
            query_all[..., DN:], cos_table[:, None, :], sin_table[:, None, :]
        ).astype(BF16)
        normed, latent, query_nope, query_rope = yield (
            (normed, latent, query_nope, query_rope),
            None,
        )
        latent_norm = rms_scale(latent[:, :KVR], gain_latent).astype(BF16)
        key_rope = rotate(latent[:, KVR:], cos_table, sin_table).astype(BF16)
        expanded = product(latent_norm, expand_weight).astype(BF16).reshape(seq, heads, DN + DV)
        key_nope = expanded[..., :DN]
        values_all = expanded[..., DN:]
        allowed = (positions[:, None] >= positions[None, :]) & (
            segments[:, None] == segments[None, :]
        )
        scores = jnp.einsum("thd,shd->hts", query_nope, key_nope, preferred_element_type=F32)
        scores = scores + jnp.einsum(
            "thd,sd->hts", query_rope, key_rope, preferred_element_type=F32
        )
        scores = jnp.where(allowed[None], scores * score_scale, -1e30)
        shifted = jnp.exp(scores - jnp.max(scores, axis=-1, keepdims=True))
        probs = shifted / jnp.sum(shifted, axis=-1, keepdims=True)
        latent_norm, key_rope, key_nope, values_all, probs = yield (
            (latent_norm, key_rope, key_nope, values_all, probs),
            None,
        )
        probs_low = probs.astype(BF16)
        attended = jnp.einsum("hts,shd->thd", probs_low, values_all, preferred_element_type=F32)
        attended = attended.reshape(seq, heads * DV).astype(BF16)
        attended = yield chips.gather_cores(attended, axis=1), None
        return (
            normed, latent, query_nope, query_rope, latent_norm, key_rope, key_nope, values_all,
            probs, probs_low, attended,
        )

    output_first, output_last, *cot_first, kept_attention = chips.lockstep(
        chips.gather_chips(output_own[:, :output_cut], ORDER_OUTPUT[0]),
        chips.gather_chips(output_own[:, output_cut:], ORDER_OUTPUT[1]),
        *chips.gather_groups(cot_in, idle=1),
        attention(),
    )
    (
        normed, latent, query_nope, query_rope, latent_norm, key_rope, key_nope, values_all,
        probs, probs_low, attended,
    ) = kept_attention
    output_parts = [output_first.reshape(D, -1), output_last.reshape(D, -1)]
    hidden = jnp.concatenate([product(attended, part) for part in output_parts], axis=1)
    hidden = inputs_f + chips.swap_cores(hidden, 0, 1)
    normed_ffn = rms_scale(hidden, gain_ffn).astype(BF16)

    half = n // 2

    def here_and_there(blocks):
        halves = []
        for last in (False, True):
            parts, start = [], 0
            for size, order in zip(TOKEN_GROUPS, ORDER_TOKENS):
                order = chips.bits(order)
                turns = [0]
                for mask in order[:-1]:
                    turns = turns + [t ^ mask for t in turns]
                turns = jnp.array([t ^ order[-1] if last else t for t in turns], jnp.int32)
                rows = jnp.take(blocks, chip ^ turns, axis=0)[:, start : start + size]
                parts.append(rows.reshape((half * size,) + rows.shape[2:]))
                start += size
            halves.append(jnp.concatenate(parts, axis=0))
        return halves

    members = []
    for routes_half in here_and_there(routes_all):
        member = jnp.any(
            routes_half[:, :, None] == jnp.arange(expert_count, dtype=jnp.int32), axis=1
        )
        members.append(jnp.pad(member.astype(F32), ((0, 0), member_pad)))
    own = (jnp.arange(expert_count, dtype=jnp.int32) == chip).astype(F32)
    own = jnp.pad(own, member_pad)[None]

    def flat(groups):
        return [v.reshape(-1, D) for v in groups]

    def blocks(groups):
        return [v.reshape(half, -1, D) for v in groups]

    def forward(groups, member):
        rows = flat(groups)
        out, (logits, gate_act, up_act, hidden_act) = expert_forward(rows, member, own, weights)
        return blocks(out), (rows, logits, gate_act, up_act, hidden_act)

    def backward(kept, groups, member):
        _, logits, gate_act, up_act, _ = kept
        cot = flat(groups)
        back, (gate_back, up_back) = expert_backward(
            cot, member, own, logits, gate_act, up_act, weights
        )
        return blocks(back), (cot, gate_back, up_back)

    def beside(function, *values):
        values = yield values, None
        return function(*values)

    rows_first = chips.lockstep(*chips.gather_groups(normed_ffn))
    *rows_last, (out_first, kept_first) = chips.lockstep(
        *chips.last_groups(rows_first), beside(forward, rows_first, members[0])
    )
    cot_first, rows_last = together(cot_first, rows_last)
    *cot_last, (out_last, kept_last) = chips.lockstep(
        *chips.last_groups(cot_first), beside(forward, rows_last, members[1])
    )
    *sent_out, (back_last, grads_last) = chips.lockstep(
        *chips.last_groups(out_last), beside(backward, kept_last, cot_last, members[1])
    )
    *sent_back, (back_first, grads_first) = chips.lockstep(
        *chips.last_groups(back_last), beside(backward, kept_first, cot_first, members[0])
    )

    def expert_grads(kept, grads):
        kept, grads = yield (kept, grads), None
        gate_w, gate_extra_w, up_w, up_extra_w = in_weights(
            [v for half_rows in kept for v in half_rows[0]],
            [half_grads[1] for half_grads in grads],
            [half_grads[2] for half_grads in grads],
            ff,
        )
        gate_w, gate_extra_w, up_w, up_extra_w, kept, grads = yield (
            (gate_w, gate_extra_w, up_w, up_extra_w, kept, grads),
            None,
        )
        down_w, down_extra_w = down_weights(
            [half_rows[4] for half_rows in kept], [v for half_grads in grads for v in half_grads[0]], ff
        )
        return gate_w, up_w, down_w, gate_extra_w, up_extra_w, down_extra_w

    *ffn_grad, expert_w = chips.lockstep(
        *chips.scatter_groups(back_first, sent_back),
        expert_grads((kept_first, kept_last), (grads_first, grads_last)),
    )
    ffn_grad = jnp.concatenate(ffn_grad, axis=0)
    gate_grad_w, up_grad_w, down_grad_w = (
        lax.psum_scatter(v, "fsdp", scatter_dimension=0, tiled=True).astype(F32)[None]
        for v in expert_w[:3]
    )
    gate_extra_w, up_extra_w, down_extra_w = expert_w[3:]
    router_grad = gate_extra_w[:, width : width + expert_count]
    shared_in_grad = jnp.concatenate([gate_extra_w[:, :width], up_extra_w[:, :width]], axis=1)
    shared_in_grad = chips.scatter_cores(shared_in_grad.reshape(n, cores * shard, 2 * width), 1)
    shared_in_grad = lax.all_to_all(
        shared_in_grad.astype(BF16), "expert", split_axis=0, concat_axis=0, tiled=True
    )
    shared_in_grad = shared_in_grad.astype(F32).reshape(n, shard, 2, width).transpose(2, 1, 0, 3)
    shared_in_grad = shared_in_grad.reshape(2, shard, n * width)
    shared_down_grad = chips.scatter_cores(down_extra_w[:width])

    _, norm_pull = jax.vjp(rms_scale, hidden, gain_ffn)
    hidden_part, gain_ffn_grad = norm_pull(ffn_grad)
    hidden_grad = cotangent.astype(F32) + hidden_part
    hidden_grad, out_first, sent_out = together(hidden_grad, out_first, sent_out)
    attn_grad_own = hidden_grad.astype(BF16)
    attn_grad = chips.swap_cores(attn_grad_own, 1, 0)

    def attention_back():
        yield (), None
        attended_grad = outer_cols(attn_grad[:, :output_cut], output_parts[0]) + outer_cols(
            attn_grad[:, output_cut:], output_parts[1]
        )
        attended_grad = chips.scatter_cores(attended_grad, 1).astype(BF16)
        attended_grad = attended_grad.reshape(seq, heads, DV)
        prob_grad = jnp.einsum("thd,shd->hts", attended_grad, values_all, preferred_element_type=F32)
        weighted = jnp.sum(probs * prob_grad, axis=-1, keepdims=True)
        score_grad = (probs * (prob_grad - weighted)).astype(BF16)
        query_nope_grad = score_scale * jnp.einsum(
            "hts,shd->thd", score_grad, key_nope, preferred_element_type=F32
        )
        query_rope_grad = score_scale * jnp.einsum(
            "hts,sd->thd", score_grad, key_rope, preferred_element_type=F32
        )
        key_nope_grad = score_scale * jnp.einsum(
            "hts,thd->shd", score_grad, query_nope, preferred_element_type=F32
        )
        key_rope_grad = score_scale * jnp.einsum(
            "hts,thd->sd", score_grad, query_rope, preferred_element_type=F32
        )
        values_grad = jnp.einsum(
            "hts,thd->shd", probs_low, attended_grad, preferred_element_type=F32
        )
        (query_nope_grad, query_rope_grad, key_nope_grad, key_rope_grad, values_grad) = yield (
            (query_nope_grad, query_rope_grad, key_nope_grad, key_rope_grad, values_grad),
            None,
        )
        expanded_grad = jnp.concatenate([key_nope_grad, values_grad], axis=2)
        expanded_grad = expanded_grad.reshape(seq, heads * (DN + DV)).astype(BF16)
        latent_back = chips.sum_cores(
            jnp.concatenate([outer_cols(expanded_grad, expand_weight), key_rope_grad], axis=1)
        )
        _, latent_pull = jax.vjp(rms_scale, latent[:, :KVR], gain_latent)
        latent_nope_grad, gain_latent_grad = latent_pull(latent_back[:, :KVR])
        gain_latent_grad = gain_latent_grad / cores
        latent_rope_grad = rotate(latent_back[:, KVR:], cos_table, -sin_table)
        latent_grad = jnp.concatenate([latent_nope_grad, latent_rope_grad], axis=1).astype(BF16)
        query_back = jnp.concatenate(
            [query_nope_grad, rotate(query_rope_grad, cos_table[:, None, :], -sin_table[:, None, :])],
            axis=2,
        )
        query_back = query_back.reshape(seq, heads * (DN + DR)).astype(BF16)
        query_back, expanded_grad, latent_grad, gain_latent_grad = yield (
            (query_back, expanded_grad, latent_grad, gain_latent_grad),
            None,
        )
        return query_back, expanded_grad, latent_grad, gain_latent_grad

    output_first_grad, output_last_grad, *block_sum, kept_back = chips.lockstep(
        chips.weight_grad(attended, attn_grad[:, :output_cut], BACK_OUTPUT[0]),
        chips.weight_grad(attended, attn_grad[:, output_cut:], BACK_OUTPUT[1]),
        *chips.scatter_groups(out_first, sent_out),
        attention_back(),
    )
    query_back, expanded_grad, latent_grad, gain_latent_grad = kept_back
    output_grad = jnp.concatenate([output_first_grad, output_last_grad], axis=1)
    output_grad = chips.swap_cores(output_grad, 0, 1)

    normed_part = lax.dynamic_index_in_dim(
        normed.reshape(seq, n, cores, shard), core, 2, keepdims=False
    ).reshape(seq, n * shard)
    query_first_grad, query_last_grad, expand_grad, latent_weight_grad = chips.lockstep(
        chips.weight_grad(normed, query_back[:, :query_cut], BACK_QUERY[0]),
        chips.weight_grad(normed, query_back[:, query_cut:], BACK_QUERY[1]),
        chips.weight_grad(latent_norm, expanded_grad, BACK_EXPAND),
        chips.weight_grad(normed_part, latent_grad, BACK_LATENT),
    )
    query_grad = jnp.concatenate([query_first_grad, query_last_grad], axis=1)
    query_grad = chips.swap_cores(query_grad, 0, 1)
    expand_grad = chips.swap_cores(expand_grad, 0, 1)

    normed_grad = outer_cols(query_back[:, :query_cut], query_parts[0]) + outer_cols(
        query_back[:, query_cut:], query_parts[1]
    )
    latent_grad_own = lax.dynamic_slice_in_dim(latent_grad, core * SEQ_DEV, SEQ_DEV, 0)
    normed_grad = chips.scatter_cores(normed_grad) + outer_cols(latent_grad_own, latent_weight)
    _, first_pull = jax.vjp(rms_scale, inputs_f, gain_attn)
    input_part, gain_attn_grad = first_pull(normed_grad)
    tokens_grad = (hidden_grad + input_part).astype(BF16)

    block_out = (hidden + jnp.concatenate(block_sum, axis=0)).astype(BF16)
    small_grad = jnp.concatenate(
        [
            gain_attn_grad.reshape(n * cores, -1),
            gain_ffn_grad.reshape(n * cores, -1),
            gain_latent_grad.reshape(n * cores, -1),
            router_grad.reshape(n * cores, -1),
        ],
        axis=1,
    )
    (small_grad,) = chips.lockstep(
        chips.scatter_chips(small_grad.reshape(n, cores, -1), ORDER_SMALL[::-1])
    )
    small_grad = chips.scatter_cores(small_grad).reshape(-1)
    return (
        block_out,
        tokens_grad,
        small_grad[: small_cut[0]],
        query_grad,
        latent_weight_grad,
        small_grad[small_cut[1] : small_cut[2]],
        expand_grad,
        output_grad,
        small_grad[small_cut[0] : small_cut[1]],
        small_grad[small_cut[2] :].reshape(shard, -1),
        shared_in_grad[0],
        shared_in_grad[1],
        shared_down_grad,
        gate_grad_w,
        up_grad_w,
        down_grad_w,
    )


def solution(mesh):
    rows = P(("expert", "fsdp"), None)
    flat = P(("expert", "fsdp"))
    experts = P("expert", "fsdp", None)
    return jax.shard_map(
        body,
        mesh=mesh,
        in_specs=(
            rows, P("expert"), rows, flat, rows, rows, flat, rows, rows, flat, rows, rows, rows,
            rows, experts, experts, experts, rows,
        ),
        out_specs=(
            rows, rows, flat, rows, rows, flat, rows, rows, flat, rows, rows, rows, rows, experts,
            experts, experts,
        ),
        check_vma=False,
    )
```

time: 1170 us -> 982 us (0.84)
  matrix products: 265 us -> 44.7 us
  waiting for transfers between devices: 542 us -> 332 us
  Pallas kernels: 0 us -> 193 us
  starting transfers between devices: 113 us -> 145 us
  other arithmetic: 117 us -> 143 us
    ppermute x76 -> x108, waiting for transfers between devices: 538 us -> 327 us  [exchange(): return lax.ppermute(value, BOTH, pairs)]
    pallas_call x0 -> x6, Pallas kernels: none -> 193 us  [the longest x4 129 us: expert_call(): pl.pallas_call(kernel, out_shape=out_shapes, in_specs=[whole_in_vmem() fo...]
    dot_general x16 -> x6, matrix products: 80.9 us -> 10.3 us  [outer_cols(): lax.dot_general(left_side, right_side, (((1,), (1,)), ((), ())), preferre...]
    dot_general x16 -> x6, matrix products: 75.1 us -> 5.22 us  [product(): return jnp.dot(left_side, right_side, preferred_element_type=F32)]
    dot_general x16 -> x12, matrix products: 69.2 us -> 21.1 us  [inner_rows(): lax.dot_general(left_side, right_side, (((0,), (0,)), ((), ())), preferre...]
    ppermute x76 -> x108, starting transfers between devices: 92.1 us -> 131 us  [exchange(): return lax.ppermute(value, BOTH, pairs)]
    dot_general x17 -> x8, matrix products: 39.5 us -> 4.81 us  [the longest x1 1.77 us: attention(): jnp.einsum('thd,sd->hts', query_rope, key_rope, preferred_element_type=F32)]
    concatenate x18 -> x30, other arithmetic: 15.5 us -> 31 us  [the longest x18 25.3 us: gather_tokens(): value = jnp.concatenate([value, other], axis=0)]
  transfers between devices with their start and end apart: 101 -> 136, of which waited for: 55 -> 66; matrix products, arithmetic and copies ran while one was open for 41% -> 24% of each run, Pallas kernels for 0% -> 20%
where the time goes in v2:
time: 982 us; the launch traced here: 971 us
  waiting for transfers between devices  332 us (34%)
  Pallas kernels  193 us (20%)
  starting transfers between devices  145 us (15%)
  other arithmetic  143 us (15%)
  local copies, waits for them, and re-layouts  94.4 us (10%)
  matrix products  44.7 us (5%)
  between operations  18.6 us (2%)
    ppermute x108, waiting for transfers between devices, exchange(): return lax.ppermute(value, BOTH, pairs)  327 us
    ppermute x108, starting transfers between devices, exchange(): return lax.ppermute(value, BOTH, pairs)  131 us
    pallas_call x4, Pallas kernels, expert_call(): pl.pallas_call(kernel, out_shape=out_shapes, in_specs=[whole_in_vmem() fo...  129 us
    pallas_call x1, Pallas kernels, in_weights(): pl.pallas_call(in_weights_kernel, grid=(width // WIDE,), out_shape=[jax.S...  38.8 us
    unnamed x443, local copies, waits for them, and re-layouts  25.4 us
    concatenate x18, other arithmetic, gather_tokens(): value = jnp.concatenate([value, other], axis=0)  25.3 us
    pallas_call x1, Pallas kernels, down_weights(): pl.pallas_call(down_weights_kernel, grid=(width // WIDE,), out_shape=[jax...  25 us
    another operation x62, other arithmetic, gather_chips(): jnp.stack([jnp.where(high, other, value), jnp.where(high, value, other)],...  21.2 us
  transfers between devices with their start and end apart: 136, of which 66 were waited for; matrix products, arithmetic and copies ran while one was open for 24% of the time, Pallas kernels for 20%

profile of v2, /device:TPU:0, one launch (start us, length us, event | category | flops | bytes accessed | tf_op | source)
XLA Modules:
  0.0 970.8 jit_solution(7493766194187348931)
XLA Ops:
  25.2 3.4 collective-permute-done.3
  28.7 9.4 collective-permute-done.7
  40.9 4.1 collective-permute-done.4
  45.1 3.6 collective-permute-done.5
  55.0 7.3 collective-permute-done.9
  68.6 14.9 %collective-permute-done.15 = bf16[2,2,2,1168]{3,2,1,0:T(2,128)(2,1)S(1)} collective-permute-done((bf16[2,2,2,1168]{3,2,1,0:T(2,128)(2,1)S(1)}, bf16[2,2,2,1168]{3,2,1,0:T(2,128)(2,1)S(1)}, u32[]{:S(2)}, u32[]{:S(2)}) %collective-permute-start.15) | collective-permute-done | bytes 18720 | tf_op jit(solution)/shard_map/ppermute | solution.py:370
  99.3 4.4 all-to-all-start
  111.0 30.0 %collective-permute-done.21 = bf16[2,2,2,2,1168]{4,3,2,1,0:T(2,128)(2,1)S(1)} collective-permute-done((bf16[2,2,2,2,1168]{4,3,2,1,0:T(2,128)(2,1)S(1)}, bf16[2,2,2,2,1168]{4,3,2,1,0:T(2,128)(2,1)S(1)}, u32[]{:S(2)}, u32[]{:S(2)}) %collective-permute-start.21) | collective-permute-done | bytes 37408 | tf_op jit(solution)/shard_map/ppermute | solution.py:370
  168.3 3.4 collective-permute-start.28
  173.3 8.6 collective-permute-done.28
  193.7 3.3 copy.195
  209.7 3.4 fusion.8
  223.4 9.9 %collective-permute-done.35 = bf16[1,48,2048]{2,1,0:T(8,128)(2,1)S(1)} collective-permute-done((bf16[1,48,2048]{2,1,0:T(8,128)(2,1)S(1)}, bf16[1,48,2048]{2,1,0:T(8,128)(2,1)S(1)}, u32[]{:S(2)}, u32[]{:S(2)}) %collective-permute-start.35) | collective-permute-done | bytes 196640 | tf_op jit(solution)/shard_map/ppermute | solution.py:370
  244.1 5.1 collective-permute-done.41
  256.2 7.0 collective-permute-done.38
  276.5 5.5 collective-permute-done.47
  292.7 15.3 %collective-permute-done.44 = bf16[2,2,2,128,512]{4,3,0,1,2:T(8,128)(2,1)} collective-permute-done((bf16[2,2,2,128,512]{4,3,0,1,2:T(8,128)(2,1)}, bf16[2,2,2,128,512]{4,3,0,1,2:T(8,128)(2,1)}, u32[]{:S(2)}, u32[]{:S(2)}) %collective-permute-start.44) | collective-permute-done | bytes 1048608 | tf_op jit(solution)/shard_map/ppermute | solution.py:370
  321.1 13.9 %collective-permute-done.51 = bf16[1,32,2048]{2,1,0:T(8,128)(2,1)S(1)} collective-permute-done((bf16[1,32,2048]{2,1,0:T(8,128)(2,1)S(1)}, bf16[1,32,2048]{2,1,0:T(8,128)(2,1)S(1)}, u32[]{:S(2)}, u32[]{:S(2)}) %collective-permute-start.51) | collective-permute-done | bytes 131104 | tf_op jit(solution)/shard_map/ppermute | solution.py:370
  335.7 3.5 collective-permute-done.50
  339.2 3.4 collective-permute-done.49
  346.7 3.8 collective-permute-done.54
  369.5 5.0 collective-permute-done.56
  382.9 29.8 %shard_map.351 = (bf16[384,2048]{1,0:T(8,128)(2,1)}, bf16[384,2048]{1,0:T(8,128)(2,1)}, bf16[256,2048]{1,0:T(8,128)(2,1)}, f32[1024,128]{1,0:T(8,128)}, bf16[102...) custom-call(bf16[384,2048]{1,0:T(8,128)(2,1)} %bitcast.105.refs_0_, ...), custom_call_target="tpu_custom_call" | custom-call | flops 20937965568 | bytes 45613056 | tf_op jit(solution)/shard_map/pallas_call | solution.py:237
  417.7 29.5 %shard_map.352 = (bf16[384,2048]{1,0:T(8,128)(2,1)}, bf16[384,2048]{1,0:T(8,128)(2,1)}, bf16[256,2048]{1,0:T(8,128)(2,1)}, f32[1024,128]{1,0:T(8,128)}, bf16[102...) custom-call(bf16[384,2048]{1,0:T(8,128)(2,1)} %bitcast.116.refs_0_.refs_3_, ...), custom_call_target="tpu_custom_call" | custom-call | flops 20937965568 | bytes 45613056 | tf_op jit(solution)/shard_map/pallas_call | solution.py:237
  452.2 35.1 %shard_map.353 = (bf16[384,2048]{1,0:T(8,128)(2,1)}, bf16[384,2048]{1,0:T(8,128)(2,1)}, bf16[256,2048]{1,0:T(8,128)(2,1)}, bf16[1024,1664]{1,0:T(8,128)(2,1)}, bf16[1024,1664]{1,0:T(8,128)(2,1)}) custom-call(bf16[384,2048]{1,0:T(8,128)(2,1)} %bitcast.122.refs_0_.refs_3_, bf16[384,2048]{1,0:T(8,128)(2,1)} %bitcast.123.refs_1_.refs_4_, ...), custom_call_target="tpu_custom_call" | custom-call | flops 20937965568 | bytes 45613056 | tf_op jit(solution)/shard_map/pallas_call | solution.py:237
  490.6 34.8 %shard_map.354 = (bf16[384,2048]{1,0:T(8,128)(2,1)}, bf16[384,2048]{1,0:T(8,128)(2,1)}, bf16[256,2048]{1,0:T(8,128)(2,1)}, bf16[1024,1664]{1,0:T(8,128)(2,1)}, bf16[1024,1664]{1,0:T(8,128)(2,1)}) custom-call(bf16[384,2048]{1,0:T(8,128)(2,1)} %bitcast.519, bf16[384,2048]{1,0:T(8,128)(2,1)} %bitcast.517, bf16[256,2048]{1,0:T(8,128)(2,1)} %bitcast.527, ...), custom_call_target="tpu_custom_call" | custom-call | flops 20937965568 | bytes 45613056 | tf_op jit(solution)/shard_map/pallas_call | solution.py:237
  537.4 38.8 %shard_map.355 = (bf16[2048,1408]{1,0:T(8,128)(2,1)}, f32[2048,256]{1,0:T(8,128)}, bf16[2048,1408]{1,0:T(8,128)(2,1)}, f32[2048,256]{1,0:T(8,128)}) custom-call(bf16[384,2048]{1,0:T(8,128)(2,1)} %bitcast.105.refs_0_, bf16[384,2048]{1,0:T(8,128)(2,1)} %bitcast.106.refs_1_, bf16[256,2048]{1,0:T(8,128)(2,1)} %bitcast.107.refs_2_, ...), custom_call_target="tpu_custom_call" | custom-call | flops 27917287424 | bytes 35651584 | tf_op jit(solution)/shard_map/pallas_call | solution.py:299
  585.3 25.0 %shard_map.356 = (bf16[1408,2048]{1,0:T(8,128)(2,1)}, f32[256,2048]{1,0:T(8,128)}) custom-call(bf16[1024,1664]{1,0:T(8,128)(2,1)} %get-tuple-element.588.hidden_first, bf16[1024,1664]{1,0:T(8,128)(2,1)} %get-tuple-element.589.hidden_last, bf16[384,2048]{1,0:T(8,128)(2,1)} %bitcast.520, bf16[384,2048]{1,0:T(8,128)(2,1)} %bitcast.518, ...), custom_call_target="tpu_custom_call" | custom-call | flops 13958643712 | bytes 22020096 | tf_op jit(solution)/shard_map/pallas_call | solution.py:337
  616.7 6.6 collective-permute-done.79
  666.5 10.8 %collective-permute-done.85 = bf16[4,32,2048]{2,1,0:T(8,128)(2,1)S(1)} collective-permute-done((bf16[4,32,2048]{2,1,0:T(8,128)(2,1)S(1)}, bf16[4,32,2048]{2,1,0:T(8,128)(2,1)S(1)}, u32[]{:S(2)}, u32[]{:S(2)}) %collective-permute-start.85) | collective-permute-done | bytes 524320 | tf_op jit(solution)/shard_map/ppermute | solution.py:370
  679.9 4.4 collective-permute-done.84
  685.8 9.8 %collective-permute-done.83 = bf16[4,48,2048]{2,1,0:T(8,128)(2,1)S(1)} collective-permute-done((bf16[4,48,2048]{2,1,0:T(8,128)(2,1)S(1)}, bf16[4,48,2048]{2,1,0:T(8,128)(2,1)S(1)}, u32[]{:S(2)}, u32[]{:S(2)}) %collective-permute-start.83) | collective-permute-done | bytes 786464 | tf_op jit(solution)/shard_map/ppermute | solution.py:370
  701.7 7.1 collective-permute-done.82
  730.8 5.8 collective-permute-done.90
  739.3 10.7 %collective-permute-done.88 = bf16[2,2,128,512]{3,2,0,1:T(8,128)(2,1)S(1)} collective-permute-done((bf16[2,2,128,512]{3,2,0,1:T(8,128)(2,1)S(1)}, bf16[2,2,128,512]{3,2,0,1:T(8,128)(2,1)S(1)}, u32[]{:S(2)}, u32[]{:S(2)}) %collective-permute-start.88) | collective-permute-done | bytes 524320 | tf_op jit(solution)/shard_map/ppermute | solution.py:370
  763.3 8.0 collective-permute-done.97
  783.9 6.8 all-to-all-start.1
  794.5 20.4 %collective-permute-done.98 = bf16[128,512]{1,0:T(8,128)(2,1)S(1)} collective-permute-done((bf16[128,512]{1,0:T(8,128)(2,1)}, bf16[128,512]{1,0:T(8,128)(2,1)S(1)}, u32[]{:S(2)}, u32[]{:S(2)}) %collective-permute-start.98) | collective-permute-done | bytes 131104 | tf_op jit(solution)/shard_map/ppermute | solution.py:370
  834.4 4.3 reshape.588
  851.4 4.2 fusion.18
  858.1 4.2 collective-permute-done.101
  887.1 5.0 collective-permute-done.113
  892.2 10.7 %collective-permute-done.112 = bf16[2,2,32,2048]{3,2,0,1:T(8,128)(2,1)S(1)} collective-permute-done((bf16[2,2,32,2048]{3,2,0,1:T(8,128)(2,1)S(1)}, bf16[2,2,32,2048]{3,2,0,1:T(8,128)(2,1)S(1)}, u32[]{:S(2)}, u32[]{:S(2)}) %collective-permute-start.112) | collective-permute-done | bytes 524320 | tf_op jit(solution)/shard_map/ppermute | solution.py:370
  924.9 10.7 %collective-permute-done.121 = bf16[64,576]{1,0:T(8,128)(2,1)S(1)} collective-permute-done((bf16[64,576]{1,0:T(8,128)(2,1)S(1)}, bf16[64,576]{1,0:T(8,128)(2,1)S(1)}, u32[]{:S(2)}, u32[]{:S(2)}) %collective-permute-start.121) | collective-permute-done | bytes 73760 | tf_op jit(solution)/shard_map/ppermute | solution.py:370
  938.5 4.2 collective-permute-done.119
  949.0 5.1 bitcast_convert_fusion
  954.1 4.7 bitcast_convert_fusion.1
  958.8 4.7 bitcast_convert_fusion.2
  (1087 shorter events, 442.9 us)
Async XLA Ops:
  22.1 23.0 %collective-permute-start.4 = (bf16[128,768]{1,0:T(8,128)(2,1)S(1)}, bf16[128,768]{1,0:T(8,128)(2,1)S(1)}, u32[]{:S(2)}, u32[]{:S(2)}) collective-permute-start(bf16[128,768]{1,0:T(8,128)(2,1)S(1)} %get-tuple-element.361), channel_id=1, source_target_pairs={{0,16},{1,17},{2,18},{3,19},{4,20},{5,21},{6,22},{7,23},{8,24},{9,... | collective-permute-start | bytes 589832 | tf_op jit(solution)/shard_map/ppermute | solution.py:370
  24.6 24.0 %collective-permute-start.5 = (bf16[128,768]{1,0:T(8,128)(2,1)S(1)}, bf16[128,768]{1,0:T(8,128)(2,1)S(1)}, u32[]{:S(2)}, u32[]{:S(2)}) collective-permute-start(bf16[128,768]{1,0:T(8,128)(2,1)S(1)} %get-tuple-element.362), channel_id=1, source_target_pairs={{0,16},{1,17},{2,18},{3,19},{4,20},{5,21},{6,22},{7,23},{8,24},{9,... | collective-permute-start | bytes 589832 | tf_op jit(solution)/shard_map/ppermute | solution.py:370
  93.1 48.8 %collective-permute-start.25 = (bf16[2,2,2,64,576]{4,3,2,1,0:T(8,128)(2,1)}, bf16[2,2,2,64,576]{4,3,2,1,0:T(8,128)(2,1)}, u32[]{:S(2)}, u32[]{:S(2)}) collective-permute-start(bf16[2,2,2,64,576]{4,3,2,1,0:T(8,128)(2,1)} %pad_maximum_fusion.30), channel_id=1, source_target_pairs={{0,8},{1,9},{2,10},{3,11},{4,12},{5,13},{6,14},{7,15},{8,0},{9,1},... | collective-permute-start | bytes 1769480 | tf_op jit(solution)/shard_map/ppermute | solution.py:370
  99.3 51.8 %all-to-all-start = ((bf16[16,64,352]{2,1,0:T(8,128)(2,1)}), bf16[16,64,352]{2,1,0:T(8,128)(2,1)}, u32[]{:S(2)}, u32[]{:S(2)}) async-start(bf16[16,64,352]{2,1,0:T(8,128)(2,1)} %all_to_all.9), calls=%async_computation | async-start | bytes 1572864 | tf_op jit(solution)/shard_map/all_to_all | solution.py:566
  103.7 256.5 %all-gather.8.cloned.1.call-start = ((), (), s32[]{:S(2)}) async-start(), calls=%async_computation.5 | async-start | bytes 2359296 | tf_op jit(solution)/shard_map/all_gather | solution.py:584
  103.8 40.6 %collective-permute-start.24 = (bf16[2,2,2,32,2048]{4,3,2,1,0:T(8,128)(2,1)}, bf16[2,2,2,32,2048]{4,3,2,1,0:T(8,128)(2,1)S(1)}, u32[]{:S(2)}, u32[]{:S(2)}) collective-permute-start(bf16[2,2,2,32,2048]{4,3,2,1,0:T(8,128)(2,1)} %pad_maximum_fusion.15), channel_id=1, source_target_pairs={{0,8},{1,9},{2,10},{3,11},{4,12},{5,13},{6,14},{7,15},{8,0},{9,1},... | collective-permute-start | bytes 3145736 | tf_op jit(solution)/shard_map/ppermute | solution.py:370
  105.6 39.7 %collective-permute-start.23 = (bf16[2,2,2,128,768]{4,3,0,2,1:T(8,128)(2,1)}, bf16[2,2,2,128,768]{4,3,0,2,1:T(8,128)(2,1)S(1)}, u32[]{:S(2)}, u32[]{:S(2)}) collective-permute-start(bf16[2,2,2,128,768]{4,3,0,2,1:T(8,128)(2,1)} %pad_maximum_fusion.8), channel_id=1, source_target_pairs={{0,2},{1,3},{2,0},{3,1},{4,6},{5,7},{6,4},{7,5},{8,10},{9,11},{10,... | collective-permute-start | bytes 4718600 | tf_op jit(solution)/shard_map/ppermute | solution.py:370
  107.1 41.9 %collective-permute-start.22 = (bf16[2,2,2,128,768]{4,3,2,1,0:T(8,128)(2,1)}, bf16[2,2,2,128,768]{4,3,2,1,0:T(8,128)(2,1)S(1)}, u32[]{:S(2)}, u32[]{:S(2)}) collective-permute-start(bf16[2,2,2,128,768]{4,3,2,1,0:T(8,128)(2,1)} %pad_maximum_fusion.7), channel_id=1, source_target_pairs={{0,4},{1,5},{2,6},{3,7},{4,0},{5,1},{6,2},{7,3},{8,12},{9,13},{10,... | collective-permute-start | bytes 4718600 | tf_op jit(solution)/shard_map/ppermute | solution.py:370
  108.6 32.4 %collective-permute-start.21 = (bf16[2,2,2,2,1168]{4,3,2,1,0:T(2,128)(2,1)S(1)}, bf16[2,2,2,2,1168]{4,3,2,1,0:T(2,128)(2,1)S(1)}, u32[]{:S(2)}, u32[]{:S(2)}) collective-permute-start(bf16[2,2,2,2,1168]{4,3,2,1,0:T(2,128)(2,1)S(1)} %pad_maximum_fusion.60), channel_id=1, source_target_pairs={{0,16},{1,17},{2,18},{3,19},{4,20},{5,21},{6,22},{7,23},{8,24},{9,... | collective-permute-start | bytes 112136 | tf_op jit(solution)/shard_map/ppermute | solution.py:370
  151.1 231.7 %all-gather.10.cloned.1.call-start = ((), (), s32[]{:S(2)}) async-start(), calls=%async_computation.9 | async-start | bytes 8650752 | tf_op jit(solution)/shard_map/all_gather | solution.py:606
  151.9 230.9 %all-gather.12.cloned.1.call-start = ((), (), s32[]{:S(2)}) async-start(), calls=%async_computation.10 | async-start | bytes 8650752 | tf_op jit(solution)/shard_map/all_gather | solution.py:606
  152.8 230.1 %all-gather.14.cloned.1.call-start = ((), (), s32[]{:S(2)}) async-start(), calls=%async_computation.11 | async-start | bytes 8650752 | tf_op jit(solution)/shard_map/all_gather | solution.py:606
  153.5 795.5 %reduce-scatter.8.cloned.1.call-start = ((), (), s32[]{:S(2)}) async-start(), calls=%async_computation.8 | async-start | bytes 8650752 | tf_op jit(solution)/shard_map/reduce_scatter | solution.py:763
  173.0 28.6 %collective-permute-start.31 = (bf16[16,1,64,576]{3,2,0,1:T(8,128)(2,1)}, bf16[16,1,64,576]{3,2,0,1:T(8,128)(2,1)}, u32[]{:S(2)}, u32[]{:S(2)}) collective-permute-start(bf16[16,1,64,576]{3,2,0,1:T(8,128)(2,1)} %bitcast.500), channel_id=1, source_target_pairs={{0,1},{1,0},{2,3},{3,2},{4,5},{5,4},{6,7},{7,6},{8,9},{9,8},{10,11... | collective-permute-start | bytes 3538952 | tf_op jit(solution)/shard_map/ppermute | solution.py:373
  269.6 38.4 %collective-permute-start.44 = (bf16[2,2,2,128,512]{4,3,0,1,2:T(8,128)(2,1)}, bf16[2,2,2,128,512]{4,3,0,1,2:T(8,128)(2,1)}, u32[]{:S(2)}, u32[]{:S(2)}) collective-permute-start(bf16[2,2,2,128,512]{4,3,0,1,2:T(8,128)(2,1)} %pad_maximum_fusion.18), channel_id=1, source_target_pairs={{0,8},{1,9},{2,10},{3,11},{4,12},{5,13},{6,14},{7,15},{8,0},{9,1},... | collective-permute-start | bytes 3145736 | tf_op jit(solution)/shard_map/ppermute | solution.py:370
  274.4 35.4 %collective-permute-start.43 = (bf16[2,2,2,128,512]{4,3,2,1,0:T(8,128)(2,1)}, bf16[2,2,2,128,512]{4,3,2,1,0:T(8,128)(2,1)S(1)}, u32[]{:S(2)}, u32[]{:S(2)}) collective-permute-start(bf16[2,2,2,128,512]{4,3,2,1,0:T(8,128)(2,1)} %pad_maximum_fusion.17), channel_id=1, source_target_pairs={{0,4},{1,5},{2,6},{3,7},{4,0},{5,1},{6,2},{7,3},{8,12},{9,13},{10,... | collective-permute-start | bytes 3145736 | tf_op jit(solution)/shard_map/ppermute | solution.py:370
  379.4 34.6 %collective-permute-start.58 = (bf16[8,48,2048]{2,1,0:T(8,128)(2,1)}, bf16[8,48,2048]{2,1,0:T(8,128)(2,1)}, u32[]{:S(2)}, u32[]{:S(2)}) collective-permute-start(bf16[8,48,2048]{2,1,0:T(8,128)(2,1)} %pad_maximum_fusion.12), channel_id=1, source_target_pairs={{0,8},{1,9},{2,10},{3,11},{4,12},{5,13},{6,14},{7,15},{8,0},{9,1},... | collective-permute-start | bytes 4718600 | tf_op jit(solution)/shard_map/ppermute | solution.py:370
  380.8 33.8 %collective-permute-start.59 = (bf16[8,48,2048]{2,1,0:T(8,128)(2,1)}, bf16[8,48,2048]{2,1,0:T(8,128)(2,1)}, u32[]{:S(2)}, u32[]{:S(2)}) collective-permute-start(bf16[8,48,2048]{2,1,0:T(8,128)(2,1)} %pad_maximum_fusion.13), channel_id=1, source_target_pairs={{0,4},{1,5},{2,6},{3,7},{4,0},{5,1},{6,2},{7,3},{8,12},{9,13},{10,... | collective-permute-start | bytes 4718600 | tf_op jit(solution)/shard_map/ppermute | solution.py:370
  381.1 31.6 %collective-permute-start.60 = (bf16[8,32,2048]{2,1,0:T(8,128)(2,1)}, bf16[8,32,2048]{2,1,0:T(8,128)(2,1)}, u32[]{:S(2)}, u32[]{:S(2)}) collective-permute-start(bf16[8,32,2048]{2,1,0:T(8,128)(2,1)} %pad_maximum_fusion.21), channel_id=1, source_target_pairs={{0,2},{1,3},{2,0},{3,1},{4,6},{5,7},{6,4},{7,5},{8,10},{9,11},{10,... | collective-permute-start | bytes 3145736 | tf_op jit(solution)/shard_map/ppermute | solution.py:370
  414.6 34.0 %collective-permute-start.62 = (bf16[8,48,2048]{2,1,0:T(8,128)(2,1)S(1)}, bf16[8,48,2048]{2,1,0:T(8,128)(2,1)}, u32[]{:S(2)}, u32[]{:S(2)}) collective-permute-start(bf16[8,48,2048]{2,1,0:T(8,128)(2,1)S(1)} %copy-done.99), channel_id=1, source_target_pairs={{0,8},{1,9},{2,10},{3,11},{4,12},{5,13},{6,14},{7,15},{8,0},{9,1},... | collective-permute-start | bytes 4718600 | tf_op jit(solution)/shard_map/ppermute | solution.py:370
  415.8 33.5 %collective-permute-start.63 = (bf16[8,48,2048]{2,1,0:T(8,128)(2,1)S(1)}, bf16[8,48,2048]{2,1,0:T(8,128)(2,1)}, u32[]{:S(2)}, u32[]{:S(2)}) collective-permute-start(bf16[8,48,2048]{2,1,0:T(8,128)(2,1)S(1)} %copy-done.98), channel_id=1, source_target_pairs={{0,4},{1,5},{2,6},{3,7},{4,0},{5,1},{6,2},{7,3},{8,12},{9,13},{10,... | collective-permute-start | bytes 4718600 | tf_op jit(solution)/shard_map/ppermute | solution.py:370
  415.8 31.5 %collective-permute-start.64 = (bf16[8,32,2048]{2,1,0:T(8,128)(2,1)}, bf16[8,32,2048]{2,1,0:T(8,128)(2,1)}, u32[]{:S(2)}, u32[]{:S(2)}) collective-permute-start(bf16[8,32,2048]{2,1,0:T(8,128)(2,1)} %pad_maximum_fusion.20), channel_id=1, source_target_pairs={{0,2},{1,3},{2,0},{3,1},{4,6},{5,7},{6,4},{7,5},{8,10},{9,11},{10,... | collective-permute-start | bytes 3145736 | tf_op jit(solution)/shard_map/ppermute | solution.py:370
  449.3 38.1 %collective-permute-start.65 = (bf16[8,48,2048]{2,1,0:T(8,128)(2,1)}, bf16[8,48,2048]{2,1,0:T(8,128)(2,1)S(1)}, u32[]{:S(2)}, u32[]{:S(2)}) collective-permute-start(bf16[8,48,2048]{2,1,0:T(8,128)(2,1)} %bitcast.552), channel_id=1, source_target_pairs={{0,8},{1,9},{2,10},{3,11},{4,12},{5,13},{6,14},{7,15},{8,0},{9,1},... | collective-permute-start | bytes 4718600 | tf_op jit(solution)/shard_map/ppermute | solution.py:370
  450.3 37.1 %collective-permute-start.66 = (bf16[8,48,2048]{2,1,0:T(8,128)(2,1)}, bf16[8,48,2048]{2,1,0:T(8,128)(2,1)S(1)}, u32[]{:S(2)}, u32[]{:S(2)}) collective-permute-start(bf16[8,48,2048]{2,1,0:T(8,128)(2,1)} %bitcast.551), channel_id=1, source_target_pairs={{0,4},{1,5},{2,6},{3,7},{4,0},{5,1},{6,2},{7,3},{8,12},{9,13},{10,... | collective-permute-start | bytes 4718600 | tf_op jit(solution)/shard_map/ppermute | solution.py:370
  450.3 37.0 %collective-permute-start.67 = (bf16[8,32,2048]{2,1,0:T(8,128)(2,1)}, bf16[8,32,2048]{2,1,0:T(8,128)(2,1)}, u32[]{:S(2)}, u32[]{:S(2)}) collective-permute-start(bf16[8,32,2048]{2,1,0:T(8,128)(2,1)} %bitcast.554), channel_id=1, source_target_pairs={{0,2},{1,3},{2,0},{3,1},{4,6},{5,7},{6,4},{7,5},{8,10},{9,11},{10,... | collective-permute-start | bytes 3145736 | tf_op jit(solution)/shard_map/ppermute | solution.py:370
  487.4 38.0 %collective-permute-start.68 = (bf16[8,48,2048]{2,1,0:T(8,128)(2,1)}, bf16[8,48,2048]{2,1,0:T(8,128)(2,1)}, u32[]{:S(2)}, u32[]{:S(2)}) collective-permute-start(bf16[8,48,2048]{2,1,0:T(8,128)(2,1)} %bitcast.550), channel_id=1, source_target_pairs={{0,8},{1,9},{2,10},{3,11},{4,12},{5,13},{6,14},{7,15},{8,0},{9,1},... | collective-permute-start | bytes 4718600 | tf_op jit(solution)/shard_map/ppermute | solution.py:370
  488.8 36.7 %collective-permute-start.69 = (bf16[8,48,2048]{2,1,0:T(8,128)(2,1)}, bf16[8,48,2048]{2,1,0:T(8,128)(2,1)}, u32[]{:S(2)}, u32[]{:S(2)}) collective-permute-start(bf16[8,48,2048]{2,1,0:T(8,128)(2,1)} %bitcast.549), channel_id=1, source_target_pairs={{0,4},{1,5},{2,6},{3,7},{4,0},{5,1},{6,2},{7,3},{8,12},{9,13},{10,... | collective-permute-start | bytes 4718600 | tf_op jit(solution)/shard_map/ppermute | solution.py:370
  490.4 35.0 %collective-permute-start.70 = (bf16[8,32,2048]{2,1,0:T(8,128)(2,1)}, bf16[8,32,2048]{2,1,0:T(8,128)(2,1)}, u32[]{:S(2)}, u32[]{:S(2)}) collective-permute-start(bf16[8,32,2048]{2,1,0:T(8,128)(2,1)} %bitcast.553), channel_id=1, source_target_pairs={{0,2},{1,3},{2,0},{3,1},{4,6},{5,7},{6,4},{7,5},{8,10},{9,11},{10,... | collective-permute-start | bytes 3145736 | tf_op jit(solution)/shard_map/ppermute | solution.py:370
  534.5 41.8 %collective-permute-start.73 = (bf16[4,32,2048]{2,1,0:T(8,128)(2,1)}, bf16[4,32,2048]{2,1,0:T(8,128)(2,1)}, u32[]{:S(2)}, u32[]{:S(2)}) collective-permute-start(bf16[4,32,2048]{2,1,0:T(8,128)(2,1)} %slice.707), channel_id=1, source_target_pairs={{0,4},{1,5},{2,6},{3,7},{4,0},{5,1},{6,2},{7,3},{8,12},{9,13},{10,... | collective-permute-start | bytes 1572872 | tf_op jit(solution)/shard_map/ppermute | solution.py:370
  534.7 43.7 %collective-permute-start.72 = (bf16[4,48,2048]{2,1,0:T(8,128)(2,1)S(1)}, bf16[4,48,2048]{2,1,0:T(8,128)(2,1)}, u32[]{:S(2)}, u32[]{:S(2)}) collective-permute-start(bf16[4,48,2048]{2,1,0:T(8,128)(2,1)S(1)} %slice.706), channel_id=1, source_target_pairs={{0,8},{1,9},{2,10},{3,11},{4,12},{5,13},{6,14},{7,15},{8,0},{9,1},... | collective-permute-start | bytes 2359304 | tf_op jit(solution)/shard_map/ppermute | solution.py:370
  535.5 45.1 %collective-permute-start.71 = (bf16[4,48,2048]{2,1,0:T(8,128)(2,1)}, bf16[4,48,2048]{2,1,0:T(8,128)(2,1)}, u32[]{:S(2)}, u32[]{:S(2)}) collective-permute-start(bf16[4,48,2048]{2,1,0:T(8,128)(2,1)} %slice.705), channel_id=1, source_target_pairs={{0,2},{1,3},{2,0},{3,1},{4,6},{5,7},{6,4},{7,5},{8,10},{9,11},{10,... | collective-permute-start | bytes 2359304 | tf_op jit(solution)/shard_map/ppermute | solution.py:370
  582.1 28.2 %collective-permute-start.76 = (bf16[2,32,2048]{2,1,0:T(8,128)(2,1)}, bf16[2,32,2048]{2,1,0:T(8,128)(2,1)S(1)}, u32[]{:S(2)}, u32[]{:S(2)}) collective-permute-start(bf16[2,32,2048]{2,1,0:T(8,128)(2,1)} %slice.713), channel_id=1, source_target_pairs={{0,8},{1,9},{2,10},{3,11},{4,12},{5,13},{6,14},{7,15},{8,0},{9,1},... | collective-permute-start | bytes 786440 | tf_op jit(solution)/shard_map/ppermute | solution.py:370
  583.5 27.0 %collective-permute-start.75 = (bf16[2,48,2048]{2,1,0:T(8,128)(2,1)}, bf16[2,48,2048]{2,1,0:T(8,128)(2,1)}, u32[]{:S(2)}, u32[]{:S(2)}) collective-permute-start(bf16[2,48,2048]{2,1,0:T(8,128)(2,1)} %slice.711), channel_id=1, source_target_pairs={{0,2},{1,3},{2,0},{3,1},{4,6},{5,7},{6,4},{7,5},{8,10},{9,11},{10,... | collective-permute-start | bytes 1179656 | tf_op jit(solution)/shard_map/ppermute | solution.py:370
  583.5 28.1 %collective-permute-start.74 = (bf16[2,48,2048]{2,1,0:T(8,128)(2,1)S(1)}, bf16[2,48,2048]{2,1,0:T(8,128)(2,1)S(1)}, u32[]{:S(2)}, u32[]{:S(2)}) collective-permute-start(bf16[2,48,2048]{2,1,0:T(8,128)(2,1)S(1)} %slice.709), channel_id=1, source_target_pairs={{0,4},{1,5},{2,6},{3,7},{4,0},{5,1},{6,2},{7,3},{8,12},{9,13},{10,... | collective-permute-start | bytes 1179656 | tf_op jit(solution)/shard_map/ppermute | solution.py:370
  628.3 325.8 %reduce-scatter.6.cloned.1.call-start = ((), (), s32[]{:S(2)}) async-start(), calls=%async_computation.7 | async-start | bytes 8650752 | tf_op jit(solution)/shard_map/reduce_scatter | solution.py:763
  628.9 329.9 %reduce-scatter.4.cloned.1.call-start = ((), (), s32[]{:S(2)}) async-start(), calls=%async_computation.6 | async-start | bytes 8650752 | tf_op jit(solution)/shard_map/reduce_scatter | solution.py:763
  637.4 119.5 %collective-permute-start.126 = (f32[88,2048]{1,0:T(8,128)}, f32[88,2048]{1,0:T(8,128)}, u32[]{:S(2)}, u32[]{:S(2)}) collective-permute-start(f32[88,2048]{1,0:T(8,128)} %slice_select_fusion.3), channel_id=1, source_target_pairs={{0,1},{1,0},{2,3},{3,2},{4,5},{5,4},{6,7},{7,6},{8,9},{9,8},{10,11... | collective-permute-start | bytes 2162696 | tf_op jit(solution)/shard_map/ppermute | solution.py:373
  641.6 139.7 %collective-permute-start.125 = (f32[16,64,352]{2,1,0:T(8,128)}, f32[16,64,352]{2,1,0:T(8,128)}, u32[]{:S(2)}, u32[]{:S(2)}) collective-permute-start(f32[16,64,352]{2,1,0:T(8,128)} %slice_select_fusion), channel_id=1, source_target_pairs={{0,1},{1,0},{2,3},{3,2},{4,5},{5,4},{6,7},{7,6},{8,9},{9,8},{10,11... | collective-permute-start | bytes 4325384 | tf_op jit(solution)/shard_map/ppermute | solution.py:373
  666.4 32.2 %collective-permute-start.86 = (f32[256,1024]{1,0:T(8,128)S(1)}, f32[256,1024]{1,0:T(8,128)S(1)}, u32[]{:S(2)}, u32[]{:S(2)}) collective-permute-start(f32[256,1024]{1,0:T(8,128)S(1)} %slice_select_fusion.2), channel_id=1, source_target_pairs={{0,1},{1,0},{2,3},{3,2},{4,5},{5,4},{6,7},{7,6},{8,9},{9,8},{10,11... | collective-permute-start | bytes 3145736 | tf_op jit(solution)/shard_map/ppermute | solution.py:373
  684.3 24.4 %collective-permute-start.82 = (bf16[1024,512]{1,0:T(8,128)(2,1)}, bf16[1024,512]{1,0:T(8,128)(2,1)}, u32[]{:S(2)}, u32[]{:S(2)}) collective-permute-start(bf16[1024,512]{1,0:T(8,128)(2,1)} %convolution_convert_fusion.4), channel_id=1, source_target_pairs={{0,4},{1,5},{2,6},{3,7},{4,0},{5,1},{6,2},{7,3},{8,12},{9,13},{10,... | collective-permute-start | bytes 3145736 | tf_op jit(solution)/shard_map/ppermute | solution.py:370
  695.6 23.9 %collective-permute-start.81 = (bf16[1024,512]{1,0:T(8,128)(2,1)}, bf16[1024,512]{1,0:T(8,128)(2,1)}, u32[]{:S(2)}, u32[]{:S(2)}) collective-permute-start(bf16[1024,512]{1,0:T(8,128)(2,1)} %convolution_convert_fusion.5), channel_id=1, source_target_pairs={{0,8},{1,9},{2,10},{3,11},{4,12},{5,13},{6,14},{7,15},{8,0},{9,1},... | collective-permute-start | bytes 3145736 | tf_op jit(solution)/shard_map/ppermute | solution.py:370
  725.0 25.9 %collective-permute-start.92 = (f32[256,576]{0,1:T(8,128)S(1)}, f32[256,576]{0,1:T(8,128)S(1)}, u32[]{:S(2)}, u32[]{:S(2)}) collective-permute-start(f32[256,576]{0,1:T(8,128)S(1)} %pad_maximum_fusion.31), channel_id=1, source_target_pairs={{0,1},{1,0},{2,3},{3,2},{4,5},{5,4},{6,7},{7,6},{8,9},{9,8},{10,11... | collective-permute-start | bytes 1769480 | tf_op jit(solution)/shard_map/ppermute | solution.py:373
  783.9 50.5 %all-to-all-start.1 = ((bf16[16,64,352]{2,1,0:T(8,128)(2,1)}), bf16[16,64,352]{2,1,0:T(8,128)(2,1)}, u32[]{:S(2)}, u32[]{:S(2)}) async-start(bf16[16,64,352]{2,1,0:T(8,128)(2,1)} %add_convert_fusion.11), calls=%async_computation.1 | async-start | bytes 1572864 | tf_op jit(solution)/shard_map/all_to_all | solution.py:770
  790.7 24.2 %collective-permute-start.98 = (bf16[128,512]{1,0:T(8,128)(2,1)}, bf16[128,512]{1,0:T(8,128)(2,1)S(1)}, u32[]{:S(2)}, u32[]{:S(2)}) collective-permute-start(bf16[128,512]{1,0:T(8,128)(2,1)} %dynamic-slice_bitcast_fusion.11), channel_id=1, source_target_pairs={{0,16},{1,17},{2,18},{3,19},{4,20},{5,21},{6,22},{7,23},{8,24},{9,... | collective-permute-start | bytes 393224 | tf_op jit(solution)/shard_map/ppermute | solution.py:370
  824.2 22.5 %collective-permute-start.109 = (bf16[512,576]{0,1:T(8,128)(2,1)}, bf16[512,576]{0,1:T(8,128)(2,1)}, u32[]{:S(2)}, u32[]{:S(2)}) collective-permute-start(bf16[512,576]{0,1:T(8,128)(2,1)} %convolution_convert_fusion.6), channel_id=1, source_target_pairs={{0,4},{1,5},{2,6},{3,7},{4,0},{5,1},{6,2},{7,3},{8,12},{9,13},{10,... | collective-permute-start | bytes 1769480 | tf_op jit(solution)/shard_map/ppermute | solution.py:370
  825.7 43.4 %collective-permute-start.108 = (bf16[256,2048]{1,0:T(8,128)(2,1)}, bf16[256,2048]{1,0:T(8,128)(2,1)}, u32[]{:S(2)}, u32[]{:S(2)}) collective-permute-start(bf16[256,2048]{1,0:T(8,128)(2,1)} %convolution_convert_fusion.1), channel_id=1, source_target_pairs={{0,4},{1,5},{2,6},{3,7},{4,0},{5,1},{6,2},{7,3},{8,12},{9,13},{10,... | collective-permute-start | bytes 3145736 | tf_op jit(solution)/shard_map/ppermute | solution.py:370
  826.3 49.0 %collective-permute-start.107 = (bf16[1024,768]{1,0:T(8,128)(2,1)}, bf16[1024,768]{1,0:T(8,128)(2,1)}, u32[]{:S(2)}, u32[]{:S(2)}) collective-permute-start(bf16[1024,768]{1,0:T(8,128)(2,1)} %convolution_convert_fusion.2), channel_id=1, source_target_pairs={{0,8},{1,9},{2,10},{3,11},{4,12},{5,13},{6,14},{7,15},{8,0},{9,1},... | collective-permute-start | bytes 4718600 | tf_op jit(solution)/shard_map/ppermute | solution.py:370
  826.3 51.2 %collective-permute-start.106 = (bf16[1024,768]{1,0:T(8,128)(2,1)}, bf16[1024,768]{1,0:T(8,128)(2,1)}, u32[]{:S(2)}, u32[]{:S(2)}) collective-permute-start(bf16[1024,768]{1,0:T(8,128)(2,1)} %convolution_convert_fusion.3), channel_id=1, source_target_pairs={{0,2},{1,3},{2,0},{3,1},{4,6},{5,7},{6,4},{7,5},{8,10},{9,11},{10,... | collective-permute-start | bytes 4718600 | tf_op jit(solution)/shard_map/ppermute | solution.py:370
  (306 other events, 2591.7 us)
Sparse Core Ops, SparseCore 0:
  151.3 9.1 all-gather.7
  162.0 17.9 all-gather.9
  181.6 16.2 all-gather.11
  199.3 17.1 all-gather.13
  628.5 13.8 reduce-scatter.7
  645.1 15.7 reduce-scatter.5
  663.8 15.0 reduce-scatter.3

commit v3 on v2

--- a/solution.py
+++ b/solution.py
@@ -27,14 +27,14 @@
 ORDER_QUERY = ((8, 4, 1, 2), (8, 2, 4, 1))
 ORDER_EXPAND = (8, 1, 2, 4)
 ORDER_LATENT = (8, 1, 2, 4)
-ORDER_SMALL = (1, 2, 4, 8)
-ORDER_OUTPUT = ((8, 1, 4, 2), (8, 2, 1, 4))
+ORDER_OUTPUT = ((8, 2), (1, 4), (4, 1))
 TOKEN_GROUPS = (48, 48, 32)
-ORDER_TOKENS = ((8, 2, 1, 4), (8, 1, 4, 2), (8, 4, 2, 1))
+ORDER_TOKENS = ((2, 1, 4), (1, 4, 2), (4, 2, 1))
+FIRST_TOKENS = 8
 BACK_QUERY = ((1, 4, 2, 8), (4, 2, 1, 8))
 BACK_EXPAND = (2, 1, 4, 8)
 BACK_LATENT = (2, 1, 4, 8)
-BACK_OUTPUT = ((4, 1, 2, 8), (2, 4, 1, 8))
+BACK_OUTPUT = ((4, 1), (1, 4), (2, 8))
 
 
 def rms_scale(values, gain_vec):
@@ -276,40 +276,39 @@
 
 def in_weights_kernel(*refs):
     groups = 2 * len(TOKEN_GROUPS)
-    rows, grads, outs = refs[:groups], refs[groups : groups + 4], refs[groups + 4 : groups + 8]
-    turned = refs[-1]
+    rows, (first, last), (out, extra_out), turned = (
+        refs[:groups], refs[groups : groups + 2], refs[groups + 2 : groups + 4], refs[-1],
+    )
     for ref, here in row_groups(rows):
         turned[:, here] = ref[...].T
-    tokens = grads[0].shape[0]
-    ff = outs[0].shape[1]
-    for first, last, joined in ((grads[0], grads[1], outs[:2]), (grads[2], grads[3], outs[2:])):
-        for out, begin in zip(joined, (0, ff)):
-            for start, size in spans(out.shape[1]):
-                there = pl.ds(begin + start, size)
-                value = product(turned[:, pl.ds(0, tokens)], first[:, there])
-                value = value + product(turned[:, pl.ds(tokens, tokens)], last[:, there])
-                out[:, pl.ds(start, size)] = value.astype(out.dtype)
-
-
-def in_weights(rows, gate_back, up_back, ff):
-    tokens, units = gate_back[0].shape
+    tokens = first.shape[0]
+    for ref, begin in ((out, 0), (extra_out, out.shape[1])):
+        for start, size in spans(ref.shape[1]):
+            there = pl.ds(begin + start, size)
+            value = product(turned[:, pl.ds(0, tokens)], first[:, there])
+            value = value + product(turned[:, pl.ds(tokens, tokens)], last[:, there])
+            ref[:, pl.ds(start, size)] = value.astype(ref.dtype)
+
+
+def in_weights(rows, acts_back, ff):
+    tokens, units = acts_back[0].shape
     width = rows[0].shape[1]
     whole = pl.BlockSpec((tokens, units), lambda i: (0, 0), pipeline_mode=pl.Buffered(1))
-    outs = [((width, ff), BF16), ((width, units - ff), F32)] * 2
+    outs = [((width, ff), BF16), ((width, units - ff), F32)]
     return pl.pallas_call(
         in_weights_kernel,
         grid=(width // WIDE,),
         out_shape=[jax.ShapeDtypeStruct(*out) for out in outs],
-        in_specs=[pl.BlockSpec((v.shape[0], WIDE), lambda i: (0, i)) for v in rows] + [whole] * 4,
+        in_specs=[pl.BlockSpec((v.shape[0], WIDE), lambda i: (0, i)) for v in rows] + [whole] * 2,
         out_specs=[pl.BlockSpec((WIDE, shape[1]), lambda i: (i, 0)) for shape, _ in outs],
         scratch_shapes=[pltpu.VMEM((WIDE, 2 * tokens), BF16)],
         compiler_params=pltpu.CompilerParams(vmem_limit_bytes=VMEM_BYTES),
         cost_estimate=pl.CostEstimate(
-            flops=8 * tokens * width * units,
-            bytes_accessed=4 * tokens * (width + 2 * units) + 4 * width * units,
+            flops=4 * tokens * width * units,
+            bytes_accessed=4 * tokens * (width + units) + 2 * width * units,
             transcendentals=0,
         ),
-    )(*rows, *gate_back, *up_back)
+    )(*rows, *acts_back)
 
 
 def down_weights_kernel(hidden_first, hidden_last, *refs):
@@ -433,8 +432,8 @@
                 advance(i, other)
         return together(*results)
 
-    def gather_chips(self, value, order):
-        done = []
+    def gather_chips(self, value, order, state=()):
+        done = list(state)
         for mask in self.bits(order):
             other = yield value, mask
             place = sum(m > mask for m in done)
@@ -443,7 +442,9 @@
                 [jnp.where(high, other, value), jnp.where(high, value, other)], axis=place
             )
             done.append(mask)
-        return value.reshape((self.n,) + value.shape[len(done) :])
+        if len(done) == len(self.bits((8, 4, 2, 1))):
+            value = value.reshape((self.n,) + value.shape[len(done) :])
+        return value
 
     def halves(self, value, mask, width):
         high = (self.chip // mask) % 2 == 1
@@ -458,21 +459,21 @@
     def scatter_chips(self, value, order, done=()):
         left = [m for m in sorted(self.bits((8, 4, 2, 1)), reverse=True) if m not in done]
         for mask in self.bits(order):
-            if mask in done:
-                continue
             place = left.index(mask)
-            high = (self.chip // mask) % 2
+            high = (self.chip // mask) % 2 == 1
             rest = value.shape[1:]
             split = value.reshape((2,) * len(left) + rest)
-            keep = lax.dynamic_index_in_dim(split, high, place, keepdims=False)
-            send = lax.dynamic_index_in_dim(split, 1 - high, place, keepdims=False)
+            lower = lax.index_in_dim(split, 0, place, keepdims=False)
+            upper = lax.index_in_dim(split, 1, place, keepdims=False)
+            keep = jnp.where(high, upper, lower)
+            send = jnp.where(high, lower, upper)
             left.remove(mask)
-            other = yield send, mask
+            other = yield send.astype(BF16), mask
             value = keep.astype(F32) + other.astype(F32)
             if left:
-                value = value.astype(send.dtype)
+                value = value.astype(BF16)
             value = value.reshape((2 ** len(left),) + rest)
-        return value[0]
+        return value if left else value[0]
 
     def weight_grad(self, rows, grads, order):
         mask = self.bits(order)[0]
@@ -482,18 +483,19 @@
         other = yield away, mask
         value = inner_rows(keep, grads) + other.astype(F32)
         value = value.astype(BF16).reshape(self.n // 2, width, -1)
-        return (yield from self.scatter_chips(value, order, (mask,)))
-
-    def gather_groups(self, value, idle=0):
-        start = 0
-        for size, order in zip(TOKEN_GROUPS, ORDER_TOKENS):
-            yield self.gather_tokens(value[start : start + size], order, idle)
-            start += size
-
-    def gather_tokens(self, value, order, idle):
-        for _ in range(idle):
+        return (yield from self.scatter_chips(value, order[1:], (mask,)))
+
+    def gather_groups(self, value, states):
+        for i, order in enumerate(ORDER_TOKENS):
+            yield self.gather_tokens(value if i == 0 else None, i, order, states)
+
+    def gather_tokens(self, value, i, order, states):
+        if i == 0:
+            states["rows"] = jnp.stack([value, (yield value, FIRST_TOKENS)])
+        else:
             yield (), None
-        value = value[None]
+        start = sum(TOKEN_GROUPS[:i])
+        value = states["rows"][:, start : start + TOKEN_GROUPS[i]]
         for mask in self.bits(order)[:-1]:
             other = yield value, mask
             value = jnp.concatenate([value, other], axis=0)
@@ -506,19 +508,24 @@
     def last_exchange(self, value, mask):
         return (yield value, mask)
 
-    def scatter_groups(self, groups, others):
-        for value, other, order in zip(groups, others, ORDER_TOKENS):
-            yield self.scatter_tokens(value, other, order)
-
-    def scatter_tokens(self, value, other, order):
-        order = self.bits(order)
+    def scatter_groups(self, groups, others, states):
+        for i, (value, other, order) in enumerate(zip(groups, others, ORDER_TOKENS)):
+            yield self.scatter_tokens(value, other, i, order, states)
+
+    def scatter_tokens(self, value, other, i, order, states):
         value = value.astype(F32) + other.astype(F32)
-        for masks in reversed(order[:-1]):
+        for mask in reversed(self.bits(order)[:-1]):
             half = value.shape[0] // 2
-            value = value.astype(other.dtype)
-            received = yield value[half:], masks
+            value = value.astype(BF16)
+            received = yield value[half:], mask
             value = value[:half].astype(F32) + received.astype(F32)
-        return value[0]
+        states[i] = value
+        if i + 1 < len(TOKEN_GROUPS):
+            yield (), None
+            return ()
+        value = jnp.concatenate([states[k] for k in range(len(TOKEN_GROUPS))], axis=1)
+        received = yield value[1].astype(BF16), FIRST_TOKENS
+        return value[0] + received.astype(F32)
 
 
 def body(
@@ -549,65 +556,114 @@
     expert_count = n * expert_gate.shape[0]
     small_cut = (shard, 2 * shard, 2 * shard + norm_latent.shape[0])
 
-    small = jnp.concatenate([norm_attn, norm_ffn, norm_latent, router.reshape(-1)])[None]
+    tokens_seq = chips.gather_cores(tokens)
+    small = jnp.concatenate([norm_attn, norm_ffn, norm_latent, router.reshape(-1)])
     query_own = chips.swap_cores(query_proj, 1, 0)
     query_cut = query_own.shape[1] // 2
     expand_own = chips.swap_cores(expand_proj, 1, 0)
+    output_own = chips.swap_cores(output_proj, 1, 0)
+    output_cut = output_own.shape[1] // 2
     width = shared_gate.shape[1] // n
-
-    def shared_weights():
-        weights = (shared_gate, shared_up)
-        for _ in range(4):
-            weights = yield weights, None
-        shared_gate_in, shared_up_in = weights
-        shared_in = jnp.stack(
-            [shared_gate_in.reshape(shard, n, -1), shared_up_in.reshape(shard, n, -1)], 2
-        )
-        shared_in = lax.all_to_all(
-            shared_in.transpose(1, 0, 2, 3).reshape(n * shard, 2 * width),
-            "expert",
-            split_axis=0,
-            concat_axis=0,
-            tiled=True,
-        ).reshape(n, 1, shard, 2 * width)
-        return shared_in
-
-    small, query_first, query_last, expand_weight, latent_own, routes_all, shared_in = chips.lockstep(
-        chips.gather_chips(chips.gather_cores(small), ORDER_SMALL),
+    tiny = jnp.concatenate([chips.gather_cores(small[None]).reshape(-1), routes.astype(BF16).reshape(-1)])
+    tiny_size = tiny.shape[0]
+    columns = latent_proj.shape[1]
+    tiny_rows = -(-tiny_size // columns)
+    tiny = jnp.pad(tiny, (0, tiny_rows * columns - tiny_size)).reshape(tiny_rows, columns)
+    latent_own = jnp.concatenate([latent_proj, tiny], axis=0)
+    tokens_seq, query_own, expand_own, output_own, latent_own = together(
+        tokens_seq, query_own, expand_own, output_own, latent_own
+    )
+
+    def shared_columns(*weights):
+        weights = yield weights, None
+        shared_in = jnp.stack([w.reshape(shard, n, -1) for w in weights], 2)
+        shared_in = shared_in.transpose(1, 0, 2, 3).reshape(n * shard, 2 * width)
+        for _ in range(3):
+            shared_in = yield shared_in, None
+        return lax.all_to_all(shared_in, "expert", split_axis=0, concat_axis=0, tiled=True)
+
+    query_first, query_last, expand_weight, latent_own, shared_in = chips.lockstep(
         chips.gather_chips(query_own[:, :query_cut], ORDER_QUERY[0]),
         chips.gather_chips(query_own[:, query_cut:], ORDER_QUERY[1]),
         chips.gather_chips(expand_own, ORDER_EXPAND),
-        chips.gather_chips(latent_proj, ORDER_LATENT),
-        chips.gather_chips(routes, ORDER_SMALL),
-        shared_weights(),
-    )
-    shared_in = lax.all_gather(shared_in, "fsdp", axis=1, tiled=True).reshape(D, 2 * width)
-    output_own = chips.swap_cores(output_proj, 1, 0)
-    output_cut = output_own.shape[1] // 2
-    small, query_first, query_last, expand_weight, latent_own, output_own, cot_in, routes_all = together(
-        small, query_first, query_last, expand_weight, latent_own, output_own, cotangent, routes_all
-    )
-    small = small.reshape(n * cores, -1)
+        chips.gather_chips(latent_own, ORDER_LATENT),
+        shared_columns(shared_gate, shared_up),
+    )
+    (
+        query_first, query_last, expand_weight, latent_own, shared_in, tokens_seq, output_own,
+        cot_in,
+    ) = together(
+        query_first, query_last, expand_weight, latent_own, shared_in, tokens_seq, output_own,
+        cotangent,
+    )
+    tiny = latent_own[:, shard:].reshape(n, -1)
+    latent_own = latent_own[:, :shard]
+    routes_all = tiny[:, cores * small.shape[0] : tiny_size].astype(jnp.int32)
+    routes_all = routes_all.reshape(n, SEQ_DEV, TOPK)
+    small = tiny[:, : cores * small.shape[0]].reshape(n * cores, -1)
     gain_attn = small[:, : small_cut[0]].reshape(-1).astype(F32)
     gain_ffn = small[:, small_cut[0] : small_cut[1]].reshape(-1).astype(F32)
     gain_latent = small[:, small_cut[1] : small_cut[2]].reshape(-1).astype(F32)
-    router_all = small[:, small_cut[2] :].reshape(D, -1)
-    extra = -(-(width + expert_count) // LANES) * LANES
-    router_at = extra - LANES
-    gate_extra = jnp.concatenate([shared_in[:, :width], router_all], axis=1)
-    gate_extra = jnp.pad(gate_extra, ((0, 0), (0, extra - width - expert_count)))
-    up_extra = jnp.pad(shared_in[:, width:], ((0, 0), (0, extra - width)))
-    member_pad = (width - router_at, extra - width - expert_count)
     query_parts = [query_first.reshape(D, -1), query_last.reshape(D, -1)]
     expand_weight = expand_weight.reshape(KVR, -1)
-    latent_weight = chips.gather_cores(latent_own[:, None], axis=1).reshape(D, -1)
-    down_extra = jnp.pad(chips.gather_cores(shared_down), ((0, extra - width), (0, 0)))
+    latent_own_rows = latent_own.reshape(n * shard, -1)
     gate_full, up_full, down_full = (
         lax.all_gather(w[0], "fsdp", axis=0, tiled=True)
         for w in (expert_gate, expert_up, expert_down)
     )
-    weights = (gate_full, gate_extra, up_full, up_extra, down_full, down_extra)
     ff = gate_full.shape[1]
+
+    def idle(rounds):
+        for _ in range(rounds):
+            yield (), None
+
+    def shared_weights(value):
+        value = yield value, None
+        return lax.all_gather(
+            value.reshape(n, 1, shard, 2 * width), "fsdp", axis=1, tiled=True
+        ).reshape(D, 2 * width)
+
+    outputs = {}
+
+    def output_weights(part):
+        if part == 0:
+            value = yield from chips.gather_chips(output_own, ORDER_OUTPUT[0])
+            outputs["first"] = value
+        else:
+            yield from idle(len(chips.bits(ORDER_OUTPUT[0])))
+        value = outputs["first"][..., part * output_cut : (part + 1) * output_cut]
+        order = chips.bits(ORDER_OUTPUT[1 + part])
+        state = chips.bits(ORDER_OUTPUT[0])
+        value = yield from chips.gather_chips(value, order[:-1], state)
+        other = yield value, order[-1]
+        return value, other
+
+    half = n // 2
+
+    extra = -(-(width + expert_count) // LANES) * LANES
+    member_pad = (width + LANES - extra, extra - width - expert_count)
+
+    def expert_members(routes_all):
+        turns = []
+        for last in (False, True):
+            for order in ORDER_TOKENS:
+                order = chips.bits((FIRST_TOKENS, *order))
+                these = [0]
+                for mask in order[:-1]:
+                    these = these + [t ^ mask for t in these]
+                turns += [t ^ order[-1] if last else t for t in these]
+        blocks = routes_all.at[chip ^ jnp.array(turns, jnp.int32)].get(mode="promise_in_bounds")
+        blocks = blocks.reshape(2, len(TOKEN_GROUPS), half, SEQ_DEV, TOPK)
+        members = []
+        for last in range(2):
+            parts, start = [], 0
+            for i, size in enumerate(TOKEN_GROUPS):
+                parts.append(blocks[last, i, :, start : start + size].reshape(half * size, TOPK))
+                start += size
+            named = jnp.concatenate(parts, axis=0)[:, :, None]
+            member = jnp.any(named == jnp.arange(expert_count, dtype=jnp.int32), axis=1)
+            members.append(jnp.pad(member.astype(F32), ((0, 0), member_pad)))
+        return members
 
     positions = jnp.arange(seq, dtype=jnp.int32)
     cos_table, sin_table = rope_tables(positions)
@@ -615,18 +671,20 @@
     score_scale = (DN + DR) ** (-0.5)
 
     def attention():
-        yield (), None
-        normed_own = rms_scale(inputs_f, gain_attn).astype(BF16)
-        normed = chips.gather_cores(normed_own)
-        latent = product(normed, latent_weight)
+        rows = yield tokens_seq, None
+        normed = rms_scale(rows.astype(F32), gain_attn).astype(BF16)
+        normed_part = lax.dynamic_index_in_dim(
+            normed.reshape(seq, n, cores, shard), core, 2, keepdims=False
+        ).reshape(seq, n * shard)
+        latent = chips.sum_cores(product(normed_part, latent_own_rows))
         query_all = jnp.concatenate([product(normed, part) for part in query_parts], axis=1)
         query_all = query_all.reshape(seq, heads, DN + DR)
         query_nope = query_all[..., :DN].astype(BF16)
         query_rope = rotate(
             query_all[..., DN:], cos_table[:, None, :], sin_table[:, None, :]
         ).astype(BF16)
-        normed, latent, query_nope, query_rope = yield (
-            (normed, latent, query_nope, query_rope),
+        normed, normed_part, latent, query_nope, query_rope = yield (
+            (normed, normed_part, latent, query_nope, query_rope),
             None,
         )
         latent_norm = rms_scale(latent[:, :KVR], gain_latent).astype(BF16)
@@ -653,49 +711,52 @@
         attended = attended.reshape(seq, heads * DV).astype(BF16)
         attended = yield chips.gather_cores(attended, axis=1), None
         return (
-            normed, latent, query_nope, query_rope, latent_norm, key_rope, key_nope, values_all,
+            normed, normed_part, latent, query_nope, query_rope, latent_norm, key_rope, key_nope, values_all,
             probs, probs_low, attended,
         )
 
-    output_first, output_last, *cot_first, kept_attention = chips.lockstep(
-        chips.gather_chips(output_own[:, :output_cut], ORDER_OUTPUT[0]),
-        chips.gather_chips(output_own[:, output_cut:], ORDER_OUTPUT[1]),
-        *chips.gather_groups(cot_in, idle=1),
+    def joined_output(parts):
+        full = []
+        for (own_part, other_part), order in zip(parts, ORDER_OUTPUT[1:]):
+            mask = chips.bits(order)[-1]
+            high = (chip // mask) % 2 == 1
+            lower = jnp.where(high, other_part, own_part)
+            upper = jnp.where(high, own_part, other_part)
+            place = sum(m > mask for m in chips.bits((8, 4, 2, 1)))
+            full.append(jnp.stack([lower, upper], axis=place).reshape(D, -1))
+        return full
+
+    def late_members(routes_all):
+        yield from idle(3)
+        routes_all = yield routes_all, None
+        return expert_members(routes_all)
+
+    states = {}
+    *output_parts, kept_attention, shared_in, members, cot_zero, cot_one, cot_two = chips.lockstep(
+        output_weights(0),
+        output_weights(1),
         attention(),
-    )
+        shared_weights(shared_in),
+        late_members(routes_all),
+        *chips.gather_groups(cot_in, states),
+    )
+    cot_first = [cot_zero, cot_one, cot_two]
     (
-        normed, latent, query_nope, query_rope, latent_norm, key_rope, key_nope, values_all,
+        normed, normed_part, latent, query_nope, query_rope, latent_norm, key_rope, key_nope, values_all,
         probs, probs_low, attended,
     ) = kept_attention
-    output_parts = [output_first.reshape(D, -1), output_last.reshape(D, -1)]
-    hidden = jnp.concatenate([product(attended, part) for part in output_parts], axis=1)
-    hidden = inputs_f + chips.swap_cores(hidden, 0, 1)
+    hidden = []
+    for (own_part, other_part), order in zip(output_parts, ORDER_OUTPUT[1:]):
+        keep, send = chips.halves(attended, chips.bits(order)[-1], D // n)
+        part = product(keep, own_part.reshape(D // 2, -1))
+        hidden.append(part + product(send, other_part.reshape(D // 2, -1)))
+    hidden = inputs_f + chips.swap_cores(jnp.concatenate(hidden, axis=1), 0, 1)
     normed_ffn = rms_scale(hidden, gain_ffn).astype(BF16)
 
-    half = n // 2
-
-    def here_and_there(blocks):
-        halves = []
-        for last in (False, True):
-            parts, start = [], 0
-            for size, order in zip(TOKEN_GROUPS, ORDER_TOKENS):
-                order = chips.bits(order)
-                turns = [0]
-                for mask in order[:-1]:
-                    turns = turns + [t ^ mask for t in turns]
-                turns = jnp.array([t ^ order[-1] if last else t for t in turns], jnp.int32)
-                rows = jnp.take(blocks, chip ^ turns, axis=0)[:, start : start + size]
-                parts.append(rows.reshape((half * size,) + rows.shape[2:]))
-                start += size
-            halves.append(jnp.concatenate(parts, axis=0))
-        return halves
-
-    members = []
-    for routes_half in here_and_there(routes_all):
-        member = jnp.any(
-            routes_half[:, :, None] == jnp.arange(expert_count, dtype=jnp.int32), axis=1
-        )
-        members.append(jnp.pad(member.astype(F32), ((0, 0), member_pad)))
+    def beside(function, *values):
+        values = yield values, None
+        return function(*values)
+
     own = (jnp.arange(expert_count, dtype=jnp.int32) == chip).astype(F32)
     own = jnp.pad(own, member_pad)[None]
 
@@ -718,11 +779,18 @@
         )
         return blocks(back), (cot, gate_back, up_back)
 
-    def beside(function, *values):
-        values = yield values, None
-        return function(*values)
-
-    rows_first = chips.lockstep(*chips.gather_groups(normed_ffn))
+    def extra_weights(shared_in, router_all, shared_down_own):
+        gate_extra = jnp.concatenate([shared_in[:, :width], router_all], axis=1)
+        gate_extra = jnp.pad(gate_extra, ((0, 0), (0, extra - width - expert_count)))
+        up_extra = jnp.pad(shared_in[:, width:], ((0, 0), (0, extra - width)))
+        down_extra = jnp.pad(chips.gather_cores(shared_down_own), ((0, extra - width), (0, 0)))
+        return gate_full, gate_extra, up_full, up_extra, down_full, down_extra
+
+    *rows_first, output_full, weights = chips.lockstep(
+        *chips.gather_groups(normed_ffn, {}),
+        beside(lambda *parts: joined_output(parts), *output_parts),
+        beside(extra_weights, shared_in, small[:, small_cut[2] :].reshape(D, -1), shared_down),
+    )
     *rows_last, (out_first, kept_first) = chips.lockstep(
         *chips.last_groups(rows_first), beside(forward, rows_first, members[0])
     )
@@ -737,56 +805,75 @@
         *chips.last_groups(back_last), beside(backward, kept_first, cot_first, members[0])
     )
 
-    def expert_grads(kept, grads):
-        kept, grads = yield (kept, grads), None
-        gate_w, gate_extra_w, up_w, up_extra_w = in_weights(
-            [v for half_rows in kept for v in half_rows[0]],
-            [half_grads[1] for half_grads in grads],
-            [half_grads[2] for half_grads in grads],
-            ff,
-        )
-        gate_w, gate_extra_w, up_w, up_extra_w, kept, grads = yield (
-            (gate_w, gate_extra_w, up_w, up_extra_w, kept, grads),
-            None,
-        )
-        down_w, down_extra_w = down_weights(
-            [half_rows[4] for half_rows in kept], [v for half_grads in grads for v in half_grads[0]], ff
-        )
-        return gate_w, up_w, down_w, gate_extra_w, up_extra_w, down_extra_w
-
-    *ffn_grad, expert_w = chips.lockstep(
-        *chips.scatter_groups(back_first, sent_back),
-        expert_grads((kept_first, kept_last), (grads_first, grads_last)),
-    )
-    ffn_grad = jnp.concatenate(ffn_grad, axis=0)
-    gate_grad_w, up_grad_w, down_grad_w = (
-        lax.psum_scatter(v, "fsdp", scatter_dimension=0, tiled=True).astype(F32)[None]
-        for v in expert_w[:3]
-    )
-    gate_extra_w, up_extra_w, down_extra_w = expert_w[3:]
-    router_grad = gate_extra_w[:, width : width + expert_count]
-    shared_in_grad = jnp.concatenate([gate_extra_w[:, :width], up_extra_w[:, :width]], axis=1)
-    shared_in_grad = chips.scatter_cores(shared_in_grad.reshape(n, cores * shard, 2 * width), 1)
-    shared_in_grad = lax.all_to_all(
-        shared_in_grad.astype(BF16), "expert", split_axis=0, concat_axis=0, tiled=True
-    )
-    shared_in_grad = shared_in_grad.astype(F32).reshape(n, shard, 2, width).transpose(2, 1, 0, 3)
-    shared_in_grad = shared_in_grad.reshape(2, shard, n * width)
-    shared_down_grad = chips.scatter_cores(down_extra_w[:width])
-
-    _, norm_pull = jax.vjp(rms_scale, hidden, gain_ffn)
-    hidden_part, gain_ffn_grad = norm_pull(ffn_grad)
-    hidden_grad = cotangent.astype(F32) + hidden_part
-    hidden_grad, out_first, sent_out = together(hidden_grad, out_first, sent_out)
-    attn_grad_own = hidden_grad.astype(BF16)
-    attn_grad = chips.swap_cores(attn_grad_own, 1, 0)
+    def down_grads(hidden_acts, cots):
+        yield from idle(2)
+        hidden_acts, cots = yield (hidden_acts, cots), None
+        return down_weights(hidden_acts, [v for groups in cots for v in groups], ff)
+
+    *_, ffn_grad, (down_w, down_extra_w) = chips.lockstep(
+        *chips.scatter_groups(back_first, sent_back, {}),
+        down_grads((kept_first[4], kept_last[4]), (grads_first[0], grads_last[0])),
+    )
+
+    middle = {}
+
+    def through_norm(ffn_grad):
+        ffn_grad = yield ffn_grad, None
+        _, norm_pull = jax.vjp(rms_scale, hidden, gain_ffn)
+        hidden_part, gain_ffn_grad = norm_pull(ffn_grad)
+        hidden_grad = cotangent.astype(F32) + hidden_part
+        middle["attn_grad"] = chips.swap_cores(hidden_grad.astype(BF16), 1, 0)
+        middle["hidden_grad"], middle["gain"] = yield (hidden_grad, gain_ffn_grad), None
+        return middle["hidden_grad"], middle["gain"]
+
+    def output_grads(part):
+        yield from idle(1)
+        grads = middle["attn_grad"][:, part * output_cut : (part + 1) * output_cut]
+        order = chips.bits(BACK_OUTPUT[part])
+        value = yield from chips.weight_grad(attended, grads, order)
+        middle["output", part] = value
+        if part == 0:
+            yield from idle(2)
+            return ()
+        value = jnp.concatenate([middle["output", 0], value], axis=-1)
+        return (yield from chips.scatter_chips(value, BACK_OUTPUT[2], order))
+
+    def in_grads(rows, gate_back, up_back):
+        rows = [v for groups in rows for v in groups]
+        yield from idle(1)
+        rows, gate_back = yield (rows, gate_back), None
+        gate_w, gate_x = yield in_weights(rows, gate_back, ff), None
+        middle["router_grad"] = gate_x[:, width : width + expert_count]
+        gate_w = lax.psum_scatter(gate_w, "fsdp", scatter_dimension=0, tiled=True)
+        gate_w, rows, up_back = yield (gate_w, rows, up_back), None
+        up_w, up_x = in_weights(rows, up_back, ff)
+        gate_w = gate_w.astype(F32)[None]
+        gate_w, up_w, gate_x, up_x = yield (gate_w, up_w, gate_x, up_x), None
+        up_w = lax.psum_scatter(up_w, "fsdp", scatter_dimension=0, tiled=True)
+        shared = jnp.concatenate([gate_x[:, :width], up_x[:, :width]], axis=1)
+        shared = chips.scatter_cores(shared.reshape(n, cores * shard, 2 * width), 1).astype(BF16)
+        shared = yield shared, None
+        shared = lax.all_to_all(shared, "expert", split_axis=0, concat_axis=0, tiled=True)
+        shared, up_w = yield (shared, up_w), None
+        shared = shared.astype(F32).reshape(n, shard, 2, width).transpose(2, 1, 0, 3)
+        return (gate_w, up_w.astype(F32)[None]), shared.reshape(2, shard, n * width)
+
+    def second_grads(down_w, down_extra_w):
+        down_w, down_extra_w = yield (down_w, down_extra_w), None
+        down_w = lax.psum_scatter(down_w, "fsdp", scatter_dimension=0, tiled=True)
+        down_extra_w = chips.scatter_cores(down_extra_w[:width])
+        down_w, down_extra_w = yield (down_w, down_extra_w), None
+        yield from idle(1)
+        down_w = yield down_w, None
+        return down_w.astype(F32)[None], down_extra_w
 
     def attention_back():
         yield (), None
-        attended_grad = outer_cols(attn_grad[:, :output_cut], output_parts[0]) + outer_cols(
-            attn_grad[:, output_cut:], output_parts[1]
-        )
-        attended_grad = chips.scatter_cores(attended_grad, 1).astype(BF16)
+        attn_grad = middle["attn_grad"]
+        attended_grad = outer_cols(attn_grad[:, :output_cut], output_full[0]) + outer_cols(
+            attn_grad[:, output_cut:], output_full[1]
+        )
+        attended_grad = yield chips.scatter_cores(attended_grad, 1).astype(BF16), None
         attended_grad = attended_grad.reshape(seq, heads, DV)
         prob_grad = jnp.einsum("thd,shd->hts", attended_grad, values_all, preferred_element_type=F32)
         weighted = jnp.sum(probs * prob_grad, axis=-1, keepdims=True)
@@ -825,58 +912,76 @@
             axis=2,
         )
         query_back = query_back.reshape(seq, heads * (DN + DR)).astype(BF16)
-        query_back, expanded_grad, latent_grad, gain_latent_grad = yield (
-            (query_back, expanded_grad, latent_grad, gain_latent_grad),
+        middle["query_back"] = query_back
+        middle["expanded_grad"] = expanded_grad
+        middle["latent_grad"] = latent_grad
+        middle["gain_latent_grad"] = gain_latent_grad
+        yield (query_back, expanded_grad, latent_grad), None
+
+    def projection_grads(rows, name, columns, order):
+        yield from idle(3)
+        return (yield from chips.weight_grad(rows, middle[name][:, columns], order))
+
+    def input_grads():
+        yield from idle(5)
+        query_back, latent_grad, latent_rows = yield (
+            (middle["query_back"], middle["latent_grad"], latent_own),
             None,
         )
-        return query_back, expanded_grad, latent_grad, gain_latent_grad
-
-    output_first_grad, output_last_grad, *block_sum, kept_back = chips.lockstep(
-        chips.weight_grad(attended, attn_grad[:, :output_cut], BACK_OUTPUT[0]),
-        chips.weight_grad(attended, attn_grad[:, output_cut:], BACK_OUTPUT[1]),
-        *chips.scatter_groups(out_first, sent_out),
+        normed_grad = outer_cols(query_back[:, :query_cut], query_parts[0]) + outer_cols(
+            query_back[:, query_cut:], query_parts[1]
+        )
+        latent_weight = chips.gather_cores(latent_rows[:, None], axis=1).reshape(D, -1)
+        latent_grad_own = lax.dynamic_slice_in_dim(latent_grad, core * SEQ_DEV, SEQ_DEV, 0)
+        normed_grad = chips.scatter_cores(normed_grad) + outer_cols(latent_grad_own, latent_weight)
+        _, first_pull = jax.vjp(rms_scale, inputs_f, gain_attn)
+        input_part, gain_attn_grad = first_pull(normed_grad)
+        tokens_grad = (middle["hidden_grad"] + input_part).astype(BF16)
+        tokens_grad, gain_attn_grad = yield (tokens_grad, gain_attn_grad), None
+        small_grad = jnp.concatenate(
+            [
+                gain_attn_grad.reshape(n * cores, -1),
+                middle["gain"].reshape(n * cores, -1),
+                middle["gain_latent_grad"].reshape(n * cores, -1),
+                middle["router_grad"].reshape(n * cores, -1),
+            ],
+            axis=1,
+        )
+        small_grad = lax.all_to_all(
+            small_grad.reshape(n, -1), "expert", split_axis=0, concat_axis=0, tiled=True
+        )
+        small_grad = jnp.sum(small_grad, axis=0).reshape(cores, -1)
+        return tokens_grad, chips.scatter_cores(small_grad).reshape(-1)
+
+    (
+        _, _, _, block_sum, _, _, output_grad, query_first_grad, query_last_grad, expand_grad,
+        latent_weight_grad, in_grad, second_grad, input_grad,
+    ) = chips.lockstep(
+        through_norm(ffn_grad),
+        *chips.scatter_groups(out_first, sent_out, {}),
         attention_back(),
-    )
-    query_back, expanded_grad, latent_grad, gain_latent_grad = kept_back
-    output_grad = jnp.concatenate([output_first_grad, output_last_grad], axis=1)
+        output_grads(0),
+        output_grads(1),
+        projection_grads(normed, "query_back", slice(0, query_cut), BACK_QUERY[0]),
+        projection_grads(normed, "query_back", slice(query_cut, None), BACK_QUERY[1]),
+        projection_grads(latent_norm, "expanded_grad", slice(None), BACK_EXPAND),
+        projection_grads(normed_part, "latent_grad", slice(None), BACK_LATENT),
+        in_grads(
+            (kept_first[0], kept_last[0]),
+            (grads_first[1], grads_last[1]),
+            (grads_first[2], grads_last[2]),
+        ),
+        second_grads(down_w, down_extra_w),
+        input_grads(),
+    )
+    (gate_grad_w, up_grad_w), shared_in_grad = in_grad
+    down_grad_w, shared_down_grad = second_grad
+    tokens_grad, small_grad = input_grad
+    block_out = (hidden + block_sum).astype(BF16)
     output_grad = chips.swap_cores(output_grad, 0, 1)
-
-    normed_part = lax.dynamic_index_in_dim(
-        normed.reshape(seq, n, cores, shard), core, 2, keepdims=False
-    ).reshape(seq, n * shard)
-    query_first_grad, query_last_grad, expand_grad, latent_weight_grad = chips.lockstep(
-        chips.weight_grad(normed, query_back[:, :query_cut], BACK_QUERY[0]),
-        chips.weight_grad(normed, query_back[:, query_cut:], BACK_QUERY[1]),
-        chips.weight_grad(latent_norm, expanded_grad, BACK_EXPAND),
-        chips.weight_grad(normed_part, latent_grad, BACK_LATENT),
-    )
     query_grad = jnp.concatenate([query_first_grad, query_last_grad], axis=1)
     query_grad = chips.swap_cores(query_grad, 0, 1)
     expand_grad = chips.swap_cores(expand_grad, 0, 1)
-
-    normed_grad = outer_cols(query_back[:, :query_cut], query_parts[0]) + outer_cols(
-        query_back[:, query_cut:], query_parts[1]
-    )
-    latent_grad_own = lax.dynamic_slice_in_dim(latent_grad, core * SEQ_DEV, SEQ_DEV, 0)
-    normed_grad = chips.scatter_cores(normed_grad) + outer_cols(latent_grad_own, latent_weight)
-    _, first_pull = jax.vjp(rms_scale, inputs_f, gain_attn)
-    input_part, gain_attn_grad = first_pull(normed_grad)
-    tokens_grad = (hidden_grad + input_part).astype(BF16)
-
-    block_out = (hidden + jnp.concatenate(block_sum, axis=0)).astype(BF16)
-    small_grad = jnp.concatenate(
-        [
-            gain_attn_grad.reshape(n * cores, -1),
-            gain_ffn_grad.reshape(n * cores, -1),
-            gain_latent_grad.reshape(n * cores, -1),
-            router_grad.reshape(n * cores, -1),
-        ],
-        axis=1,
-    )
-    (small_grad,) = chips.lockstep(
-        chips.scatter_chips(small_grad.reshape(n, cores, -1), ORDER_SMALL[::-1])
-    )
-    small_grad = chips.scatter_cores(small_grad).reshape(-1)
     return (
         block_out,
         tokens_grad,

time: 982 us -> 894 us (0.910)
  waiting for transfers between devices: 332 us -> 235 us
  other arithmetic: 143 us -> 164 us
  starting transfers between devices: 145 us -> 134 us
    ppermute x108 -> x84, waiting for transfers between devices: 327 us -> 232 us  [exchange(): return lax.ppermute(value, BOTH, pairs)]
    ppermute x108 -> x84, starting transfers between devices: 131 us -> 100 us  [exchange(): return lax.ppermute(value, BOTH, pairs)]
    reshape x8 -> x15, local copies, waits for them, and re-layouts: 3.59 us -> 18.1 us  [the longest x3 8.62 us: in_grads(): shared.reshape(2, shard, n * width)]
    all_gather x1, starting transfers between devices: 0.04 us -> 11.6 us  [shared_weights(): lax.all_gather(value.reshape(n, 1, shard, 2 * width), 'fsdp', axis=1, til...]
    select_n x8 -> x18, other arithmetic: 2.88 us -> 13.2 us  [the longest x16 12.6 us: scatter_chips(): send = jnp.where(high, lower, upper)]
    unnamed x443 -> x368, local copies, waits for them, and re-layouts: 25.4 us -> 15.5 us
    concatenate x18 -> x12, other arithmetic: 25.3 us -> 16.1 us  [gather_tokens(): value = jnp.concatenate([value, other], axis=0)]
    pallas_call x1 -> x2, Pallas kernels: 38.8 us -> 44.3 us  [in_weights(): pl.pallas_call(in_weights_kernel, grid=(width // WIDE,), out_shape=[jax.S...]
  transfers between devices with their start and end apart: 136 -> 114, of which waited for: 66 -> 50; matrix products, arithmetic and copies ran while one was open for 24% -> 29% of each run, Pallas kernels for 20% -> 22%
where the time goes in v3:
time: 894 us; the launch traced here: 888 us
  waiting for transfers between devices  235 us (26%)
  Pallas kernels  199 us (22%)
  other arithmetic  164 us (18%)
  starting transfers between devices  134 us (15%)
  local copies, waits for them, and re-layouts  87.1 us (10%)
  matrix products  51.8 us (6%)
  between operations  17.6 us (2%)
    ppermute x84, waiting for transfers between devices, exchange(): return lax.ppermute(value, BOTH, pairs)  232 us
    pallas_call x4, Pallas kernels, expert_call(): pl.pallas_call(kernel, out_shape=out_shapes, in_specs=[whole_in_vmem() fo...  129 us
    ppermute x84, starting transfers between devices, exchange(): return lax.ppermute(value, BOTH, pairs)  100 us
    pallas_call x2, Pallas kernels, in_weights(): pl.pallas_call(in_weights_kernel, grid=(width // WIDE,), out_shape=[jax.S...  44.3 us
    another operation x39, other arithmetic, gather_chips(): jnp.stack([jnp.where(high, other, value), jnp.where(high, value, other)],...  25.8 us
    pallas_call x1, Pallas kernels, down_weights(): pl.pallas_call(down_weights_kernel, grid=(width // WIDE,), out_shape=[jax...  25 us
    dot_general x12, matrix products, inner_rows(): lax.dot_general(left_side, right_side, (((0,), (0,)), ((), ())), preferre...  21.2 us
  transfers between devices with their start and end apart: 114, of which 50 were waited for; matrix products, arithmetic and copies ran while one was open for 29% of the time, Pallas kernels for 22%

profile of v3, /device:TPU:0, one launch (start us, length us, event | category | flops | bytes accessed | tf_op | source)
XLA Modules:
  0.0 888.0 jit_solution(13982782952473696733)
XLA Ops:
  21.0 3.7 collective-permute-start.8
  36.8 4.8 collective-permute-done.8
  45.2 3.6 collective-permute-done.5
  48.7 4.0 collective-permute-done.6
  58.2 3.6 collective-permute-done.12
  62.8 3.3 collective-permute-done.11
  71.8 7.1 collective-permute-done.16
  79.1 8.2 collective-permute-done.15
  96.6 6.4 all-to-all-start
  103.0 11.6 %all-gather.8.cloned.1.call-start = ((), (), s32[]{:S(2)}) async-start(), calls=%async_computation.6 | async-start | bytes 2359296 | tf_op jit(solution)/shard_map/all_gather | solution.py:622
  119.7 21.0 %collective-permute-done.19 = bf16[2,2,2,32,2048]{4,3,2,1,0:T(8,128)(2,1)} collective-permute-done((bf16[2,2,2,32,2048]{4,3,2,1,0:T(8,128)(2,1)}, bf16[2,2,2,32,2048]{4,3,2,1,0:T(8,128)(2,1)}, u32[]{:S(2)}, u32[]{:S(2)}) %collective-permute-start.19) | collective-permute-done | bytes 1048608 | tf_op jit(solution)/shard_map/ppermute | solution.py:369
  147.4 6.3 collective-permute-done.17
  180.4 7.0 collective-permute-done.21
  189.4 8.3 collective-permute-done.23
  211.8 3.3 fusion.11
  244.8 4.1 collective-permute-done.29
  253.6 4.3 collective-permute-done.31
  273.0 17.5 %collective-permute-done.34 = bf16[2,2,2,128,512]{4,3,2,1,0:T(8,128)(2,1)} collective-permute-done((bf16[2,2,2,128,512]{4,3,2,1,0:T(8,128)(2,1)}, bf16[2,2,2,128,512]{4,3,2,1,0:T(8,128)(2,1)}, u32[]{:S(2)}, u32[]{:S(2)}) %collective-permute-start.34) | collective-permute-done | bytes 1048608 | tf_op jit(solution)/shard_map/ppermute | solution.py:369
  304.8 4.0 collective-permute-start.37
  319.5 13.0 %collective-permute-done.37 = bf16[128,2048]{1,0:T(8,128)(2,1)S(1)} collective-permute-done((bf16[128,2048]{1,0:T(8,128)(2,1)S(1)}, bf16[128,2048]{1,0:T(8,128)(2,1)S(1)}, u32[]{:S(2)}, u32[]{:S(2)}) %collective-permute-start.37) | collective-permute-done | bytes 524320 | tf_op jit(solution)/shard_map/ppermute | solution.py:369
  335.8 4.8 collective-permute-done.41
  349.2 8.5 collective-permute-done.44
  358.8 4.1 collective-permute-done.42
  368.6 29.4 %shard_map.306 = (bf16[384,2048]{1,0:T(8,128)(2,1)}, bf16[384,2048]{1,0:T(8,128)(2,1)}, bf16[256,2048]{1,0:T(8,128)(2,1)}, f32[1024,128]{1,0:T(8,128)}, bf16[102...) custom-call(bf16[384,2048]{1,0:T(8,128)(2,1)} %bitcast.471, ...), custom_call_target="tpu_custom_call" | custom-call | flops 20937965568 | bytes 45613056 | tf_op jit(solution)/shard_map/pallas_call | solution.py:237
  404.1 29.9 %shard_map.307 = (bf16[384,2048]{1,0:T(8,128)(2,1)}, bf16[384,2048]{1,0:T(8,128)(2,1)}, bf16[256,2048]{1,0:T(8,128)(2,1)}, f32[1024,128]{1,0:T(8,128)}, bf16[102...) custom-call(bf16[384,2048]{1,0:T(8,128)(2,1)} %bitcast.94.refs_0_.refs_3_, ...), custom_call_target="tpu_custom_call" | custom-call | flops 20937965568 | bytes 45613056 | tf_op jit(solution)/shard_map/pallas_call | solution.py:237
  438.5 34.8 %shard_map.308 = (bf16[384,2048]{1,0:T(8,128)(2,1)}, bf16[384,2048]{1,0:T(8,128)(2,1)}, bf16[256,2048]{1,0:T(8,128)(2,1)}, bf16[1024,1664]{1,0:T(8,128)(2,1)}, bf16[1024,1664]{1,0:T(8,128)(2,1)}) custom-call(bf16[384,2048]{1,0:T(8,128)(2,1)} %bitcast.501, bf16[384,2048]{1,0:T(8,128)(2,1)} %bitcast.101.refs_1_.refs_4_, ...), custom_call_target="tpu_custom_call" | custom-call | flops 20937965568 | bytes 45613056 | tf_op jit(solution)/shard_map/pallas_call | solution.py:237
  477.4 35.3 %shard_map.309 = (bf16[384,2048]{1,0:T(8,128)(2,1)}, bf16[384,2048]{1,0:T(8,128)(2,1)}, bf16[256,2048]{1,0:T(8,128)(2,1)}, bf16[1024,1664]{1,0:T(8,128)(2,1)}, bf16[1024,1664]{1,0:T(8,128)(2,1)}) custom-call(bf16[384,2048]{1,0:T(8,128)(2,1)} %bitcast.474, bf16[384,2048]{1,0:T(8,128)(2,1)} %bitcast.476, bf16[256,2048]{1,0:T(8,128)(2,1)} %bitcast.484, ...), custom_call_target="tpu_custom_call" | custom-call | flops 20937965568 | bytes 45613056 | tf_op jit(solution)/shard_map/pallas_call | solution.py:237
  524.5 6.4 collective-permute-done.59
  534.6 4.2 collective-permute-done.58
  547.8 4.1 collective-permute-done.60
  558.1 25.0 %shard_map.310 = (bf16[1408,2048]{1,0:T(8,128)(2,1)}, f32[256,2048]{1,0:T(8,128)}) custom-call(bf16[1024,1664]{1,0:T(8,128)(2,1)} %get-tuple-element.620.hidden_first, bf16[1024,1664]{1,0:T(8,128)(2,1)} %get-tuple-element.621.hidden_last, bf16[384,2048]{1,0:T(8,128)(2,1)} %bitcast.475, bf16[384,2048]{1,0:T(8,128)(2,1)} %bitcast.477, ...), custom_call_target="tpu_custom_call" | custom-call | flops 13958643712 | bytes 22020096 | tf_op jit(solution)/shard_map/pallas_call | solution.py:336
  599.2 3.5 collective-permute-done.66
  604.7 5.2 collective-permute-done.64
  628.9 22.1 %shard_map.311 = (bf16[2048,1408]{1,0:T(8,128)(2,1)}, f32[2048,256]{1,0:T(8,128)}) custom-call(bf16[384,2048]{1,0:T(8,128)(2,1)} %bitcast.472, bf16[384,2048]{1,0:T(8,128)(2,1)} %bitcast.88.refs_1_, bf16[256,2048]{1,0:T(8,128)(2,1)} %bitcast.89.refs_2_, bf16[384,2048]{1,0:T(8,128)(2,1)} %bitcast.94.refs_0_.refs_3_, ...), custom_call_target="tpu_custom_call" | custom-call | flops 13958643712 | bytes 22020096 | tf_op jit(solution)/shard_map/pallas_call | solution.py:298
  675.0 6.6 collective-permute-done.76
  681.9 9.8 %collective-permute-done.77 = bf16[2,2,128,512]{3,2,0,1:T(8,128)(2,1)S(1)} collective-permute-done((bf16[2,2,128,512]{3,2,0,1:T(8,128)(2,1)S(1)}, bf16[2,2,128,512]{3,2,0,1:T(8,128)(2,1)S(1)}, u32[]{:S(2)}, u32[]{:S(2)}) %collective-permute-start.77) | collective-permute-done | bytes 524320 | tf_op jit(solution)/shard_map/ppermute | solution.py:369
  692.8 3.4 collective-permute-done.78
  709.6 4.7 bitcast_convert_fusion.2
  714.3 22.3 %shard_map.312 = (bf16[2048,1408]{1,0:T(8,128)(2,1)}, f32[2048,256]{1,0:T(8,128)}) custom-call(bf16[384,2048]{1,0:T(8,128)(2,1)} %bitcast.473, bf16[384,2048]{1,0:T(8,128)(2,1)} %bitcast.88.refs_1_, bf16[256,2048]{1,0:T(8,128)(2,1)} %bitcast.89.refs_2_, bf16[384,2048]{1,0:T(8,128)(2,1)} %bitcast.94.refs_0_.refs_3_, ...), custom_call_target="tpu_custom_call" | custom-call | flops 13958643712 | bytes 22020096 | tf_op jit(solution)/shard_map/pallas_call | solution.py:298
  736.6 5.2 bitcast_convert_fusion.1
  747.4 3.2 collective-permute-done.82
  782.9 5.0 collective-permute-done.86
  789.1 3.3 collective-permute-done.84
  796.1 5.8 all-to-all-start.1
  811.8 8.8 collective-permute-done.93
  821.3 3.8 collective-permute-done.92
  833.0 5.9 all-to-all-start.2
  844.9 4.7 bitcast_convert_fusion
  (942 shorter events, 415.8 us)
Async XLA Ops:
  24.7 24.0 %collective-permute-start.5 = (bf16[128,768]{1,0:T(8,128)(2,1)}, bf16[128,768]{1,0:T(8,128)(2,1)}, u32[]{:S(2)}, u32[]{:S(2)}) collective-permute-start(bf16[128,768]{1,0:T(8,128)(2,1)} %get-tuple-element.389), channel_id=1, source_target_pairs={{0,16},{1,17},{2,18},{3,19},{4,20},{5,21},{6,22},{7,23},{8,24},{9,... | collective-permute-start | bytes 589832 | tf_op jit(solution)/shard_map/ppermute | solution.py:369
  27.6 25.1 %collective-permute-start.6 = (bf16[128,768]{1,0:T(8,128)(2,1)}, bf16[128,768]{1,0:T(8,128)(2,1)}, u32[]{:S(2)}, u32[]{:S(2)}) collective-permute-start(bf16[128,768]{1,0:T(8,128)(2,1)} %get-tuple-element.390), channel_id=1, source_target_pairs={{0,16},{1,17},{2,18},{3,19},{4,20},{5,21},{6,22},{7,23},{8,24},{9,... | collective-permute-start | bytes 589832 | tf_op jit(solution)/shard_map/ppermute | solution.py:369
  93.1 23.5 %collective-permute-start.20 = (bf16[2,2,2,70,576]{4,2,3,1,0:T(2,128)(2,1)}, bf16[2,2,2,70,576]{4,2,3,1,0:T(2,128)(2,1)}, u32[]{:S(2)}, u32[]{:S(2)}) collective-permute-start(bf16[2,2,2,70,576]{4,2,3,1,0:T(2,128)(2,1)} %copy.338), channel_id=1, source_target_pairs={{0,8},{1,9},{2,10},{3,11},{4,12},{5,13},{6,14},{7,15},{8,0},{9,1},... | collective-permute-start | bytes 1935368 | tf_op jit(solution)/shard_map/ppermute | solution.py:369
  94.3 46.4 %collective-permute-start.19 = (bf16[2,2,2,32,2048]{4,3,2,1,0:T(8,128)(2,1)}, bf16[2,2,2,32,2048]{4,3,2,1,0:T(8,128)(2,1)}, u32[]{:S(2)}, u32[]{:S(2)}) collective-permute-start(bf16[2,2,2,32,2048]{4,3,2,1,0:T(8,128)(2,1)} %pad_maximum_fusion.18), channel_id=1, source_target_pairs={{0,8},{1,9},{2,10},{3,11},{4,12},{5,13},{6,14},{7,15},{8,0},{9,1},... | collective-permute-start | bytes 3145736 | tf_op jit(solution)/shard_map/ppermute | solution.py:369
  95.1 48.5 %collective-permute-start.18 = (bf16[2,2,2,128,768]{4,3,0,2,1:T(8,128)(2,1)}, bf16[2,2,2,128,768]{4,3,0,2,1:T(8,128)(2,1)}, u32[]{:S(2)}, u32[]{:S(2)}) collective-permute-start(bf16[2,2,2,128,768]{4,3,0,2,1:T(8,128)(2,1)} %pad_maximum_fusion.10), channel_id=1, source_target_pairs={{0,2},{1,3},{2,0},{3,1},{4,6},{5,7},{6,4},{7,5},{8,10},{9,11},{10,... | collective-permute-start | bytes 4718600 | tf_op jit(solution)/shard_map/ppermute | solution.py:369
  96.6 59.2 %all-to-all-start = ((bf16[16,64,352]{2,1,0:T(8,128)(2,1)}), bf16[16,64,352]{2,1,0:T(8,128)(2,1)}, u32[]{:S(2)}, u32[]{:S(2)}) async-start(bf16[16,64,352]{2,1,0:T(8,128)(2,1)} %bitcast.464), calls=%async_computation | async-start | bytes 1572864 | tf_op jit(solution)/shard_map/all_to_all | solution.py:583
  103.0 98.9 %all-gather.8.cloned.1.call-start = ((), (), s32[]{:S(2)}) async-start(), calls=%async_computation.6 | async-start | bytes 2359296 | tf_op jit(solution)/shard_map/all_gather | solution.py:622
  114.6 39.0 %collective-permute-start.17 = (bf16[2,2,2,128,768]{4,3,2,1,0:T(8,128)(2,1)}, bf16[2,2,2,128,768]{4,3,2,1,0:T(8,128)(2,1)S(1)}, u32[]{:S(2)}, u32[]{:S(2)}) collective-permute-start(bf16[2,2,2,128,768]{4,3,2,1,0:T(8,128)(2,1)} %pad_maximum_fusion.9), channel_id=1, source_target_pairs={{0,4},{1,5},{2,6},{3,7},{4,0},{5,1},{6,2},{7,3},{8,12},{9,13},{10,... | collective-permute-start | bytes 4718600 | tf_op jit(solution)/shard_map/ppermute | solution.py:369
  155.8 176.7 %all-gather.10.cloned.1.call-start = ((), (), s32[]{:S(2)}) async-start(), calls=%async_computation.10 | async-start | bytes 8650752 | tf_op jit(solution)/shard_map/all_gather | solution.py:611
  156.6 176.0 %all-gather.12.cloned.1.call-start = ((), (), s32[]{:S(2)}) async-start(), calls=%async_computation.11 | async-start | bytes 8650752 | tf_op jit(solution)/shard_map/all_gather | solution.py:611
  157.3 175.3 %all-gather.14.cloned.1.call-start = ((), (), s32[]{:S(2)}) async-start(), calls=%async_computation.12 | async-start | bytes 8650752 | tf_op jit(solution)/shard_map/all_gather | solution.py:611
  157.9 455.5 %reduce-scatter.4.cloned.1.call-start = ((), (), s32[]{:S(2)}) async-start(), calls=%async_computation.7 | async-start | bytes 8650752 | tf_op jit(solution)/shard_map/reduce_scatter | solution.py:863
  164.0 23.5 %collective-permute-start.21 = (bf16[128,1024]{1,0:T(8,128)(2,1)}, bf16[128,1024]{1,0:T(8,128)(2,1)}, u32[]{:S(2)}, u32[]{:S(2)}) collective-permute-start(bf16[128,1024]{1,0:T(8,128)(2,1)} %pad_maximum_fusion.56), channel_id=1, source_target_pairs={{0,16},{1,17},{2,18},{3,19},{4,20},{5,21},{6,22},{7,23},{8,24},{9,... | collective-permute-start | bytes 786440 | tf_op jit(solution)/shard_map/ppermute | solution.py:369
  166.5 31.3 %collective-permute-start.23 = (bf16[128,2048]{1,0:T(8,128)(2,1)}, bf16[128,2048]{1,0:T(8,128)(2,1)}, u32[]{:S(2)}, u32[]{:S(2)}) collective-permute-start(bf16[128,2048]{1,0:T(8,128)(2,1)} %param.36), channel_id=1, source_target_pairs={{0,16},{1,17},{2,18},{3,19},{4,20},{5,21},{6,22},{7,23},{8,24},{9,... | collective-permute-start | bytes 1572872 | tf_op jit(solution)/shard_map/ppermute | solution.py:369
  238.2 24.9 %collective-permute-start.32 = (bf16[4,48,2048]{2,1,0:T(8,128)(2,1)}, bf16[4,48,2048]{2,1,0:T(8,128)(2,1)}, u32[]{:S(2)}, u32[]{:S(2)}) collective-permute-start(bf16[4,48,2048]{2,1,0:T(8,128)(2,1)} %pad_maximum_fusion.27), channel_id=1, source_target_pairs={{0,8},{1,9},{2,10},{3,11},{4,12},{5,13},{6,14},{7,15},{8,0},{9,1},... | collective-permute-start | bytes 2359304 | tf_op jit(solution)/shard_map/ppermute | solution.py:369
  267.5 22.9 %collective-permute-start.34 = (bf16[2,2,2,128,512]{4,3,2,1,0:T(8,128)(2,1)}, bf16[2,2,2,128,512]{4,3,2,1,0:T(8,128)(2,1)}, u32[]{:S(2)}, u32[]{:S(2)}) collective-permute-start(bf16[2,2,2,128,512]{4,3,2,1,0:T(8,128)(2,1)} %pad_maximum_fusion.19), channel_id=1, source_target_pairs={{0,8},{1,9},{2,10},{3,11},{4,12},{5,13},{6,14},{7,15},{8,0},{9,1},... | collective-permute-start | bytes 3145736 | tf_op jit(solution)/shard_map/ppermute | solution.py:369
  304.8 27.7 %collective-permute-start.37 = (bf16[128,2048]{1,0:T(8,128)(2,1)S(1)}, bf16[128,2048]{1,0:T(8,128)(2,1)S(1)}, u32[]{:S(2)}, u32[]{:S(2)}) collective-permute-start(bf16[128,2048]{1,0:T(8,128)(2,1)S(1)} %multiply_convert_fusion.1), channel_id=1, source_target_pairs={{0,16},{1,17},{2,18},{3,19},{4,20},{5,21},{6,22},{7,23},{8,24},{9,... | collective-permute-start | bytes 1572872 | tf_op jit(solution)/shard_map/ppermute | solution.py:369
  365.9 32.1 %collective-permute-start.47 = (bf16[8,32,2048]{2,1,0:T(8,128)(2,1)}, bf16[8,32,2048]{2,1,0:T(8,128)(2,1)}, u32[]{:S(2)}, u32[]{:S(2)}) collective-permute-start(bf16[8,32,2048]{2,1,0:T(8,128)(2,1)} %pad_maximum_fusion.23), channel_id=1, source_target_pairs={{0,2},{1,3},{2,0},{3,1},{4,6},{5,7},{6,4},{7,5},{8,10},{9,11},{10,... | collective-permute-start | bytes 3145736 | tf_op jit(solution)/shard_map/ppermute | solution.py:369
  367.3 33.4 %collective-permute-start.45 = (bf16[8,48,2048]{2,1,0:T(8,128)(2,1)S(1)}, bf16[8,48,2048]{2,1,0:T(8,128)(2,1)}, u32[]{:S(2)}, u32[]{:S(2)}) collective-permute-start(bf16[8,48,2048]{2,1,0:T(8,128)(2,1)S(1)} %pad_maximum_fusion.14), channel_id=1, source_target_pairs={{0,8},{1,9},{2,10},{3,11},{4,12},{5,13},{6,14},{7,15},{8,0},{9,1},... | collective-permute-start | bytes 4718600 | tf_op jit(solution)/shard_map/ppermute | solution.py:369
  368.1 32.9 %collective-permute-start.46 = (bf16[8,48,2048]{2,1,0:T(8,128)(2,1)}, bf16[8,48,2048]{2,1,0:T(8,128)(2,1)}, u32[]{:S(2)}, u32[]{:S(2)}) collective-permute-start(bf16[8,48,2048]{2,1,0:T(8,128)(2,1)} %pad_maximum_fusion.15), channel_id=1, source_target_pairs={{0,4},{1,5},{2,6},{3,7},{4,0},{5,1},{6,2},{7,3},{8,12},{9,13},{10,... | collective-permute-start | bytes 4718600 | tf_op jit(solution)/shard_map/ppermute | solution.py:369
  401.0 33.1 %collective-permute-start.50 = (bf16[8,32,2048]{2,1,0:T(8,128)(2,1)}, bf16[8,32,2048]{2,1,0:T(8,128)(2,1)}, u32[]{:S(2)}, u32[]{:S(2)}) collective-permute-start(bf16[8,32,2048]{2,1,0:T(8,128)(2,1)} %pad_maximum_fusion.22), channel_id=1, source_target_pairs={{0,2},{1,3},{2,0},{3,1},{4,6},{5,7},{6,4},{7,5},{8,10},{9,11},{10,... | collective-permute-start | bytes 3145736 | tf_op jit(solution)/shard_map/ppermute | solution.py:369
  402.1 32.5 %collective-permute-start.48 = (bf16[8,48,2048]{2,1,0:T(8,128)(2,1)}, bf16[8,48,2048]{2,1,0:T(8,128)(2,1)S(1)}, u32[]{:S(2)}, u32[]{:S(2)}) collective-permute-start(bf16[8,48,2048]{2,1,0:T(8,128)(2,1)} %pad_maximum_fusion.12), channel_id=1, source_target_pairs={{0,8},{1,9},{2,10},{3,11},{4,12},{5,13},{6,14},{7,15},{8,0},{9,1},... | collective-permute-start | bytes 4718600 | tf_op jit(solution)/shard_map/ppermute | solution.py:369
  403.9 32.6 %collective-permute-start.49 = (bf16[8,48,2048]{2,1,0:T(8,128)(2,1)}, bf16[8,48,2048]{2,1,0:T(8,128)(2,1)}, u32[]{:S(2)}, u32[]{:S(2)}) collective-permute-start(bf16[8,48,2048]{2,1,0:T(8,128)(2,1)} %pad_maximum_fusion.13), channel_id=1, source_target_pairs={{0,4},{1,5},{2,6},{3,7},{4,0},{5,1},{6,2},{7,3},{8,12},{9,13},{10,... | collective-permute-start | bytes 4718600 | tf_op jit(solution)/shard_map/ppermute | solution.py:369
  436.5 36.7 %collective-permute-start.53 = (bf16[8,32,2048]{2,1,0:T(8,128)(2,1)}, bf16[8,32,2048]{2,1,0:T(8,128)(2,1)}, u32[]{:S(2)}, u32[]{:S(2)}) collective-permute-start(bf16[8,32,2048]{2,1,0:T(8,128)(2,1)} %bitcast.508), channel_id=1, source_target_pairs={{0,2},{1,3},{2,0},{3,1},{4,6},{5,7},{6,4},{7,5},{8,10},{9,11},{10,... | collective-permute-start | bytes 3145736 | tf_op jit(solution)/shard_map/ppermute | solution.py:369
  437.0 36.3 %collective-permute-start.51 = (bf16[8,48,2048]{2,1,0:T(8,128)(2,1)}, bf16[8,48,2048]{2,1,0:T(8,128)(2,1)S(1)}, u32[]{:S(2)}, u32[]{:S(2)}) collective-permute-start(bf16[8,48,2048]{2,1,0:T(8,128)(2,1)} %bitcast.506), channel_id=1, source_target_pairs={{0,8},{1,9},{2,10},{3,11},{4,12},{5,13},{6,14},{7,15},{8,0},{9,1},... | collective-permute-start | bytes 4718600 | tf_op jit(solution)/shard_map/ppermute | solution.py:369
  438.3 35.0 %collective-permute-start.52 = (bf16[8,48,2048]{2,1,0:T(8,128)(2,1)}, bf16[8,48,2048]{2,1,0:T(8,128)(2,1)}, u32[]{:S(2)}, u32[]{:S(2)}) collective-permute-start(bf16[8,48,2048]{2,1,0:T(8,128)(2,1)} %bitcast.505), channel_id=1, source_target_pairs={{0,4},{1,5},{2,6},{3,7},{4,0},{5,1},{6,2},{7,3},{8,12},{9,13},{10,... | collective-permute-start | bytes 4718600 | tf_op jit(solution)/shard_map/ppermute | solution.py:369
  473.3 41.6 %collective-permute-start.56 = (bf16[8,32,2048]{2,1,0:T(8,128)(2,1)}, bf16[8,32,2048]{2,1,0:T(8,128)(2,1)}, u32[]{:S(2)}, u32[]{:S(2)}) collective-permute-start(bf16[8,32,2048]{2,1,0:T(8,128)(2,1)} %bitcast.507), channel_id=1, source_target_pairs={{0,2},{1,3},{2,0},{3,1},{4,6},{5,7},{6,4},{7,5},{8,10},{9,11},{10,... | collective-permute-start | bytes 3145736 | tf_op jit(solution)/shard_map/ppermute | solution.py:369
  474.8 40.1 %collective-permute-start.54 = (bf16[8,48,2048]{2,1,0:T(8,128)(2,1)}, bf16[8,48,2048]{2,1,0:T(8,128)(2,1)}, u32[]{:S(2)}, u32[]{:S(2)}) collective-permute-start(bf16[8,48,2048]{2,1,0:T(8,128)(2,1)} %bitcast.504), channel_id=1, source_target_pairs={{0,8},{1,9},{2,10},{3,11},{4,12},{5,13},{6,14},{7,15},{8,0},{9,1},... | collective-permute-start | bytes 4718600 | tf_op jit(solution)/shard_map/ppermute | solution.py:369
  476.0 38.9 %collective-permute-start.55 = (bf16[8,48,2048]{2,1,0:T(8,128)(2,1)}, bf16[8,48,2048]{2,1,0:T(8,128)(2,1)}, u32[]{:S(2)}, u32[]{:S(2)}) collective-permute-start(bf16[8,48,2048]{2,1,0:T(8,128)(2,1)} %bitcast.503), channel_id=1, source_target_pairs={{0,4},{1,5},{2,6},{3,7},{4,0},{5,1},{6,2},{7,3},{8,12},{9,13},{10,... | collective-permute-start | bytes 4718600 | tf_op jit(solution)/shard_map/ppermute | solution.py:369
  555.4 27.8 %collective-permute-start.63 = (bf16[128,2048]{1,0:T(8,128)(2,1)S(1)}, bf16[128,2048]{1,0:T(8,128)(2,1)S(1)}, u32[]{:S(2)}, u32[]{:S(2)}) collective-permute-start(bf16[128,2048]{1,0:T(8,128)(2,1)S(1)} %fusion.40), channel_id=1, source_target_pairs={{0,16},{1,17},{2,18},{3,19},{4,20},{5,21},{6,22},{7,23},{8,24},{9,... | collective-permute-start | bytes 1572872 | tf_op jit(solution)/shard_map/ppermute | solution.py:369
  584.5 122.2 %reduce-scatter.6.cloned.1.call-start = ((), (), s32[]{:S(2)}) async-start(), calls=%async_computation.8 | async-start | bytes 8650752 | tf_op jit(solution)/shard_map/reduce_scatter | solution.py:847
  613.4 38.7 %collective-permute-start.72 = (bf16[2,32,2048]{2,1,0:T(8,128)(2,1)}, bf16[2,32,2048]{2,1,0:T(8,128)(2,1)}, u32[]{:S(2)}, u32[]{:S(2)}) collective-permute-start(bf16[2,32,2048]{2,1,0:T(8,128)(2,1)} %slice.889), channel_id=1, source_target_pairs={{0,8},{1,9},{2,10},{3,11},{4,12},{5,13},{6,14},{7,15},{8,0},{9,1},... | collective-permute-start | bytes 786440 | tf_op jit(solution)/shard_map/ppermute | solution.py:369
  614.4 38.7 %collective-permute-start.70 = (bf16[2,48,2048]{2,1,0:T(8,128)(2,1)}, bf16[2,48,2048]{2,1,0:T(8,128)(2,1)}, u32[]{:S(2)}, u32[]{:S(2)}) collective-permute-start(bf16[2,48,2048]{2,1,0:T(8,128)(2,1)} %slice.885), channel_id=1, source_target_pairs={{0,4},{1,5},{2,6},{3,7},{4,0},{5,1},{6,2},{7,3},{8,12},{9,13},{10,... | collective-permute-start | bytes 1179656 | tf_op jit(solution)/shard_map/ppermute | solution.py:369
  616.0 38.2 %collective-permute-start.71 = (bf16[2,48,2048]{2,1,0:T(8,128)(2,1)}, bf16[2,48,2048]{2,1,0:T(8,128)(2,1)}, u32[]{:S(2)}, u32[]{:S(2)}) collective-permute-start(bf16[2,48,2048]{2,1,0:T(8,128)(2,1)} %slice.887), channel_id=1, source_target_pairs={{0,2},{1,3},{2,0},{3,1},{4,6},{5,7},{6,4},{7,5},{8,10},{9,11},{10,... | collective-permute-start | bytes 1179656 | tf_op jit(solution)/shard_map/ppermute | solution.py:369
  627.6 28.9 %collective-permute-start.73 = (bf16[1024,512]{1,0:T(8,128)(2,1)}, bf16[1024,512]{1,0:T(8,128)(2,1)}, u32[]{:S(2)}, u32[]{:S(2)}) collective-permute-start(bf16[1024,512]{1,0:T(8,128)(2,1)} %convolution_convert_fusion.5), channel_id=1, source_target_pairs={{0,8},{1,9},{2,10},{3,11},{4,12},{5,13},{6,14},{7,15},{8,0},{9,1},... | collective-permute-start | bytes 3145736 | tf_op jit(solution)/shard_map/ppermute | solution.py:369
  628.2 30.2 %collective-permute-start.74 = (bf16[1024,512]{1,0:T(8,128)(2,1)}, bf16[1024,512]{1,0:T(8,128)(2,1)}, u32[]{:S(2)}, u32[]{:S(2)}) collective-permute-start(bf16[1024,512]{1,0:T(8,128)(2,1)} %convolution_convert_fusion.4), channel_id=1, source_target_pairs={{0,2},{1,3},{2,0},{3,1},{4,6},{5,7},{6,4},{7,5},{8,10},{9,11},{10,... | collective-permute-start | bytes 3145736 | tf_op jit(solution)/shard_map/ppermute | solution.py:369
  662.5 169.4 %reduce-scatter.8.cloned.1.call-start = ((), (), s32[]{:S(2)}) async-start(), calls=%async_computation.9 | async-start | bytes 8650752 | tf_op jit(solution)/shard_map/reduce_scatter | solution.py:852
  672.6 23.6 %collective-permute-start.78 = (bf16[128,2048]{1,0:T(8,128)(2,1)S(1)}, bf16[128,2048]{1,0:T(8,128)(2,1)S(1)}, u32[]{:S(2)}, u32[]{:S(2)}) collective-permute-start(bf16[128,2048]{1,0:T(8,128)(2,1)S(1)} %copy-done.139), channel_id=1, source_target_pairs={{0,16},{1,17},{2,18},{3,19},{4,20},{5,21},{6,22},{7,23},{8,24},{9,... | collective-permute-start | bytes 1572872 | tf_op jit(solution)/shard_map/ppermute | solution.py:369
  673.5 23.8 %collective-permute-start.75 = (f32[256,576]{0,1:T(8,128)S(1)}, f32[256,576]{0,1:T(8,128)S(1)}, u32[]{:S(2)}, u32[]{:S(2)}) collective-permute-start(f32[256,576]{0,1:T(8,128)S(1)} %pad_maximum_fusion.33), channel_id=1, source_target_pairs={{0,1},{1,0},{2,3},{3,2},{4,5},{5,4},{6,7},{7,6},{8,9},{9,8},{10,11... | collective-permute-start | bytes 1769480 | tf_op jit(solution)/shard_map/ppermute | solution.py:372
  706.8 35.0 %collective-permute-start.80 = (bf16[2,128,1024]{2,1,0:T(8,128)(2,1)}, bf16[2,128,1024]{2,1,0:T(8,128)(2,1)S(1)}, u32[]{:S(2)}, u32[]{:S(2)}) collective-permute-start(bf16[2,128,1024]{2,1,0:T(8,128)(2,1)} %select_bitcast_fusion.19), channel_id=1, source_target_pairs={{0,4},{1,5},{2,6},{3,7},{4,0},{5,1},{6,2},{7,3},{8,12},{9,13},{10,... | collective-permute-start | bytes 1572872 | tf_op jit(solution)/shard_map/ppermute | solution.py:369
  707.2 35.6 %collective-permute-start.83 = (bf16[512,576]{0,1:T(8,128)(2,1)}, bf16[512,576]{0,1:T(8,128)(2,1)}, u32[]{:S(2)}, u32[]{:S(2)}) collective-permute-start(bf16[512,576]{0,1:T(8,128)(2,1)} %convolution_convert_fusion.6), channel_id=1, source_target_pairs={{0,4},{1,5},{2,6},{3,7},{4,0},{5,1},{6,2},{7,3},{8,12},{9,13},{10,... | collective-permute-start | bytes 1769480 | tf_op jit(solution)/shard_map/ppermute | solution.py:369
  708.8 41.8 %collective-permute-start.82 = (bf16[256,2048]{1,0:T(8,128)(2,1)}, bf16[256,2048]{1,0:T(8,128)(2,1)}, u32[]{:S(2)}, u32[]{:S(2)}) collective-permute-start(bf16[256,2048]{1,0:T(8,128)(2,1)} %convolution_convert_fusion.1), channel_id=1, source_target_pairs={{0,4},{1,5},{2,6},{3,7},{4,0},{5,1},{6,2},{7,3},{8,12},{9,13},{10,... | collective-permute-start | bytes 3145736 | tf_op jit(solution)/shard_map/ppermute | solution.py:369
  709.3 46.5 %collective-permute-start.79 = (bf16[1024,768]{1,0:T(8,128)(2,1)}, bf16[1024,768]{1,0:T(8,128)(2,1)}, u32[]{:S(2)}, u32[]{:S(2)}) collective-permute-start(bf16[1024,768]{1,0:T(8,128)(2,1)} %convolution_convert_fusion.3), channel_id=1, source_target_pairs={{0,2},{1,3},{2,0},{3,1},{4,6},{5,7},{6,4},{7,5},{8,10},{9,11},{10,... | collective-permute-start | bytes 4718600 | tf_op jit(solution)/shard_map/ppermute | solution.py:369
  709.6 43.8 %collective-permute-start.81 = (bf16[1024,768]{1,0:T(8,128)(2,1)}, bf16[1024,768]{1,0:T(8,128)(2,1)}, u32[]{:S(2)}, u32[]{:S(2)}) collective-permute-start(bf16[1024,768]{1,0:T(8,128)(2,1)} %convolution_convert_fusion.2), channel_id=1, source_target_pairs={{0,8},{1,9},{2,10},{3,11},{4,12},{5,13},{6,14},{7,15},{8,0},{9,1},... | collective-permute-start | bytes 4718600 | tf_op jit(solution)/shard_map/ppermute | solution.py:369
  796.1 35.8 %all-to-all-start.1 = ((bf16[16,64,352]{2,1,0:T(8,128)(2,1)}), bf16[16,64,352]{2,1,0:T(8,128)(2,1)S(1)}, u32[]{:S(2)}, u32[]{:S(2)}) async-start(bf16[16,64,352]{2,1,0:T(8,128)(2,1)} %add_convert_fusion.11), calls=%async_computation.3 | async-start | bytes 1572864 | tf_op jit(solution)/shard_map/all_to_all | solution.py:856
  833.0 35.9 %all-to-all-start.2 = ((f32[16,1,2336]{2,1,0:T(1,128)}), f32[16,1,2336]{2,1,0:T(1,128)}, u32[]{:S(2)}, u32[]{:S(2)}) async-start(f32[16,1,2336]{2,1,0:T(1,128)} %all_to_all.23), calls=%async_computation.5 | async-start | bytes 311296 | tf_op jit(solution)/shard_map/all_to_all | solution.py:950
  841.9 25.0 %collective-permute-start.96 = (bf16[128,768]{1,0:T(8,128)(2,1)}, bf16[128,768]{1,0:T(8,128)(2,1)}, u32[]{:S(2)}, u32[]{:S(2)}) collective-permute-start(bf16[128,768]{1,0:T(8,128)(2,1)} %select_bitcast_fusion.45), channel_id=1, source_target_pairs={{0,16},{1,17},{2,18},{3,19},{4,20},{5,21},{6,22},{7,23},{8,24},{9,... | collective-permute-start | bytes 589832 | tf_op jit(solution)/shard_map/ppermute | solution.py:369
  844.8 25.3 %collective-permute-start.97 = (bf16[128,768]{1,0:T(8,128)(2,1)}, bf16[128,768]{1,0:T(8,128)(2,1)}, u32[]{:S(2)}, u32[]{:S(2)}) collective-permute-start(bf16[128,768]{1,0:T(8,128)(2,1)} %select_bitcast_fusion.44), channel_id=1, source_target_pairs={{0,16},{1,17},{2,18},{3,19},{4,20},{5,21},{6,22},{7,23},{8,24},{9,... | collective-permute-start | bytes 589832 | tf_op jit(solution)/shard_map/ppermute | solution.py:369
  (248 other events, 2030.5 us)
Sparse Core Ops, SparseCore 0:
  155.9 10.7 all-gather.7
  168.3 17.1 all-gather.9
  187.0 17.1 all-gather.11
  205.6 17.1 all-gather.13
  584.6 12.6 reduce-scatter.3
  662.6 11.8 reduce-scatter.5
  761.8 13.4 reduce-scatter.7

commit v4 on v3

--- a/solution.py
+++ b/solution.py
@@ -34,7 +34,7 @@
 BACK_QUERY = ((1, 4, 2, 8), (4, 2, 1, 8))
 BACK_EXPAND = (2, 1, 4, 8)
 BACK_LATENT = (2, 1, 4, 8)
-BACK_OUTPUT = ((4, 1), (1, 4), (2, 8))
+BACK_OUTPUT = ((4, 2), (2, 4), (1, 8))
 
 
 def rms_scale(values, gain_vec):
@@ -294,7 +294,7 @@
     tokens, units = acts_back[0].shape
     width = rows[0].shape[1]
     whole = pl.BlockSpec((tokens, units), lambda i: (0, 0), pipeline_mode=pl.Buffered(1))
-    outs = [((width, ff), BF16), ((width, units - ff), F32)]
+    outs = [((width, ff), BF16), ((width, units - ff), BF16)]
     return pl.pallas_call(
         in_weights_kernel,
         grid=(width // WIDE,),
@@ -475,14 +475,16 @@
             value = value.reshape((2 ** len(left),) + rest)
         return value if left else value[0]
 
+    def first_halves(self, rows, order):
+        return self.halves(rows, self.bits(order)[0], rows.shape[1] // self.n)
+
     def weight_grad(self, rows, grads, order):
         mask = self.bits(order)[0]
-        width = rows.shape[1] // self.n
-        keep, send = self.halves(rows, mask, width)
+        keep, send = rows
         away = inner_rows(send, grads).astype(BF16)
         other = yield away, mask
         value = inner_rows(keep, grads) + other.astype(F32)
-        value = value.astype(BF16).reshape(self.n // 2, width, -1)
+        value = value.astype(BF16).reshape(self.n // 2, -1, grads.shape[1])
         return (yield from self.scatter_chips(value, order[1:], (mask,)))
 
     def gather_groups(self, value, states):
@@ -786,11 +788,21 @@
         down_extra = jnp.pad(chips.gather_cores(shared_down_own), ((0, extra - width), (0, 0)))
         return gate_full, gate_extra, up_full, up_extra, down_full, down_extra
 
-    *rows_first, output_full, weights = chips.lockstep(
+    def backward_halves(attended, normed, latent_norm, normed_part):
+        return (
+            [chips.first_halves(attended, order) for order in BACK_OUTPUT[:2]],
+            [chips.first_halves(normed, order) for order in BACK_QUERY],
+            chips.first_halves(latent_norm, BACK_EXPAND),
+            chips.first_halves(normed_part, BACK_LATENT),
+        )
+
+    *rows_first, halves, output_full, weights = chips.lockstep(
         *chips.gather_groups(normed_ffn, {}),
+        beside(backward_halves, attended, normed, latent_norm, normed_part),
         beside(lambda *parts: joined_output(parts), *output_parts),
         beside(extra_weights, shared_in, small[:, small_cut[2] :].reshape(D, -1), shared_down),
     )
+    attended_halves, normed_halves, latent_halves, normed_part_halves = halves
     *rows_last, (out_first, kept_first) = chips.lockstep(
         *chips.last_groups(rows_first), beside(forward, rows_first, members[0])
     )
@@ -830,7 +842,7 @@
         yield from idle(1)
         grads = middle["attn_grad"][:, part * output_cut : (part + 1) * output_cut]
         order = chips.bits(BACK_OUTPUT[part])
-        value = yield from chips.weight_grad(attended, grads, order)
+        value = yield from chips.weight_grad(attended_halves[part], grads, order)
         middle["output", part] = value
         if part == 0:
             yield from idle(2)
@@ -840,18 +852,18 @@
 
     def in_grads(rows, gate_back, up_back):
         rows = [v for groups in rows for v in groups]
-        yield from idle(1)
+        yield from idle(2)
         rows, gate_back = yield (rows, gate_back), None
         gate_w, gate_x = yield in_weights(rows, gate_back, ff), None
         middle["router_grad"] = gate_x[:, width : width + expert_count]
         gate_w = lax.psum_scatter(gate_w, "fsdp", scatter_dimension=0, tiled=True)
-        gate_w, rows, up_back = yield (gate_w, rows, up_back), None
+        rows, up_back = together(rows, up_back, gate_x)[:2]
         up_w, up_x = in_weights(rows, up_back, ff)
+        gate_w, up_w, gate_x, up_x = yield (gate_w, up_w, gate_x, up_x), None
         gate_w = gate_w.astype(F32)[None]
-        gate_w, up_w, gate_x, up_x = yield (gate_w, up_w, gate_x, up_x), None
         up_w = lax.psum_scatter(up_w, "fsdp", scatter_dimension=0, tiled=True)
         shared = jnp.concatenate([gate_x[:, :width], up_x[:, :width]], axis=1)
-        shared = chips.scatter_cores(shared.reshape(n, cores * shard, 2 * width), 1).astype(BF16)
+        shared = chips.scatter_cores(shared.reshape(n, cores * shard, 2 * width), 1)
         shared = yield shared, None
         shared = lax.all_to_all(shared, "expert", split_axis=0, concat_axis=0, tiled=True)
         shared, up_w = yield (shared, up_w), None
@@ -922,15 +934,15 @@
         yield from idle(3)
         return (yield from chips.weight_grad(rows, middle[name][:, columns], order))
 
+    back_cut = heads * (DN + DR) * 5 // 12 // LANES * LANES
+
     def input_grads():
-        yield from idle(5)
-        query_back, latent_grad, latent_rows = yield (
-            (middle["query_back"], middle["latent_grad"], latent_own),
-            None,
-        )
+        yield from idle(4)
+        query_back, latent_grad = yield (middle["query_back"], middle["latent_grad"]), None
         normed_grad = outer_cols(query_back[:, :query_cut], query_parts[0]) + outer_cols(
             query_back[:, query_cut:], query_parts[1]
         )
+        normed_grad, latent_grad, latent_rows = yield (normed_grad, latent_grad, latent_own), None
         latent_weight = chips.gather_cores(latent_rows[:, None], axis=1).reshape(D, -1)
         latent_grad_own = lax.dynamic_slice_in_dim(latent_grad, core * SEQ_DEV, SEQ_DEV, 0)
         normed_grad = chips.scatter_cores(normed_grad) + outer_cols(latent_grad_own, latent_weight)
@@ -943,7 +955,7 @@
                 gain_attn_grad.reshape(n * cores, -1),
                 middle["gain"].reshape(n * cores, -1),
                 middle["gain_latent_grad"].reshape(n * cores, -1),
-                middle["router_grad"].reshape(n * cores, -1),
+                middle["router_grad"].astype(F32).reshape(n * cores, -1),
             ],
             axis=1,
         )
@@ -962,10 +974,10 @@
         attention_back(),
         output_grads(0),
         output_grads(1),
-        projection_grads(normed, "query_back", slice(0, query_cut), BACK_QUERY[0]),
-        projection_grads(normed, "query_back", slice(query_cut, None), BACK_QUERY[1]),
-        projection_grads(latent_norm, "expanded_grad", slice(None), BACK_EXPAND),
-        projection_grads(normed_part, "latent_grad", slice(None), BACK_LATENT),
+        projection_grads(normed_halves[0], "query_back", slice(0, back_cut), BACK_QUERY[0]),
+        projection_grads(normed_halves[1], "query_back", slice(back_cut, None), BACK_QUERY[1]),
+        projection_grads(latent_halves, "expanded_grad", slice(None), BACK_EXPAND),
+        projection_grads(normed_part_halves, "latent_grad", slice(None), BACK_LATENT),
         in_grads(
             (kept_first[0], kept_last[0]),
             (grads_first[1], grads_last[1]),

time: 894 us -> 875 us (0.979)
  waiting for transfers between devices: 235 us -> 209 us
    ppermute x84, waiting for transfers between devices: 232 us -> 207 us  [exchange(): return lax.ppermute(value, BOTH, pairs)]
    unnamed x368 -> x328, local copies, waits for them, and re-layouts: 15.5 us -> 18.9 us
    another operation x39 -> x38, other arithmetic: 25.8 us -> 25.2 us  [gather_chips(): jnp.stack([jnp.where(high, other, value), jnp.where(high, value, other)],...]
  transfers between devices with their start and end apart: 114 -> 114, of which waited for: 50 -> 50; matrix products, arithmetic and copies ran while one was open for 29% -> 30% of each run, Pallas kernels for 22% -> 23%
where the time goes in v4:
time: 875 us; the launch traced here: 865 us
  waiting for transfers between devices  209 us (24%)
  Pallas kernels  200 us (23%)
  other arithmetic  169 us (19%)
  starting transfers between devices  134 us (15%)
  local copies, waits for them, and re-layouts  86.6 us (10%)
  matrix products  48.1 us (5%)
  between operations  17.5 us (2%)
    ppermute x84, waiting for transfers between devices, exchange(): return lax.ppermute(value, BOTH, pairs)  207 us
    pallas_call x4, Pallas kernels, expert_call(): pl.pallas_call(kernel, out_shape=out_shapes, in_specs=[whole_in_vmem() fo...  130 us
    ppermute x84, starting transfers between devices, exchange(): return lax.ppermute(value, BOTH, pairs)  102 us
    pallas_call x2, Pallas kernels, in_weights(): pl.pallas_call(in_weights_kernel, grid=(width // WIDE,), out_shape=[jax.S...  45.4 us
    another operation x38, other arithmetic, gather_chips(): jnp.stack([jnp.where(high, other, value), jnp.where(high, value, other)],...  25.2 us
    pallas_call x1, Pallas kernels, down_weights(): pl.pallas_call(down_weights_kernel, grid=(width // WIDE,), out_shape=[jax...  25 us
    unnamed x328, local copies, waits for them, and re-layouts  18.9 us
    dot_general x12, matrix products, inner_rows(): lax.dot_general(left_side, right_side, (((0,), (0,)), ((), ())), preferre...  18.6 us
  transfers between devices with their start and end apart: 114, of which 50 were waited for; matrix products, arithmetic and copies ran while one was open for 30% of the time, Pallas kernels for 23%

profile of v4, /device:TPU:0, one launch (start us, length us, event | category | flops | bytes accessed | tf_op | source)
XLA Modules:
  0.0 864.5 jit_solution(15155069327346933317)
XLA Ops:
  21.1 3.7 collective-permute-start.8
  35.9 5.9 collective-permute-done.8
  45.7 3.2 collective-permute-done.5
  48.9 4.0 collective-permute-done.6
  58.3 3.3 collective-permute-done.12
  62.7 3.3 collective-permute-done.11
  71.9 7.1 collective-permute-done.16
  79.2 8.2 collective-permute-done.15
  96.7 6.2 all-to-all-start
  102.9 11.5 %all-gather.8.cloned.1.call-start = ((), (), s32[]{:S(2)}) async-start(), calls=%async_computation.6 | async-start | bytes 2359296 | tf_op jit(solution)/shard_map/all_gather | solution.py:624
  119.8 21.0 %collective-permute-done.19 = bf16[2,2,2,32,2048]{4,3,2,1,0:T(8,128)(2,1)} collective-permute-done((bf16[2,2,2,32,2048]{4,3,2,1,0:T(8,128)(2,1)}, bf16[2,2,2,32,2048]{4,3,2,1,0:T(8,128)(2,1)}, u32[]{:S(2)}, u32[]{:S(2)}) %collective-permute-start.19) | collective-permute-done | bytes 1048608 | tf_op jit(solution)/shard_map/ppermute | solution.py:369
  147.6 5.7 collective-permute-done.17
  166.1 3.0 fusion.135
  171.4 3.0 copy.343
  178.7 6.8 collective-permute-done.21
  187.4 8.4 collective-permute-done.23
  209.1 3.9 fusion.12
  239.9 3.4 collective-permute-done.29
  249.0 4.5 collective-permute-done.31
  267.3 18.0 %collective-permute-done.34 = bf16[2,2,2,128,512]{4,3,2,1,0:T(8,128)(2,1)} collective-permute-done((bf16[2,2,2,128,512]{4,3,2,1,0:T(8,128)(2,1)}, bf16[2,2,2,128,512]{4,3,2,1,0:T(8,128)(2,1)}, u32[]{:S(2)}, u32[]{:S(2)}) %collective-permute-start.34) | collective-permute-done | bytes 1048608 | tf_op jit(solution)/shard_map/ppermute | solution.py:369
  298.6 4.3 collective-permute-start.37
  330.2 4.7 collective-permute-done.41
  335.0 3.4 collective-permute-done.40
  343.5 8.9 %collective-permute-done.44 = bf16[4,32,2048]{2,1,0:T(8,128)(2,1)S(1)} collective-permute-done((bf16[4,32,2048]{2,1,0:T(8,128)(2,1)S(1)}, bf16[4,32,2048]{2,1,0:T(8,128)(2,1)S(1)}, u32[]{:S(2)}, u32[]{:S(2)}) %collective-permute-start.44) | collective-permute-done | bytes 524320 | tf_op jit(solution)/shard_map/ppermute | solution.py:369
  353.5 4.0 collective-permute-done.42
  363.5 29.5 %shard_map.306 = (bf16[384,2048]{1,0:T(8,128)(2,1)}, bf16[384,2048]{1,0:T(8,128)(2,1)}, bf16[256,2048]{1,0:T(8,128)(2,1)}, f32[1024,128]{1,0:T(8,128)}, bf16[102...) custom-call(bf16[384,2048]{1,0:T(8,128)(2,1)} %bitcast.87.refs_0_, ...), custom_call_target="tpu_custom_call" | custom-call | flops 20937965568 | bytes 45613056 | tf_op jit(solution)/shard_map/pallas_call | solution.py:237
  399.4 29.9 %shard_map.307 = (bf16[384,2048]{1,0:T(8,128)(2,1)}, bf16[384,2048]{1,0:T(8,128)(2,1)}, bf16[256,2048]{1,0:T(8,128)(2,1)}, f32[1024,128]{1,0:T(8,128)}, bf16[102...) custom-call(bf16[384,2048]{1,0:T(8,128)(2,1)} %bitcast.94.refs_0_.refs_3_, ...), custom_call_target="tpu_custom_call" | custom-call | flops 20937965568 | bytes 45613056 | tf_op jit(solution)/shard_map/pallas_call | solution.py:237
  433.9 34.7 %shard_map.308 = (bf16[384,2048]{1,0:T(8,128)(2,1)}, bf16[384,2048]{1,0:T(8,128)(2,1)}, bf16[256,2048]{1,0:T(8,128)(2,1)}, bf16[1024,1664]{1,0:T(8,128)(2,1)}, bf16[1024,1664]{1,0:T(8,128)(2,1)}) custom-call(bf16[384,2048]{1,0:T(8,128)(2,1)} %bitcast.100.refs_0_.refs_3_, bf16[384,2048]{1,0:T(8,128)(2,1)} %bitcast.101.refs_1_.refs_4_, ...), custom_call_target="tpu_custom_call" | custom-call | flops 20937965568 | bytes 45613056 | tf_op jit(solution)/shard_map/pallas_call | solution.py:237
  471.8 35.4 %shard_map.309 = (bf16[384,2048]{1,0:T(8,128)(2,1)}, bf16[384,2048]{1,0:T(8,128)(2,1)}, bf16[256,2048]{1,0:T(8,128)(2,1)}, bf16[1024,1664]{1,0:T(8,128)(2,1)}, bf16[1024,1664]{1,0:T(8,128)(2,1)}) custom-call(bf16[384,2048]{1,0:T(8,128)(2,1)} %bitcast.479, bf16[384,2048]{1,0:T(8,128)(2,1)} %bitcast.481, bf16[256,2048]{1,0:T(8,128)(2,1)} %bitcast.490, ...), custom_call_target="tpu_custom_call" | custom-call | flops 20937965568 | bytes 45613056 | tf_op jit(solution)/shard_map/pallas_call | solution.py:237
  519.9 5.5 collective-permute-done.59
  525.6 4.6 collective-permute-done.57
  530.5 3.5 collective-permute-done.58
  542.2 5.3 collective-permute-done.60
  549.4 2.9 collective-permute-start.63
  552.3 25.0 %shard_map.310 = (bf16[1408,2048]{1,0:T(8,128)(2,1)}, f32[256,2048]{1,0:T(8,128)}) custom-call(bf16[1024,1664]{1,0:T(8,128)(2,1)} %get-tuple-element.692.hidden_first, bf16[1024,1664]{1,0:T(8,128)(2,1)} %get-tuple-element.693.hidden_last, bf16[384,2048]{1,0:T(8,128)(2,1)} %bitcast.480, bf16[384,2048]{1,0:T(8,128)(2,1)} %bitcast.482, ...), custom_call_target="tpu_custom_call" | custom-call | flops 13958643712 | bytes 22020096 | tf_op jit(solution)/shard_map/pallas_call | solution.py:336
  593.3 4.0 collective-permute-done.66
  600.0 5.1 collective-permute-done.64
  627.5 14.9 %collective-permute-done.73 = bf16[1024,512]{1,0:T(8,128)(2,1)S(1)} collective-permute-done((bf16[1024,512]{1,0:T(8,128)(2,1)S(1)}, bf16[1024,512]{1,0:T(8,128)(2,1)S(1)}, u32[]{:S(2)}, u32[]{:S(2)}) %collective-permute-start.73) | collective-permute-done | bytes 1048608 | tf_op jit(solution)/shard_map/ppermute | solution.py:369
  650.6 22.0 %shard_map.311 = (bf16[2048,1408]{1,0:T(8,128)(2,1)}, bf16[2048,256]{1,0:T(8,128)(2,1)}) custom-call(bf16[384,2048]{1,0:T(8,128)(2,1)} %bitcast.87.refs_0_, bf16[384,2048]{1,0:T(8,128)(2,1)} %bitcast.88.refs_1_, bf16[256,2048]{1,0:T(8,128)(2,1)} %bitcast.89.refs_2_, bf16[384,2048]{1,0:T(8,128)(2,1)} %bitcast.94.refs_0_.refs_3_, ...), custom_call_target="tpu_custom_call" | custom-call | flops 13958643712 | bytes 22020096 | tf_op jit(solution)/shard_map/pallas_call | solution.py:298
  693.6 23.5 %shard_map.312 = (bf16[2048,1408]{1,0:T(8,128)(2,1)}, bf16[2048,256]{1,0:T(8,128)(2,1)}) custom-call(bf16[384,2048]{1,0:T(8,128)(2,1)} %bitcast.87.refs_0_, bf16[384,2048]{1,0:T(8,128)(2,1)} %bitcast.88.refs_1_, bf16[256,2048]{1,0:T(8,128)(2,1)} %bitcast.89.refs_2_, bf16[384,2048]{1,0:T(8,128)(2,1)} %bitcast.94.refs_0_.refs_3_, ...), custom_call_target="tpu_custom_call" | custom-call | flops 13958643712 | bytes 22020096 | tf_op jit(solution)/shard_map/pallas_call | solution.py:298
  717.1 5.2 bitcast_convert_fusion.2
  762.9 4.8 collective-permute-done.86
  774.3 4.5 all-to-all-start.1
  784.5 12.1 %collective-permute-done.93 = bf16[2,64,576]{2,1,0:T(8,128)(2,1)S(1)} collective-permute-done((bf16[2,64,576]{2,1,0:T(8,128)(2,1)}, bf16[2,64,576]{2,1,0:T(8,128)(2,1)S(1)}, u32[]{:S(2)}, u32[]{:S(2)}) %collective-permute-start.93) | collective-permute-done | bytes 147488 | tf_op jit(solution)/shard_map/ppermute | solution.py:369
  797.3 3.8 collective-permute-done.92
  809.2 5.8 all-to-all-start.2
  820.9 4.7 bitcast_convert_fusion
  825.6 4.1 reshape.699
  (914 shorter events, 397.0 us)
Async XLA Ops:
  24.8 24.0 %collective-permute-start.5 = (bf16[128,768]{1,0:T(8,128)(2,1)}, bf16[128,768]{1,0:T(8,128)(2,1)}, u32[]{:S(2)}, u32[]{:S(2)}) collective-permute-start(bf16[128,768]{1,0:T(8,128)(2,1)} %get-tuple-element.430), channel_id=1, source_target_pairs={{0,16},{1,17},{2,18},{3,19},{4,20},{5,21},{6,22},{7,23},{8,24},{9,... | collective-permute-start | bytes 589832 | tf_op jit(solution)/shard_map/ppermute | solution.py:369
  27.7 25.1 %collective-permute-start.6 = (bf16[128,768]{1,0:T(8,128)(2,1)}, bf16[128,768]{1,0:T(8,128)(2,1)}, u32[]{:S(2)}, u32[]{:S(2)}) collective-permute-start(bf16[128,768]{1,0:T(8,128)(2,1)} %get-tuple-element.431), channel_id=1, source_target_pairs={{0,16},{1,17},{2,18},{3,19},{4,20},{5,21},{6,22},{7,23},{8,24},{9,... | collective-permute-start | bytes 589832 | tf_op jit(solution)/shard_map/ppermute | solution.py:369
  93.2 23.5 %collective-permute-start.20 = (bf16[2,2,2,70,576]{4,2,3,1,0:T(2,128)(2,1)}, bf16[2,2,2,70,576]{4,2,3,1,0:T(2,128)(2,1)}, u32[]{:S(2)}, u32[]{:S(2)}) collective-permute-start(bf16[2,2,2,70,576]{4,2,3,1,0:T(2,128)(2,1)} %copy.338), channel_id=1, source_target_pairs={{0,8},{1,9},{2,10},{3,11},{4,12},{5,13},{6,14},{7,15},{8,0},{9,1},... | collective-permute-start | bytes 1935368 | tf_op jit(solution)/shard_map/ppermute | solution.py:369
  94.2 46.6 %collective-permute-start.19 = (bf16[2,2,2,32,2048]{4,3,2,1,0:T(8,128)(2,1)}, bf16[2,2,2,32,2048]{4,3,2,1,0:T(8,128)(2,1)}, u32[]{:S(2)}, u32[]{:S(2)}) collective-permute-start(bf16[2,2,2,32,2048]{4,3,2,1,0:T(8,128)(2,1)} %pad_maximum_fusion.18), channel_id=1, source_target_pairs={{0,8},{1,9},{2,10},{3,11},{4,12},{5,13},{6,14},{7,15},{8,0},{9,1},... | collective-permute-start | bytes 3145736 | tf_op jit(solution)/shard_map/ppermute | solution.py:369
  95.2 48.5 %collective-permute-start.18 = (bf16[2,2,2,128,768]{4,3,0,2,1:T(8,128)(2,1)}, bf16[2,2,2,128,768]{4,3,0,2,1:T(8,128)(2,1)}, u32[]{:S(2)}, u32[]{:S(2)}) collective-permute-start(bf16[2,2,2,128,768]{4,3,0,2,1:T(8,128)(2,1)} %pad_maximum_fusion.9), channel_id=1, source_target_pairs={{0,2},{1,3},{2,0},{3,1},{4,6},{5,7},{6,4},{7,5},{8,10},{9,11},{10,... | collective-permute-start | bytes 4718600 | tf_op jit(solution)/shard_map/ppermute | solution.py:369
  96.7 58.7 %all-to-all-start = ((bf16[16,64,352]{2,1,0:T(8,128)(2,1)}), bf16[16,64,352]{2,1,0:T(8,128)(2,1)}, u32[]{:S(2)}, u32[]{:S(2)}) async-start(bf16[16,64,352]{2,1,0:T(8,128)(2,1)} %bitcast.472), calls=%async_computation | async-start | bytes 1572864 | tf_op jit(solution)/shard_map/all_to_all | solution.py:585
  102.9 96.4 %all-gather.8.cloned.1.call-start = ((), (), s32[]{:S(2)}) async-start(), calls=%async_computation.6 | async-start | bytes 2359296 | tf_op jit(solution)/shard_map/all_gather | solution.py:624
  114.4 38.8 %collective-permute-start.17 = (bf16[2,2,2,128,768]{4,3,2,1,0:T(8,128)(2,1)}, bf16[2,2,2,128,768]{4,3,2,1,0:T(8,128)(2,1)S(1)}, u32[]{:S(2)}, u32[]{:S(2)}) collective-permute-start(bf16[2,2,2,128,768]{4,3,2,1,0:T(8,128)(2,1)} %pad_maximum_fusion.8), channel_id=1, source_target_pairs={{0,4},{1,5},{2,6},{3,7},{4,0},{5,1},{6,2},{7,3},{8,12},{9,13},{10,... | collective-permute-start | bytes 4718600 | tf_op jit(solution)/shard_map/ppermute | solution.py:369
  155.4 171.2 %all-gather.10.cloned.1.call-start = ((), (), s32[]{:S(2)}) async-start(), calls=%async_computation.10 | async-start | bytes 8650752 | tf_op jit(solution)/shard_map/all_gather | solution.py:613
  156.2 170.4 %all-gather.12.cloned.1.call-start = ((), (), s32[]{:S(2)}) async-start(), calls=%async_computation.11 | async-start | bytes 8650752 | tf_op jit(solution)/shard_map/all_gather | solution.py:613
  156.9 169.7 %all-gather.14.cloned.1.call-start = ((), (), s32[]{:S(2)}) async-start(), calls=%async_computation.12 | async-start | bytes 8650752 | tf_op jit(solution)/shard_map/all_gather | solution.py:613
  162.3 23.2 %collective-permute-start.21 = (bf16[128,1024]{1,0:T(8,128)(2,1)}, bf16[128,1024]{1,0:T(8,128)(2,1)}, u32[]{:S(2)}, u32[]{:S(2)}) collective-permute-start(bf16[128,1024]{1,0:T(8,128)(2,1)} %pad_maximum_fusion.56), channel_id=1, source_target_pairs={{0,16},{1,17},{2,18},{3,19},{4,20},{5,21},{6,22},{7,23},{8,24},{9,... | collective-permute-start | bytes 786440 | tf_op jit(solution)/shard_map/ppermute | solution.py:369
  164.8 31.1 %collective-permute-start.23 = (bf16[128,2048]{1,0:T(8,128)(2,1)}, bf16[128,2048]{1,0:T(8,128)(2,1)}, u32[]{:S(2)}, u32[]{:S(2)}) collective-permute-start(bf16[128,2048]{1,0:T(8,128)(2,1)} %param.36), channel_id=1, source_target_pairs={{0,16},{1,17},{2,18},{3,19},{4,20},{5,21},{6,22},{7,23},{8,24},{9,... | collective-permute-start | bytes 1572872 | tf_op jit(solution)/shard_map/ppermute | solution.py:369
  232.4 25.3 %collective-permute-start.32 = (bf16[4,48,2048]{2,1,0:T(8,128)(2,1)}, bf16[4,48,2048]{2,1,0:T(8,128)(2,1)}, u32[]{:S(2)}, u32[]{:S(2)}) collective-permute-start(bf16[4,48,2048]{2,1,0:T(8,128)(2,1)} %pad_maximum_fusion.27), channel_id=1, source_target_pairs={{0,8},{1,9},{2,10},{3,11},{4,12},{5,13},{6,14},{7,15},{8,0},{9,1},... | collective-permute-start | bytes 2359304 | tf_op jit(solution)/shard_map/ppermute | solution.py:369
  262.2 23.1 %collective-permute-start.34 = (bf16[2,2,2,128,512]{4,3,2,1,0:T(8,128)(2,1)}, bf16[2,2,2,128,512]{4,3,2,1,0:T(8,128)(2,1)}, u32[]{:S(2)}, u32[]{:S(2)}) collective-permute-start(bf16[2,2,2,128,512]{4,3,2,1,0:T(8,128)(2,1)} %pad_maximum_fusion.19), channel_id=1, source_target_pairs={{0,8},{1,9},{2,10},{3,11},{4,12},{5,13},{6,14},{7,15},{8,0},{9,1},... | collective-permute-start | bytes 3145736 | tf_op jit(solution)/shard_map/ppermute | solution.py:369
  291.8 317.1 %reduce-scatter.4.cloned.1.call-start = ((), (), s32[]{:S(2)}) async-start(), calls=%async_computation.7 | async-start | bytes 8650752 | tf_op jit(solution)/shard_map/reduce_scatter | solution.py:875
  298.3 26.9 %collective-permute-start.38 = (bf16[88,2048]{1,0:T(8,128)(2,1)S(1)}, bf16[88,2048]{1,0:T(8,128)(2,1)S(1)}, u32[]{:S(2)}, u32[]{:S(2)}) collective-permute-start(bf16[88,2048]{1,0:T(8,128)(2,1)S(1)} %copy-done.137), channel_id=1, source_target_pairs={{0,1},{1,0},{2,3},{3,2},{4,5},{5,4},{6,7},{7,6},{8,9},{9,8},{10,11... | collective-permute-start | bytes 1081352 | tf_op jit(solution)/shard_map/ppermute | solution.py:372
  298.6 27.9 %collective-permute-start.37 = (bf16[128,2048]{1,0:T(8,128)(2,1)S(1)}, bf16[128,2048]{1,0:T(8,128)(2,1)S(1)}, u32[]{:S(2)}, u32[]{:S(2)}) collective-permute-start(bf16[128,2048]{1,0:T(8,128)(2,1)S(1)} %multiply_convert_fusion.1), channel_id=1, source_target_pairs={{0,16},{1,17},{2,18},{3,19},{4,20},{5,21},{6,22},{7,23},{8,24},{9,... | collective-permute-start | bytes 1572872 | tf_op jit(solution)/shard_map/ppermute | solution.py:369
  360.5 32.4 %collective-permute-start.47 = (bf16[8,32,2048]{2,1,0:T(8,128)(2,1)}, bf16[8,32,2048]{2,1,0:T(8,128)(2,1)}, u32[]{:S(2)}, u32[]{:S(2)}) collective-permute-start(bf16[8,32,2048]{2,1,0:T(8,128)(2,1)} %pad_maximum_fusion.23), channel_id=1, source_target_pairs={{0,2},{1,3},{2,0},{3,1},{4,6},{5,7},{6,4},{7,5},{8,10},{9,11},{10,... | collective-permute-start | bytes 3145736 | tf_op jit(solution)/shard_map/ppermute | solution.py:369
  361.8 33.9 %collective-permute-start.45 = (bf16[8,48,2048]{2,1,0:T(8,128)(2,1)}, bf16[8,48,2048]{2,1,0:T(8,128)(2,1)}, u32[]{:S(2)}, u32[]{:S(2)}) collective-permute-start(bf16[8,48,2048]{2,1,0:T(8,128)(2,1)} %pad_maximum_fusion.13), channel_id=1, source_target_pairs={{0,8},{1,9},{2,10},{3,11},{4,12},{5,13},{6,14},{7,15},{8,0},{9,1},... | collective-permute-start | bytes 4718600 | tf_op jit(solution)/shard_map/ppermute | solution.py:369
  362.3 33.3 %collective-permute-start.46 = (bf16[8,48,2048]{2,1,0:T(8,128)(2,1)}, bf16[8,48,2048]{2,1,0:T(8,128)(2,1)}, u32[]{:S(2)}, u32[]{:S(2)}) collective-permute-start(bf16[8,48,2048]{2,1,0:T(8,128)(2,1)} %pad_maximum_fusion.14), channel_id=1, source_target_pairs={{0,4},{1,5},{2,6},{3,7},{4,0},{5,1},{6,2},{7,3},{8,12},{9,13},{10,... | collective-permute-start | bytes 4718600 | tf_op jit(solution)/shard_map/ppermute | solution.py:369
  395.6 33.7 %collective-permute-start.50 = (bf16[8,32,2048]{2,1,0:T(8,128)(2,1)}, bf16[8,32,2048]{2,1,0:T(8,128)(2,1)}, u32[]{:S(2)}, u32[]{:S(2)}) collective-permute-start(bf16[8,32,2048]{2,1,0:T(8,128)(2,1)} %pad_maximum_fusion.22), channel_id=1, source_target_pairs={{0,2},{1,3},{2,0},{3,1},{4,6},{5,7},{6,4},{7,5},{8,10},{9,11},{10,... | collective-permute-start | bytes 3145736 | tf_op jit(solution)/shard_map/ppermute | solution.py:369
  396.8 32.9 %collective-permute-start.48 = (bf16[8,48,2048]{2,1,0:T(8,128)(2,1)S(1)}, bf16[8,48,2048]{2,1,0:T(8,128)(2,1)}, u32[]{:S(2)}, u32[]{:S(2)}) collective-permute-start(bf16[8,48,2048]{2,1,0:T(8,128)(2,1)S(1)} %copy-done.108), channel_id=1, source_target_pairs={{0,8},{1,9},{2,10},{3,11},{4,12},{5,13},{6,14},{7,15},{8,0},{9,1},... | collective-permute-start | bytes 4718600 | tf_op jit(solution)/shard_map/ppermute | solution.py:369
  397.9 33.0 %collective-permute-start.49 = (bf16[8,48,2048]{2,1,0:T(8,128)(2,1)}, bf16[8,48,2048]{2,1,0:T(8,128)(2,1)}, u32[]{:S(2)}, u32[]{:S(2)}) collective-permute-start(bf16[8,48,2048]{2,1,0:T(8,128)(2,1)} %pad_maximum_fusion.12), channel_id=1, source_target_pairs={{0,4},{1,5},{2,6},{3,7},{4,0},{5,1},{6,2},{7,3},{8,12},{9,13},{10,... | collective-permute-start | bytes 4718600 | tf_op jit(solution)/shard_map/ppermute | solution.py:369
  430.9 37.8 %collective-permute-start.53 = (bf16[8,32,2048]{2,1,0:T(8,128)(2,1)}, bf16[8,32,2048]{2,1,0:T(8,128)(2,1)}, u32[]{:S(2)}, u32[]{:S(2)}) collective-permute-start(bf16[8,32,2048]{2,1,0:T(8,128)(2,1)} %bitcast.511), channel_id=1, source_target_pairs={{0,2},{1,3},{2,0},{3,1},{4,6},{5,7},{6,4},{7,5},{8,10},{9,11},{10,... | collective-permute-start | bytes 3145736 | tf_op jit(solution)/shard_map/ppermute | solution.py:369
  431.7 37.0 %collective-permute-start.51 = (bf16[8,48,2048]{2,1,0:T(8,128)(2,1)}, bf16[8,48,2048]{2,1,0:T(8,128)(2,1)S(1)}, u32[]{:S(2)}, u32[]{:S(2)}) collective-permute-start(bf16[8,48,2048]{2,1,0:T(8,128)(2,1)} %bitcast.509), channel_id=1, source_target_pairs={{0,8},{1,9},{2,10},{3,11},{4,12},{5,13},{6,14},{7,15},{8,0},{9,1},... | collective-permute-start | bytes 4718600 | tf_op jit(solution)/shard_map/ppermute | solution.py:369
  432.0 36.7 %collective-permute-start.52 = (bf16[8,48,2048]{2,1,0:T(8,128)(2,1)}, bf16[8,48,2048]{2,1,0:T(8,128)(2,1)}, u32[]{:S(2)}, u32[]{:S(2)}) collective-permute-start(bf16[8,48,2048]{2,1,0:T(8,128)(2,1)} %bitcast.508), channel_id=1, source_target_pairs={{0,4},{1,5},{2,6},{3,7},{4,0},{5,1},{6,2},{7,3},{8,12},{9,13},{10,... | collective-permute-start | bytes 4718600 | tf_op jit(solution)/shard_map/ppermute | solution.py:369
  468.7 40.7 %collective-permute-start.56 = (bf16[8,32,2048]{2,1,0:T(8,128)(2,1)}, bf16[8,32,2048]{2,1,0:T(8,128)(2,1)}, u32[]{:S(2)}, u32[]{:S(2)}) collective-permute-start(bf16[8,32,2048]{2,1,0:T(8,128)(2,1)} %bitcast.510), channel_id=1, source_target_pairs={{0,2},{1,3},{2,0},{3,1},{4,6},{5,7},{6,4},{7,5},{8,10},{9,11},{10,... | collective-permute-start | bytes 3145736 | tf_op jit(solution)/shard_map/ppermute | solution.py:369
  469.8 39.5 %collective-permute-start.54 = (bf16[8,48,2048]{2,1,0:T(8,128)(2,1)}, bf16[8,48,2048]{2,1,0:T(8,128)(2,1)}, u32[]{:S(2)}, u32[]{:S(2)}) collective-permute-start(bf16[8,48,2048]{2,1,0:T(8,128)(2,1)} %bitcast.507), channel_id=1, source_target_pairs={{0,8},{1,9},{2,10},{3,11},{4,12},{5,13},{6,14},{7,15},{8,0},{9,1},... | collective-permute-start | bytes 4718600 | tf_op jit(solution)/shard_map/ppermute | solution.py:369
  471.8 37.6 %collective-permute-start.55 = (bf16[8,48,2048]{2,1,0:T(8,128)(2,1)}, bf16[8,48,2048]{2,1,0:T(8,128)(2,1)}, u32[]{:S(2)}, u32[]{:S(2)}) collective-permute-start(bf16[8,48,2048]{2,1,0:T(8,128)(2,1)} %bitcast.506), channel_id=1, source_target_pairs={{0,4},{1,5},{2,6},{3,7},{4,0},{5,1},{6,2},{7,3},{8,12},{9,13},{10,... | collective-permute-start | bytes 4718600 | tf_op jit(solution)/shard_map/ppermute | solution.py:369
  549.4 28.0 %collective-permute-start.63 = (bf16[128,2048]{1,0:T(8,128)(2,1)S(1)}, bf16[128,2048]{1,0:T(8,128)(2,1)S(1)}, u32[]{:S(2)}, u32[]{:S(2)}) collective-permute-start(bf16[128,2048]{1,0:T(8,128)(2,1)S(1)} %fusion.40), channel_id=1, source_target_pairs={{0,16},{1,17},{2,18},{3,19},{4,20},{5,21},{6,22},{7,23},{8,24},{9,... | collective-permute-start | bytes 1572872 | tf_op jit(solution)/shard_map/ppermute | solution.py:369
  578.8 160.9 %reduce-scatter.6.cloned.1.call-start = ((), (), s32[]{:S(2)}) async-start(), calls=%async_computation.8 | async-start | bytes 8650752 | tf_op jit(solution)/shard_map/reduce_scatter | solution.py:859
  618.2 24.2 %collective-permute-start.73 = (bf16[1024,512]{1,0:T(8,128)(2,1)S(1)}, bf16[1024,512]{1,0:T(8,128)(2,1)S(1)}, u32[]{:S(2)}, u32[]{:S(2)}) collective-permute-start(bf16[1024,512]{1,0:T(8,128)(2,1)S(1)} %copy-done.122), channel_id=1, source_target_pairs={{0,8},{1,9},{2,10},{3,11},{4,12},{5,13},{6,14},{7,15},{8,0},{9,1},... | collective-permute-start | bytes 3145736 | tf_op jit(solution)/shard_map/ppermute | solution.py:369
  620.1 23.7 %collective-permute-start.74 = (bf16[1024,512]{1,0:T(8,128)(2,1)S(1)}, bf16[1024,512]{1,0:T(8,128)(2,1)S(1)}, u32[]{:S(2)}, u32[]{:S(2)}) collective-permute-start(bf16[1024,512]{1,0:T(8,128)(2,1)S(1)} %copy-done.121), channel_id=1, source_target_pairs={{0,4},{1,5},{2,6},{3,7},{4,0},{5,1},{6,2},{7,3},{8,12},{9,13},{10,... | collective-permute-start | bytes 3145736 | tf_op jit(solution)/shard_map/ppermute | solution.py:369
  645.3 28.8 %collective-permute-start.76 = (bf16[2,2,128,512]{3,2,0,1:T(8,128)(2,1)S(1)}, bf16[2,2,128,512]{3,2,0,1:T(8,128)(2,1)}, u32[]{:S(2)}, u32[]{:S(2)}) collective-permute-start(bf16[2,2,128,512]{3,2,0,1:T(8,128)(2,1)S(1)} %select_bitcast_fusion.21), channel_id=1, source_target_pairs={{0,4},{1,5},{2,6},{3,7},{4,0},{5,1},{6,2},{7,3},{8,12},{9,13},{10,... | collective-permute-start | bytes 1572872 | tf_op jit(solution)/shard_map/ppermute | solution.py:369
  647.0 28.4 %collective-permute-start.77 = (bf16[2,2,128,512]{3,2,0,1:T(8,128)(2,1)}, bf16[2,2,128,512]{3,2,0,1:T(8,128)(2,1)}, u32[]{:S(2)}, u32[]{:S(2)}) collective-permute-start(bf16[2,2,128,512]{3,2,0,1:T(8,128)(2,1)} %select_bitcast_fusion.20), channel_id=1, source_target_pairs={{0,8},{1,9},{2,10},{3,11},{4,12},{5,13},{6,14},{7,15},{8,0},{9,1},... | collective-permute-start | bytes 1572872 | tf_op jit(solution)/shard_map/ppermute | solution.py:369
  647.9 30.6 %collective-permute-start.78 = (bf16[128,2048]{1,0:T(8,128)(2,1)}, bf16[128,2048]{1,0:T(8,128)(2,1)}, u32[]{:S(2)}, u32[]{:S(2)}) collective-permute-start(bf16[128,2048]{1,0:T(8,128)(2,1)} %fusion.41), channel_id=1, source_target_pairs={{0,16},{1,17},{2,18},{3,19},{4,20},{5,21},{6,22},{7,23},{8,24},{9,... | collective-permute-start | bytes 1572872 | tf_op jit(solution)/shard_map/ppermute | solution.py:369
  650.6 30.1 %collective-permute-start.75 = (f32[256,576]{0,1:T(8,128)}, f32[256,576]{0,1:T(8,128)}, u32[]{:S(2)}, u32[]{:S(2)}) collective-permute-start(f32[256,576]{0,1:T(8,128)} %pad_maximum_fusion.33), channel_id=1, source_target_pairs={{0,1},{1,0},{2,3},{3,2},{4,5},{5,4},{6,7},{7,6},{8,9},{9,8},{10,11... | collective-permute-start | bytes 1769480 | tf_op jit(solution)/shard_map/ppermute | solution.py:372
  688.5 119.6 %reduce-scatter.8.cloned.1.call-start = ((), (), s32[]{:S(2)}) async-start(), calls=%async_computation.9 | async-start | bytes 8650752 | tf_op jit(solution)/shard_map/reduce_scatter | solution.py:864
  688.5 33.7 %collective-permute-start.80 = (bf16[2,128,1024]{2,1,0:T(8,128)(2,1)}, bf16[2,128,1024]{2,1,0:T(8,128)(2,1)S(1)}, u32[]{:S(2)}, u32[]{:S(2)}) collective-permute-start(bf16[2,128,1024]{2,1,0:T(8,128)(2,1)} %select_bitcast_fusion.19), channel_id=1, source_target_pairs={{0,2},{1,3},{2,0},{3,1},{4,6},{5,7},{6,4},{7,5},{8,10},{9,11},{10,... | collective-permute-start | bytes 1572872 | tf_op jit(solution)/shard_map/ppermute | solution.py:369
  688.9 34.3 %collective-permute-start.83 = (bf16[512,576]{0,1:T(8,128)(2,1)}, bf16[512,576]{0,1:T(8,128)(2,1)}, u32[]{:S(2)}, u32[]{:S(2)}) collective-permute-start(bf16[512,576]{0,1:T(8,128)(2,1)} %convolution_convert_fusion.6), channel_id=1, source_target_pairs={{0,4},{1,5},{2,6},{3,7},{4,0},{5,1},{6,2},{7,3},{8,12},{9,13},{10,... | collective-permute-start | bytes 1769480 | tf_op jit(solution)/shard_map/ppermute | solution.py:369
  689.3 38.4 %collective-permute-start.82 = (bf16[256,2048]{1,0:T(8,128)(2,1)}, bf16[256,2048]{1,0:T(8,128)(2,1)}, u32[]{:S(2)}, u32[]{:S(2)}) collective-permute-start(bf16[256,2048]{1,0:T(8,128)(2,1)} %convolution_convert_fusion.1), channel_id=1, source_target_pairs={{0,4},{1,5},{2,6},{3,7},{4,0},{5,1},{6,2},{7,3},{8,12},{9,13},{10,... | collective-permute-start | bytes 3145736 | tf_op jit(solution)/shard_map/ppermute | solution.py:369
  691.0 40.3 %collective-permute-start.79 = (bf16[1024,640]{1,0:T(8,128)(2,1)}, bf16[1024,640]{1,0:T(8,128)(2,1)}, u32[]{:S(2)}, u32[]{:S(2)}) collective-permute-start(bf16[1024,640]{1,0:T(8,128)(2,1)} %convolution_convert_fusion.3), channel_id=1, source_target_pairs={{0,2},{1,3},{2,0},{3,1},{4,6},{5,7},{6,4},{7,5},{8,10},{9,11},{10,... | collective-permute-start | bytes 3932168 | tf_op jit(solution)/shard_map/ppermute | solution.py:369
  692.6 42.2 %collective-permute-start.81 = (bf16[1024,896]{1,0:T(8,128)(2,1)}, bf16[1024,896]{1,0:T(8,128)(2,1)}, u32[]{:S(2)}, u32[]{:S(2)}) collective-permute-start(bf16[1024,896]{1,0:T(8,128)(2,1)} %convolution_convert_fusion.2), channel_id=1, source_target_pairs={{0,8},{1,9},{2,10},{3,11},{4,12},{5,13},{6,14},{7,15},{8,0},{9,1},... | collective-permute-start | bytes 5505032 | tf_op jit(solution)/shard_map/ppermute | solution.py:369
  774.3 33.8 %all-to-all-start.1 = ((bf16[16,64,352]{2,1,0:T(8,128)(2,1)}), bf16[16,64,352]{2,1,0:T(8,128)(2,1)}, u32[]{:S(2)}, u32[]{:S(2)}) async-start(bf16[16,64,352]{2,1,0:T(8,128)(2,1)} %select_add_fusion), calls=%async_computation.3 | async-start | bytes 1572864 | tf_op jit(solution)/shard_map/all_to_all | solution.py:868
  809.2 35.3 %all-to-all-start.2 = ((f32[16,1,2336]{2,1,0:T(1,128)}), f32[16,1,2336]{2,1,0:T(1,128)}, u32[]{:S(2)}, u32[]{:S(2)}) async-start(f32[16,1,2336]{2,1,0:T(1,128)} %all_to_all.23), calls=%async_computation.5 | async-start | bytes 311296 | tf_op jit(solution)/shard_map/all_to_all | solution.py:962
  818.0 24.6 %collective-permute-start.96 = (bf16[128,640]{1,0:T(8,128)(2,1)}, bf16[128,640]{1,0:T(8,128)(2,1)}, u32[]{:S(2)}, u32[]{:S(2)}) collective-permute-start(bf16[128,640]{1,0:T(8,128)(2,1)} %select_bitcast_fusion.51), channel_id=1, source_target_pairs={{0,16},{1,17},{2,18},{3,19},{4,20},{5,21},{6,22},{7,23},{8,24},{9,... | collective-permute-start | bytes 491528 | tf_op jit(solution)/shard_map/ppermute | solution.py:369
  820.7 25.4 %collective-permute-start.97 = (bf16[128,896]{1,0:T(8,128)(2,1)}, bf16[128,896]{1,0:T(8,128)(2,1)}, u32[]{:S(2)}, u32[]{:S(2)}) collective-permute-start(bf16[128,896]{1,0:T(8,128)(2,1)} %select_bitcast_fusion.44), channel_id=1, source_target_pairs={{0,16},{1,17},{2,18},{3,19},{4,20},{5,21},{6,22},{7,23},{8,24},{9,... | collective-permute-start | bytes 688136 | tf_op jit(solution)/shard_map/ppermute | solution.py:369
  (228 other events, 1897.2 us)
Sparse Core Ops, SparseCore 0:
  155.5 10.8 all-gather.7
  167.9 17.1 all-gather.9
  186.7 17.1 all-gather.11
  291.9 17.9 all-gather.13
  578.9 13.2 reduce-scatter.3
  688.6 12.9 reduce-scatter.5
  739.8 12.8 reduce-scatter.7

commit v5 on v4

--- a/solution.py
+++ b/solution.py
@@ -276,9 +276,8 @@
 
 def in_weights_kernel(*refs):
     groups = 2 * len(TOKEN_GROUPS)
-    rows, (first, last), (out, extra_out), turned = (
-        refs[:groups], refs[groups : groups + 2], refs[groups + 2 : groups + 4], refs[-1],
-    )
+    rows, (first, last) = refs[:groups], refs[groups : groups + 2]
+    out, extra_out, turned = refs[-3:]
     for ref, here in row_groups(rows):
         turned[:, here] = ref[...].T
     tokens = first.shape[0]
@@ -290,25 +289,33 @@
             ref[:, pl.ds(start, size)] = value.astype(ref.dtype)
 
 
-def in_weights(rows, acts_back, ff):
+def in_weights(rows, acts_back, ff, part, earlier=()):
     tokens, units = acts_back[0].shape
     width = rows[0].shape[1]
+    first_step, steps = 0, width // WIDE
+    if part is not None:
+        steps = steps // 2
+        first_step = part * steps
     whole = pl.BlockSpec((tokens, units), lambda i: (0, 0), pipeline_mode=pl.Buffered(1))
     outs = [((width, ff), BF16), ((width, units - ff), BF16)]
+    given = len(rows) + 2
     return pl.pallas_call(
         in_weights_kernel,
-        grid=(width // WIDE,),
+        grid=(steps,),
         out_shape=[jax.ShapeDtypeStruct(*out) for out in outs],
-        in_specs=[pl.BlockSpec((v.shape[0], WIDE), lambda i: (0, i)) for v in rows] + [whole] * 2,
-        out_specs=[pl.BlockSpec((WIDE, shape[1]), lambda i: (i, 0)) for shape, _ in outs],
+        in_specs=[pl.BlockSpec((v.shape[0], WIDE), lambda i: (0, i + first_step)) for v in rows]
+        + [whole] * 2
+        + [pl.BlockSpec(memory_space=pl.ANY) for _ in earlier],
+        out_specs=[pl.BlockSpec((WIDE, shape[1]), lambda i: (i + first_step, 0)) for shape, _ in outs],
         scratch_shapes=[pltpu.VMEM((WIDE, 2 * tokens), BF16)],
+        input_output_aliases={given + k: k for k in range(len(earlier))},
         compiler_params=pltpu.CompilerParams(vmem_limit_bytes=VMEM_BYTES),
         cost_estimate=pl.CostEstimate(
-            flops=4 * tokens * width * units,
-            bytes_accessed=4 * tokens * (width + units) + 2 * width * units,
+            flops=2 * tokens * width * units,
+            bytes_accessed=4 * tokens * (width + units) + width * units,
             transcendentals=0,
         ),
-    )(*rows, *acts_back)
+    )(*rows, *acts_back, *earlier)
 
 
 def down_weights_kernel(hidden_first, hidden_last, *refs):
@@ -817,14 +824,23 @@
         *chips.last_groups(back_last), beside(backward, kept_first, cot_first, members[0])
     )
 
-    def down_grads(hidden_acts, cots):
-        yield from idle(2)
+    def down_grads(hidden_acts, cots, rows, gate_back):
+        rows = [v for groups in rows for v in groups]
+        rows, gate_back = yield (rows, gate_back), None
+        gate_part = in_weights(rows, gate_back, ff, 0)
+        gate_part = yield gate_part, None
         hidden_acts, cots = yield (hidden_acts, cots), None
-        return down_weights(hidden_acts, [v for groups in cots for v in groups], ff)
-
-    *_, ffn_grad, (down_w, down_extra_w) = chips.lockstep(
+        down = down_weights(hidden_acts, [v for groups in cots for v in groups], ff)
+        return down, gate_part
+
+    *_, ffn_grad, ((down_w, down_extra_w), gate_part) = chips.lockstep(
         *chips.scatter_groups(back_first, sent_back, {}),
-        down_grads((kept_first[4], kept_last[4]), (grads_first[0], grads_last[0])),
+        down_grads(
+            (kept_first[4], kept_last[4]),
+            (grads_first[0], grads_last[0]),
+            (kept_first[0], kept_last[0]),
+            (grads_first[1], grads_last[1]),
+        ),
     )
 
     middle = {}
@@ -850,15 +866,15 @@
         value = jnp.concatenate([middle["output", 0], value], axis=-1)
         return (yield from chips.scatter_chips(value, BACK_OUTPUT[2], order))
 
-    def in_grads(rows, gate_back, up_back):
+    def in_grads(rows, gate_back, up_back, gate_part):
         rows = [v for groups in rows for v in groups]
         yield from idle(2)
-        rows, gate_back = yield (rows, gate_back), None
-        gate_w, gate_x = yield in_weights(rows, gate_back, ff), None
+        rows, gate_back, gate_part = yield (rows, gate_back, gate_part), None
+        gate_w, gate_x = yield in_weights(rows, gate_back, ff, 1, gate_part), None
         middle["router_grad"] = gate_x[:, width : width + expert_count]
         gate_w = lax.psum_scatter(gate_w, "fsdp", scatter_dimension=0, tiled=True)
         rows, up_back = together(rows, up_back, gate_x)[:2]
-        up_w, up_x = in_weights(rows, up_back, ff)
+        up_w, up_x = in_weights(rows, up_back, ff, None)
         gate_w, up_w, gate_x, up_x = yield (gate_w, up_w, gate_x, up_x), None
         gate_w = gate_w.astype(F32)[None]
         up_w = lax.psum_scatter(up_w, "fsdp", scatter_dimension=0, tiled=True)
@@ -982,6 +998,7 @@
             (kept_first[0], kept_last[0]),
             (grads_first[1], grads_last[1]),
             (grads_first[2], grads_last[2]),
+            gate_part,
         ),
         second_grads(down_w, down_extra_w),
         input_grads(),

time: 875 us -> 868 us (level)
  starting transfers between devices: 134 us -> 120 us
  waiting for transfers between devices: 209 us -> 197 us
    ppermute x84, waiting for transfers between devices: 207 us -> 195 us  [exchange(): return lax.ppermute(value, BOTH, pairs)]
    all_gather x1, starting transfers between devices: 11.5 us -> 0.22 us  [shared_weights(): lax.all_gather(value.reshape(n, 1, shard, 2 * width), 'fsdp', axis=1, til...]
    pallas_call x2 -> x3, Pallas kernels: 45.4 us -> 49.6 us  [in_weights(): pl.pallas_call(in_weights_kernel, grid=(steps,), out_shape=[jax.ShapeDtyp...]
    unnamed x328 -> x360, local copies, waits for them, and re-layouts: 18.9 us -> 20.9 us
  transfers between devices with their start and end apart: 114 -> 114, of which waited for: 50 -> 48; matrix products, arithmetic and copies ran while one was open for 30% -> 30% of each run, Pallas kernels for 23% -> 24%
where the time goes in v5:
time: 868 us; the launch traced here: 852 us
  Pallas kernels  204 us (24%)
  waiting for transfers between devices  197 us (23%)
  other arithmetic  177 us (20%)
  starting transfers between devices  120 us (14%)
  local copies, waits for them, and re-layouts  88.2 us (10%)
  matrix products  48.2 us (6%)
  between operations  17.6 us (2%)
    ppermute x84, waiting for transfers between devices, exchange(): return lax.ppermute(value, BOTH, pairs)  195 us
    pallas_call x4, Pallas kernels, expert_call(): pl.pallas_call(kernel, out_shape=out_shapes, in_specs=[whole_in_vmem() fo...  129 us
    ppermute x84, starting transfers between devices, exchange(): return lax.ppermute(value, BOTH, pairs)  99.7 us
    pallas_call x3, Pallas kernels, in_weights(): pl.pallas_call(in_weights_kernel, grid=(steps,), out_shape=[jax.ShapeDtyp...  49.6 us
    another operation x38, other arithmetic, gather_chips(): jnp.stack([jnp.where(high, other, value), jnp.where(high, value, other)],...  26.7 us
    pallas_call x1, Pallas kernels, down_weights(): pl.pallas_call(down_weights_kernel, grid=(width // WIDE,), out_shape=[jax...  25 us
    unnamed x360, local copies, waits for them, and re-layouts  20.9 us
    dot_general x12, matrix products, inner_rows(): lax.dot_general(left_side, right_side, (((0,), (0,)), ((), ())), preferre...  18.6 us
  transfers between devices with their start and end apart: 114, of which 48 were waited for; matrix products, arithmetic and copies ran while one was open for 30% of the time, Pallas kernels for 24%

profile of v5, /device:TPU:0, one launch (start us, length us, event | category | flops | bytes accessed | tf_op | source)
XLA Modules:
  0.0 852.5 jit_solution(10475901013603119624)
XLA Ops:
  21.1 3.7 collective-permute-start.8
  24.8 2.9 collective-permute-start.5
  36.9 5.0 collective-permute-done.8
  48.8 4.0 collective-permute-done.6
  58.3 3.5 collective-permute-done.12
  61.9 4.4 collective-permute-done.11
  71.9 7.1 collective-permute-done.16
  79.2 8.2 collective-permute-done.15
  96.7 6.4 all-to-all-start
  105.3 11.4 %collective-permute-done.20 = bf16[2,2,2,70,576]{4,2,3,1,0:T(2,128)(2,1)} collective-permute-done((bf16[2,2,2,70,576]{4,2,3,1,0:T(2,128)(2,1)}, bf16[2,2,2,70,576]{4,2,3,1,0:T(2,128)(2,1)}, u32[]{:S(2)}, u32[]{:S(2)}) %collective-permute-start.20) | collective-permute-done | bytes 645152 | tf_op jit(solution)/shard_map/ppermute | solution.py:376
  119.8 21.0 %collective-permute-done.19 = bf16[2,2,2,32,2048]{4,3,2,1,0:T(8,128)(2,1)} collective-permute-done((bf16[2,2,2,32,2048]{4,3,2,1,0:T(8,128)(2,1)}, bf16[2,2,2,32,2048]{4,3,2,1,0:T(8,128)(2,1)}, u32[]{:S(2)}, u32[]{:S(2)}) %collective-permute-start.19) | collective-permute-done | bytes 1048608 | tf_op jit(solution)/shard_map/ppermute | solution.py:376
  156.6 3.0 collective-permute-start.21
  161.4 3.0 fusion.135
  166.8 3.0 copy.345
  175.0 3.5 collective-permute-done.21
  180.6 8.5 collective-permute-done.23
  202.4 4.0 fusion.12
  228.3 3.7 collective-permute-done.28
  233.3 3.0 collective-permute-done.29
  242.0 5.0 collective-permute-done.31
  259.6 17.7 %collective-permute-done.34 = bf16[2,2,2,128,512]{4,3,2,1,0:T(8,128)(2,1)} collective-permute-done((bf16[2,2,2,128,512]{4,3,2,1,0:T(8,128)(2,1)}, bf16[2,2,2,128,512]{4,3,2,1,0:T(8,128)(2,1)}, u32[]{:S(2)}, u32[]{:S(2)}) %collective-permute-start.34) | collective-permute-done | bytes 1048608 | tf_op jit(solution)/shard_map/ppermute | solution.py:376
  321.6 4.8 collective-permute-done.41
  326.5 3.4 collective-permute-done.40
  335.0 8.8 %collective-permute-done.44 = bf16[4,32,2048]{2,1,0:T(8,128)(2,1)S(1)} collective-permute-done((bf16[4,32,2048]{2,1,0:T(8,128)(2,1)S(1)}, bf16[4,32,2048]{2,1,0:T(8,128)(2,1)S(1)}, u32[]{:S(2)}, u32[]{:S(2)}) %collective-permute-start.44) | collective-permute-done | bytes 524320 | tf_op jit(solution)/shard_map/ppermute | solution.py:376
  344.9 4.0 collective-permute-done.42
  355.0 29.5 %shard_map.306 = (bf16[384,2048]{1,0:T(8,128)(2,1)}, bf16[384,2048]{1,0:T(8,128)(2,1)}, bf16[256,2048]{1,0:T(8,128)(2,1)}, f32[1024,128]{1,0:T(8,128)}, bf16[102...) custom-call(bf16[384,2048]{1,0:T(8,128)(2,1)} %bitcast.87.refs_0_, ...), custom_call_target="tpu_custom_call" | custom-call | flops 20937965568 | bytes 45613056 | tf_op jit(solution)/shard_map/pallas_call | solution.py:237
  390.8 29.9 %shard_map.307 = (bf16[384,2048]{1,0:T(8,128)(2,1)}, bf16[384,2048]{1,0:T(8,128)(2,1)}, bf16[256,2048]{1,0:T(8,128)(2,1)}, f32[1024,128]{1,0:T(8,128)}, bf16[102...) custom-call(bf16[384,2048]{1,0:T(8,128)(2,1)} %bitcast.94.refs_0_.refs_3_, ...), custom_call_target="tpu_custom_call" | custom-call | flops 20937965568 | bytes 45613056 | tf_op jit(solution)/shard_map/pallas_call | solution.py:237
  425.8 34.8 %shard_map.308 = (bf16[384,2048]{1,0:T(8,128)(2,1)}, bf16[384,2048]{1,0:T(8,128)(2,1)}, bf16[256,2048]{1,0:T(8,128)(2,1)}, bf16[1024,1664]{1,0:T(8,128)(2,1)}, bf16[1024,1664]{1,0:T(8,128)(2,1)}) custom-call(bf16[384,2048]{1,0:T(8,128)(2,1)} %bitcast.100.refs_0_.refs_3_, bf16[384,2048]{1,0:T(8,128)(2,1)} %bitcast.101.refs_1_.refs_4_, ...), custom_call_target="tpu_custom_call" | custom-call | flops 20937965568 | bytes 45613056 | tf_op jit(solution)/shard_map/pallas_call | solution.py:237
  463.0 35.3 %shard_map.309 = (bf16[384,2048]{1,0:T(8,128)(2,1)}, bf16[384,2048]{1,0:T(8,128)(2,1)}, bf16[256,2048]{1,0:T(8,128)(2,1)}, bf16[1024,1664]{1,0:T(8,128)(2,1)}, bf16[1024,1664]{1,0:T(8,128)(2,1)}) custom-call(bf16[384,2048]{1,0:T(8,128)(2,1)} %bitcast.479, bf16[384,2048]{1,0:T(8,128)(2,1)} %bitcast.481, bf16[256,2048]{1,0:T(8,128)(2,1)} %bitcast.490, ...), custom_call_target="tpu_custom_call" | custom-call | flops 20937965568 | bytes 45613056 | tf_op jit(solution)/shard_map/pallas_call | solution.py:237
  517.2 13.6 %shard_map.310 = (bf16[2048,1408]{1,0:T(8,128)(2,1)}, bf16[2048,256]{1,0:T(8,128)(2,1)}) custom-call(bf16[384,2048]{1,0:T(8,128)(2,1)} %bitcast.87.refs_0_, bf16[384,2048]{1,0:T(8,128)(2,1)} %bitcast.88.refs_1_, bf16[256,2048]{1,0:T(8,128)(2,1)} %bitcast.89.refs_2_, bf16[384,2048]{1,0:T(8,128)(2,1)} %bitcast.94.refs_0_.refs_3_, ...), custom_call_target="tpu_custom_call" | custom-call | flops 6979321856 | bytes 18612224 | tf_op jit(solution)/shard_map/pallas_call | solution.py:302
  542.0 4.7 collective-permute-done.60
  549.7 25.0 %shard_map.311 = (bf16[1408,2048]{1,0:T(8,128)(2,1)}, f32[256,2048]{1,0:T(8,128)}) custom-call(bf16[1024,1664]{1,0:T(8,128)(2,1)} %get-tuple-element.720.hidden_first, bf16[1024,1664]{1,0:T(8,128)(2,1)} %get-tuple-element.721.hidden_last, bf16[384,2048]{1,0:T(8,128)(2,1)} %bitcast.480, bf16[384,2048]{1,0:T(8,128)(2,1)} %bitcast.482, ...), custom_call_target="tpu_custom_call" | custom-call | flops 13958643712 | bytes 22020096 | tf_op jit(solution)/shard_map/pallas_call | solution.py:343
  597.2 4.9 collective-permute-done.64
  623.6 16.4 %collective-permute-done.73 = bf16[1024,512]{1,0:T(8,128)(2,1)S(1)} collective-permute-done((bf16[1024,512]{1,0:T(8,128)(2,1)S(1)}, bf16[1024,512]{1,0:T(8,128)(2,1)S(1)}, u32[]{:S(2)}, u32[]{:S(2)}) %collective-permute-start.73) | collective-permute-done | bytes 1048608 | tf_op jit(solution)/shard_map/ppermute | solution.py:376
  649.0 13.8 %shard_map.312 = (bf16[2048,1408]{1,0:T(8,128)(2,1)}, bf16[2048,256]{1,0:T(8,128)(2,1)}) custom-call(bf16[384,2048]{1,0:T(8,128)(2,1)} %bitcast.87.refs_0_, bf16[384,2048]{1,0:T(8,128)(2,1)} %bitcast.88.refs_1_, bf16[256,2048]{1,0:T(8,128)(2,1)} %bitcast.89.refs_2_, ...), custom_call_target="tpu_custom_call", output_to_operand_aliasing={{0}: (8, {}), {1}: (9, {})} | custom-call | flops 6979321856 | bytes 18612224 | tf_op jit(solution)/shard_map/pallas_call | solution.py:302
  684.0 5.5 bitcast_convert_fusion.2
  689.4 22.2 %shard_map.313 = (bf16[2048,1408]{1,0:T(8,128)(2,1)}, bf16[2048,256]{1,0:T(8,128)(2,1)}) custom-call(bf16[384,2048]{1,0:T(8,128)(2,1)} %bitcast.87.refs_0_, bf16[384,2048]{1,0:T(8,128)(2,1)} %bitcast.88.refs_1_, bf16[256,2048]{1,0:T(8,128)(2,1)} %bitcast.89.refs_2_, bf16[384,2048]{1,0:T(8,128)(2,1)} %bitcast.94.refs_0_.refs_3_, ...), custom_call_target="tpu_custom_call" | custom-call | flops 6979321856 | bytes 18612224 | tf_op jit(solution)/shard_map/pallas_call | solution.py:302
  746.6 2.9 bitcast_convert_fusion.1
  752.3 4.2 collective-permute-done.86
  763.2 4.5 all-to-all-start.1
  773.4 12.0 %collective-permute-done.93 = bf16[2,64,576]{2,1,0:T(8,128)(2,1)S(1)} collective-permute-done((bf16[2,64,576]{2,1,0:T(8,128)(2,1)}, bf16[2,64,576]{2,1,0:T(8,128)(2,1)S(1)}, u32[]{:S(2)}, u32[]{:S(2)}) %collective-permute-start.93) | collective-permute-done | bytes 147488 | tf_op jit(solution)/shard_map/ppermute | solution.py:376
  786.1 2.9 collective-permute-done.92
  797.2 5.8 all-to-all-start.2
  802.9 2.8 collective-permute-start.99
  805.9 2.7 collective-permute-start.96
  808.8 4.7 bitcast_convert_fusion
  813.5 4.1 reshape.699
  817.6 2.8 copy.452
  (947 shorter events, 397.0 us)
Async XLA Ops:
  24.8 24.0 %collective-permute-start.5 = (bf16[128,768]{1,0:T(8,128)(2,1)}, bf16[128,768]{1,0:T(8,128)(2,1)}, u32[]{:S(2)}, u32[]{:S(2)}) collective-permute-start(bf16[128,768]{1,0:T(8,128)(2,1)} %get-tuple-element.446), channel_id=1, source_target_pairs={{0,16},{1,17},{2,18},{3,19},{4,20},{5,21},{6,22},{7,23},{8,24},{9,... | collective-permute-start | bytes 589832 | tf_op jit(solution)/shard_map/ppermute | solution.py:376
  27.7 25.1 %collective-permute-start.6 = (bf16[128,768]{1,0:T(8,128)(2,1)}, bf16[128,768]{1,0:T(8,128)(2,1)}, u32[]{:S(2)}, u32[]{:S(2)}) collective-permute-start(bf16[128,768]{1,0:T(8,128)(2,1)} %get-tuple-element.447), channel_id=1, source_target_pairs={{0,16},{1,17},{2,18},{3,19},{4,20},{5,21},{6,22},{7,23},{8,24},{9,... | collective-permute-start | bytes 589832 | tf_op jit(solution)/shard_map/ppermute | solution.py:376
  93.2 23.5 %collective-permute-start.20 = (bf16[2,2,2,70,576]{4,2,3,1,0:T(2,128)(2,1)}, bf16[2,2,2,70,576]{4,2,3,1,0:T(2,128)(2,1)}, u32[]{:S(2)}, u32[]{:S(2)}) collective-permute-start(bf16[2,2,2,70,576]{4,2,3,1,0:T(2,128)(2,1)} %copy.340), channel_id=1, source_target_pairs={{0,8},{1,9},{2,10},{3,11},{4,12},{5,13},{6,14},{7,15},{8,0},{9,1},... | collective-permute-start | bytes 1935368 | tf_op jit(solution)/shard_map/ppermute | solution.py:376
  94.4 46.4 %collective-permute-start.19 = (bf16[2,2,2,32,2048]{4,3,2,1,0:T(8,128)(2,1)}, bf16[2,2,2,32,2048]{4,3,2,1,0:T(8,128)(2,1)}, u32[]{:S(2)}, u32[]{:S(2)}) collective-permute-start(bf16[2,2,2,32,2048]{4,3,2,1,0:T(8,128)(2,1)} %pad_maximum_fusion.18), channel_id=1, source_target_pairs={{0,8},{1,9},{2,10},{3,11},{4,12},{5,13},{6,14},{7,15},{8,0},{9,1},... | collective-permute-start | bytes 3145736 | tf_op jit(solution)/shard_map/ppermute | solution.py:376
  95.2 48.5 %collective-permute-start.18 = (bf16[2,2,2,128,768]{4,3,0,2,1:T(8,128)(2,1)}, bf16[2,2,2,128,768]{4,3,0,2,1:T(8,128)(2,1)}, u32[]{:S(2)}, u32[]{:S(2)}) collective-permute-start(bf16[2,2,2,128,768]{4,3,0,2,1:T(8,128)(2,1)} %pad_maximum_fusion.9), channel_id=1, source_target_pairs={{0,2},{1,3},{2,0},{3,1},{4,6},{5,7},{6,4},{7,5},{8,10},{9,11},{10,... | collective-permute-start | bytes 4718600 | tf_op jit(solution)/shard_map/ppermute | solution.py:376
  96.7 53.0 %all-to-all-start = ((bf16[16,64,352]{2,1,0:T(8,128)(2,1)}), bf16[16,64,352]{2,1,0:T(8,128)(2,1)}, u32[]{:S(2)}, u32[]{:S(2)}) async-start(bf16[16,64,352]{2,1,0:T(8,128)(2,1)} %bitcast.472), calls=%async_computation | async-start | bytes 1572864 | tf_op jit(solution)/shard_map/all_to_all | solution.py:592
  103.1 89.3 %all-gather.8.cloned.1.call-start = ((), (), s32[]{:S(2)}) async-start(), calls=%async_computation.6 | async-start | bytes 2359296 | tf_op jit(solution)/shard_map/all_gather | solution.py:631
  103.3 44.3 %collective-permute-start.17 = (bf16[2,2,2,128,768]{4,3,2,1,0:T(8,128)(2,1)}, bf16[2,2,2,128,768]{4,3,2,1,0:T(8,128)(2,1)S(1)}, u32[]{:S(2)}, u32[]{:S(2)}) collective-permute-start(bf16[2,2,2,128,768]{4,3,2,1,0:T(8,128)(2,1)} %pad_maximum_fusion.8), channel_id=1, source_target_pairs={{0,4},{1,5},{2,6},{3,7},{4,0},{5,1},{6,2},{7,3},{8,12},{9,13},{10,... | collective-permute-start | bytes 4718600 | tf_op jit(solution)/shard_map/ppermute | solution.py:376
  149.7 168.3 %all-gather.10.cloned.1.call-start = ((), (), s32[]{:S(2)}) async-start(), calls=%async_computation.10 | async-start | bytes 8650752 | tf_op jit(solution)/shard_map/all_gather | solution.py:620
  150.5 167.6 %all-gather.12.cloned.1.call-start = ((), (), s32[]{:S(2)}) async-start(), calls=%async_computation.11 | async-start | bytes 8650752 | tf_op jit(solution)/shard_map/all_gather | solution.py:620
  151.2 166.9 %all-gather.14.cloned.1.call-start = ((), (), s32[]{:S(2)}) async-start(), calls=%async_computation.12 | async-start | bytes 8650752 | tf_op jit(solution)/shard_map/all_gather | solution.py:620
  159.7 29.4 %collective-permute-start.23 = (bf16[128,2048]{1,0:T(8,128)(2,1)}, bf16[128,2048]{1,0:T(8,128)(2,1)}, u32[]{:S(2)}, u32[]{:S(2)}) collective-permute-start(bf16[128,2048]{1,0:T(8,128)(2,1)} %param.36), channel_id=1, source_target_pairs={{0,16},{1,17},{2,18},{3,19},{4,20},{5,21},{6,22},{7,23},{8,24},{9,... | collective-permute-start | bytes 1572872 | tf_op jit(solution)/shard_map/ppermute | solution.py:376
  223.2 23.7 %collective-permute-start.31 = (bf16[4,48,2048]{2,1,0:T(8,128)(2,1)}, bf16[4,48,2048]{2,1,0:T(8,128)(2,1)}, u32[]{:S(2)}, u32[]{:S(2)}) collective-permute-start(bf16[4,48,2048]{2,1,0:T(8,128)(2,1)} %pad_maximum_fusion.26), channel_id=1, source_target_pairs={{0,2},{1,3},{2,0},{3,1},{4,6},{5,7},{6,4},{7,5},{8,10},{9,11},{10,... | collective-permute-start | bytes 2359304 | tf_op jit(solution)/shard_map/ppermute | solution.py:376
  223.2 27.4 %collective-permute-start.32 = (bf16[4,48,2048]{2,1,0:T(8,128)(2,1)}, bf16[4,48,2048]{2,1,0:T(8,128)(2,1)}, u32[]{:S(2)}, u32[]{:S(2)}) collective-permute-start(bf16[4,48,2048]{2,1,0:T(8,128)(2,1)} %pad_maximum_fusion.27), channel_id=1, source_target_pairs={{0,8},{1,9},{2,10},{3,11},{4,12},{5,13},{6,14},{7,15},{8,0},{9,1},... | collective-permute-start | bytes 2359304 | tf_op jit(solution)/shard_map/ppermute | solution.py:376
  254.2 23.1 %collective-permute-start.34 = (bf16[2,2,2,128,512]{4,3,2,1,0:T(8,128)(2,1)}, bf16[2,2,2,128,512]{4,3,2,1,0:T(8,128)(2,1)}, u32[]{:S(2)}, u32[]{:S(2)}) collective-permute-start(bf16[2,2,2,128,512]{4,3,2,1,0:T(8,128)(2,1)} %pad_maximum_fusion.19), channel_id=1, source_target_pairs={{0,8},{1,9},{2,10},{3,11},{4,12},{5,13},{6,14},{7,15},{8,0},{9,1},... | collective-permute-start | bytes 3145736 | tf_op jit(solution)/shard_map/ppermute | solution.py:376
  255.7 22.5 %collective-permute-start.35 = (bf16[2,2,2,128,512]{4,3,2,0,1:T(8,128)(2,1)}, bf16[2,2,2,128,512]{4,3,2,0,1:T(8,128)(2,1)}, u32[]{:S(2)}, u32[]{:S(2)}) collective-permute-start(bf16[2,2,2,128,512]{4,3,2,0,1:T(8,128)(2,1)} %pad_maximum_fusion.20), channel_id=1, source_target_pairs={{0,2},{1,3},{2,0},{3,1},{4,6},{5,7},{6,4},{7,5},{8,10},{9,11},{10,... | collective-permute-start | bytes 3145736 | tf_op jit(solution)/shard_map/ppermute | solution.py:376
  284.6 320.9 %reduce-scatter.4.cloned.1.call-start = ((), (), s32[]{:S(2)}) async-start(), calls=%async_computation.7 | async-start | bytes 8650752 | tf_op jit(solution)/shard_map/reduce_scatter | solution.py:891
  291.2 25.6 %collective-permute-start.38 = (bf16[88,2048]{1,0:T(8,128)(2,1)S(1)}, bf16[88,2048]{1,0:T(8,128)(2,1)S(1)}, u32[]{:S(2)}, u32[]{:S(2)}) collective-permute-start(bf16[88,2048]{1,0:T(8,128)(2,1)S(1)} %copy-done.153), channel_id=1, source_target_pairs={{0,1},{1,0},{2,3},{3,2},{4,5},{5,4},{6,7},{7,6},{8,9},{9,8},{10,11... | collective-permute-start | bytes 1081352 | tf_op jit(solution)/shard_map/ppermute | solution.py:379
  291.6 26.4 %collective-permute-start.37 = (bf16[128,2048]{1,0:T(8,128)(2,1)S(1)}, bf16[128,2048]{1,0:T(8,128)(2,1)S(1)}, u32[]{:S(2)}, u32[]{:S(2)}) collective-permute-start(bf16[128,2048]{1,0:T(8,128)(2,1)S(1)} %multiply_convert_fusion.1), channel_id=1, source_target_pairs={{0,16},{1,17},{2,18},{3,19},{4,20},{5,21},{6,22},{7,23},{8,24},{9,... | collective-permute-start | bytes 1572872 | tf_op jit(solution)/shard_map/ppermute | solution.py:376
  352.0 32.6 %collective-permute-start.47 = (bf16[8,32,2048]{2,1,0:T(8,128)(2,1)}, bf16[8,32,2048]{2,1,0:T(8,128)(2,1)}, u32[]{:S(2)}, u32[]{:S(2)}) collective-permute-start(bf16[8,32,2048]{2,1,0:T(8,128)(2,1)} %pad_maximum_fusion.23), channel_id=1, source_target_pairs={{0,2},{1,3},{2,0},{3,1},{4,6},{5,7},{6,4},{7,5},{8,10},{9,11},{10,... | collective-permute-start | bytes 3145736 | tf_op jit(solution)/shard_map/ppermute | solution.py:376
  353.1 33.6 %collective-permute-start.45 = (bf16[8,48,2048]{2,1,0:T(8,128)(2,1)}, bf16[8,48,2048]{2,1,0:T(8,128)(2,1)}, u32[]{:S(2)}, u32[]{:S(2)}) collective-permute-start(bf16[8,48,2048]{2,1,0:T(8,128)(2,1)} %pad_maximum_fusion.13), channel_id=1, source_target_pairs={{0,8},{1,9},{2,10},{3,11},{4,12},{5,13},{6,14},{7,15},{8,0},{9,1},... | collective-permute-start | bytes 4718600 | tf_op jit(solution)/shard_map/ppermute | solution.py:376
  353.9 33.2 %collective-permute-start.46 = (bf16[8,48,2048]{2,1,0:T(8,128)(2,1)}, bf16[8,48,2048]{2,1,0:T(8,128)(2,1)}, u32[]{:S(2)}, u32[]{:S(2)}) collective-permute-start(bf16[8,48,2048]{2,1,0:T(8,128)(2,1)} %pad_maximum_fusion.14), channel_id=1, source_target_pairs={{0,4},{1,5},{2,6},{3,7},{4,0},{5,1},{6,2},{7,3},{8,12},{9,13},{10,... | collective-permute-start | bytes 4718600 | tf_op jit(solution)/shard_map/ppermute | solution.py:376
  387.1 33.6 %collective-permute-start.50 = (bf16[8,32,2048]{2,1,0:T(8,128)(2,1)S(1)}, bf16[8,32,2048]{2,1,0:T(8,128)(2,1)}, u32[]{:S(2)}, u32[]{:S(2)}) collective-permute-start(bf16[8,32,2048]{2,1,0:T(8,128)(2,1)S(1)} %copy-done.138), channel_id=1, source_target_pairs={{0,2},{1,3},{2,0},{3,1},{4,6},{5,7},{6,4},{7,5},{8,10},{9,11},{10,... | collective-permute-start | bytes 3145736 | tf_op jit(solution)/shard_map/ppermute | solution.py:376
  388.3 32.7 %collective-permute-start.48 = (bf16[8,48,2048]{2,1,0:T(8,128)(2,1)S(1)}, bf16[8,48,2048]{2,1,0:T(8,128)(2,1)}, u32[]{:S(2)}, u32[]{:S(2)}) collective-permute-start(bf16[8,48,2048]{2,1,0:T(8,128)(2,1)S(1)} %copy-done.124), channel_id=1, source_target_pairs={{0,8},{1,9},{2,10},{3,11},{4,12},{5,13},{6,14},{7,15},{8,0},{9,1},... | collective-permute-start | bytes 4718600 | tf_op jit(solution)/shard_map/ppermute | solution.py:376
  389.3 32.7 %collective-permute-start.49 = (bf16[8,48,2048]{2,1,0:T(8,128)(2,1)}, bf16[8,48,2048]{2,1,0:T(8,128)(2,1)}, u32[]{:S(2)}, u32[]{:S(2)}) collective-permute-start(bf16[8,48,2048]{2,1,0:T(8,128)(2,1)} %pad_maximum_fusion.12), channel_id=1, source_target_pairs={{0,4},{1,5},{2,6},{3,7},{4,0},{5,1},{6,2},{7,3},{8,12},{9,13},{10,... | collective-permute-start | bytes 4718600 | tf_op jit(solution)/shard_map/ppermute | solution.py:376
  422.0 38.5 %collective-permute-start.53 = (bf16[8,32,2048]{2,1,0:T(8,128)(2,1)}, bf16[8,32,2048]{2,1,0:T(8,128)(2,1)S(1)}, u32[]{:S(2)}, u32[]{:S(2)}) collective-permute-start(bf16[8,32,2048]{2,1,0:T(8,128)(2,1)} %bitcast.511), channel_id=1, source_target_pairs={{0,2},{1,3},{2,0},{3,1},{4,6},{5,7},{6,4},{7,5},{8,10},{9,11},{10,... | collective-permute-start | bytes 3145736 | tf_op jit(solution)/shard_map/ppermute | solution.py:376
  422.9 37.6 %collective-permute-start.51 = (bf16[8,48,2048]{2,1,0:T(8,128)(2,1)}, bf16[8,48,2048]{2,1,0:T(8,128)(2,1)S(1)}, u32[]{:S(2)}, u32[]{:S(2)}) collective-permute-start(bf16[8,48,2048]{2,1,0:T(8,128)(2,1)} %bitcast.509), channel_id=1, source_target_pairs={{0,8},{1,9},{2,10},{3,11},{4,12},{5,13},{6,14},{7,15},{8,0},{9,1},... | collective-permute-start | bytes 4718600 | tf_op jit(solution)/shard_map/ppermute | solution.py:376
  423.9 36.7 %collective-permute-start.52 = (bf16[8,48,2048]{2,1,0:T(8,128)(2,1)}, bf16[8,48,2048]{2,1,0:T(8,128)(2,1)}, u32[]{:S(2)}, u32[]{:S(2)}) collective-permute-start(bf16[8,48,2048]{2,1,0:T(8,128)(2,1)} %bitcast.508), channel_id=1, source_target_pairs={{0,4},{1,5},{2,6},{3,7},{4,0},{5,1},{6,2},{7,3},{8,12},{9,13},{10,... | collective-permute-start | bytes 4718600 | tf_op jit(solution)/shard_map/ppermute | solution.py:376
  460.6 42.3 %collective-permute-start.56 = (bf16[8,32,2048]{2,1,0:T(8,128)(2,1)}, bf16[8,32,2048]{2,1,0:T(8,128)(2,1)}, u32[]{:S(2)}, u32[]{:S(2)}) collective-permute-start(bf16[8,32,2048]{2,1,0:T(8,128)(2,1)} %bitcast.510), channel_id=1, source_target_pairs={{0,2},{1,3},{2,0},{3,1},{4,6},{5,7},{6,4},{7,5},{8,10},{9,11},{10,... | collective-permute-start | bytes 3145736 | tf_op jit(solution)/shard_map/ppermute | solution.py:376
  461.4 41.6 %collective-permute-start.54 = (bf16[8,48,2048]{2,1,0:T(8,128)(2,1)}, bf16[8,48,2048]{2,1,0:T(8,128)(2,1)}, u32[]{:S(2)}, u32[]{:S(2)}) collective-permute-start(bf16[8,48,2048]{2,1,0:T(8,128)(2,1)} %bitcast.507), channel_id=1, source_target_pairs={{0,8},{1,9},{2,10},{3,11},{4,12},{5,13},{6,14},{7,15},{8,0},{9,1},... | collective-permute-start | bytes 4718600 | tf_op jit(solution)/shard_map/ppermute | solution.py:376
  462.9 40.0 %collective-permute-start.55 = (bf16[8,48,2048]{2,1,0:T(8,128)(2,1)}, bf16[8,48,2048]{2,1,0:T(8,128)(2,1)}, u32[]{:S(2)}, u32[]{:S(2)}) collective-permute-start(bf16[8,48,2048]{2,1,0:T(8,128)(2,1)} %bitcast.506), channel_id=1, source_target_pairs={{0,4},{1,5},{2,6},{3,7},{4,0},{5,1},{6,2},{7,3},{8,12},{9,13},{10,... | collective-permute-start | bytes 4718600 | tf_op jit(solution)/shard_map/ppermute | solution.py:376
  548.7 26.1 %collective-permute-start.63 = (bf16[128,2048]{1,0:T(8,128)(2,1)S(1)}, bf16[128,2048]{1,0:T(8,128)(2,1)S(1)}, u32[]{:S(2)}, u32[]{:S(2)}) collective-permute-start(bf16[128,2048]{1,0:T(8,128)(2,1)S(1)} %fusion.40), channel_id=1, source_target_pairs={{0,16},{1,17},{2,18},{3,19},{4,20},{5,21},{6,22},{7,23},{8,24},{9,... | collective-permute-start | bytes 1572872 | tf_op jit(solution)/shard_map/ppermute | solution.py:376
  576.1 153.6 %reduce-scatter.6.cloned.1.call-start = ((), (), s32[]{:S(2)}) async-start(), calls=%async_computation.8 | async-start | bytes 8650752 | tf_op jit(solution)/shard_map/reduce_scatter | solution.py:875
  616.3 23.8 %collective-permute-start.73 = (bf16[1024,512]{1,0:T(8,128)(2,1)S(1)}, bf16[1024,512]{1,0:T(8,128)(2,1)S(1)}, u32[]{:S(2)}, u32[]{:S(2)}) collective-permute-start(bf16[1024,512]{1,0:T(8,128)(2,1)S(1)} %copy-done.140), channel_id=1, source_target_pairs={{0,8},{1,9},{2,10},{3,11},{4,12},{5,13},{6,14},{7,15},{8,0},{9,1},... | collective-permute-start | bytes 3145736 | tf_op jit(solution)/shard_map/ppermute | solution.py:376
  616.4 24.3 %collective-permute-start.74 = (bf16[1024,512]{1,0:T(8,128)(2,1)S(1)}, bf16[1024,512]{1,0:T(8,128)(2,1)S(1)}, u32[]{:S(2)}, u32[]{:S(2)}) collective-permute-start(bf16[1024,512]{1,0:T(8,128)(2,1)S(1)} %copy-done.139), channel_id=1, source_target_pairs={{0,4},{1,5},{2,6},{3,7},{4,0},{5,1},{6,2},{7,3},{8,12},{9,13},{10,... | collective-permute-start | bytes 3145736 | tf_op jit(solution)/shard_map/ppermute | solution.py:376
  643.9 22.3 %collective-permute-start.77 = (bf16[2,2,128,512]{3,2,0,1:T(8,128)(2,1)}, bf16[2,2,128,512]{3,2,0,1:T(8,128)(2,1)}, u32[]{:S(2)}, u32[]{:S(2)}) collective-permute-start(bf16[2,2,128,512]{3,2,0,1:T(8,128)(2,1)} %select_bitcast_fusion.20), channel_id=1, source_target_pairs={{0,8},{1,9},{2,10},{3,11},{4,12},{5,13},{6,14},{7,15},{8,0},{9,1},... | collective-permute-start | bytes 1572872 | tf_op jit(solution)/shard_map/ppermute | solution.py:376
  645.0 24.2 %collective-permute-start.78 = (bf16[128,2048]{1,0:T(8,128)(2,1)}, bf16[128,2048]{1,0:T(8,128)(2,1)}, u32[]{:S(2)}, u32[]{:S(2)}) collective-permute-start(bf16[128,2048]{1,0:T(8,128)(2,1)} %fusion.41), channel_id=1, source_target_pairs={{0,16},{1,17},{2,18},{3,19},{4,20},{5,21},{6,22},{7,23},{8,24},{9,... | collective-permute-start | bytes 1572872 | tf_op jit(solution)/shard_map/ppermute | solution.py:376
  649.0 22.5 %collective-permute-start.75 = (f32[256,576]{0,1:T(8,128)}, f32[256,576]{0,1:T(8,128)}, u32[]{:S(2)}, u32[]{:S(2)}) collective-permute-start(f32[256,576]{0,1:T(8,128)} %pad_maximum_fusion.33), channel_id=1, source_target_pairs={{0,1},{1,0},{2,3},{3,2},{4,5},{5,4},{6,7},{7,6},{8,9},{9,8},{10,11... | collective-permute-start | bytes 1769480 | tf_op jit(solution)/shard_map/ppermute | solution.py:379
  679.2 116.9 %reduce-scatter.8.cloned.1.call-start = ((), (), s32[]{:S(2)}) async-start(), calls=%async_computation.9 | async-start | bytes 8650752 | tf_op jit(solution)/shard_map/reduce_scatter | solution.py:880
  679.3 32.4 %collective-permute-start.80 = (bf16[2,128,1024]{2,1,0:T(8,128)(2,1)}, bf16[2,128,1024]{2,1,0:T(8,128)(2,1)}, u32[]{:S(2)}, u32[]{:S(2)}) collective-permute-start(bf16[2,128,1024]{2,1,0:T(8,128)(2,1)} %select_bitcast_fusion.19), channel_id=1, source_target_pairs={{0,2},{1,3},{2,0},{3,1},{4,6},{5,7},{6,4},{7,5},{8,10},{9,11},{10,... | collective-permute-start | bytes 1572872 | tf_op jit(solution)/shard_map/ppermute | solution.py:376
  680.3 33.6 %collective-permute-start.83 = (bf16[512,576]{0,1:T(8,128)(2,1)}, bf16[512,576]{0,1:T(8,128)(2,1)}, u32[]{:S(2)}, u32[]{:S(2)}) collective-permute-start(bf16[512,576]{0,1:T(8,128)(2,1)} %convolution_convert_fusion.6), channel_id=1, source_target_pairs={{0,4},{1,5},{2,6},{3,7},{4,0},{5,1},{6,2},{7,3},{8,12},{9,13},{10,... | collective-permute-start | bytes 1769480 | tf_op jit(solution)/shard_map/ppermute | solution.py:376
  680.7 37.7 %collective-permute-start.82 = (bf16[256,2048]{1,0:T(8,128)(2,1)}, bf16[256,2048]{1,0:T(8,128)(2,1)}, u32[]{:S(2)}, u32[]{:S(2)}) collective-permute-start(bf16[256,2048]{1,0:T(8,128)(2,1)} %convolution_convert_fusion.1), channel_id=1, source_target_pairs={{0,4},{1,5},{2,6},{3,7},{4,0},{5,1},{6,2},{7,3},{8,12},{9,13},{10,... | collective-permute-start | bytes 3145736 | tf_op jit(solution)/shard_map/ppermute | solution.py:376
  682.3 39.2 %collective-permute-start.79 = (bf16[1024,640]{1,0:T(8,128)(2,1)}, bf16[1024,640]{1,0:T(8,128)(2,1)}, u32[]{:S(2)}, u32[]{:S(2)}) collective-permute-start(bf16[1024,640]{1,0:T(8,128)(2,1)} %convolution_convert_fusion.3), channel_id=1, source_target_pairs={{0,2},{1,3},{2,0},{3,1},{4,6},{5,7},{6,4},{7,5},{8,10},{9,11},{10,... | collective-permute-start | bytes 3932168 | tf_op jit(solution)/shard_map/ppermute | solution.py:376
  683.4 41.7 %collective-permute-start.81 = (bf16[1024,896]{1,0:T(8,128)(2,1)}, bf16[1024,896]{1,0:T(8,128)(2,1)}, u32[]{:S(2)}, u32[]{:S(2)}) collective-permute-start(bf16[1024,896]{1,0:T(8,128)(2,1)} %convolution_convert_fusion.2), channel_id=1, source_target_pairs={{0,8},{1,9},{2,10},{3,11},{4,12},{5,13},{6,14},{7,15},{8,0},{9,1},... | collective-permute-start | bytes 5505032 | tf_op jit(solution)/shard_map/ppermute | solution.py:376
  763.2 32.9 %all-to-all-start.1 = ((bf16[16,64,352]{2,1,0:T(8,128)(2,1)}), bf16[16,64,352]{2,1,0:T(8,128)(2,1)}, u32[]{:S(2)}, u32[]{:S(2)}) async-start(bf16[16,64,352]{2,1,0:T(8,128)(2,1)} %select_add_fusion), calls=%async_computation.3 | async-start | bytes 1572864 | tf_op jit(solution)/shard_map/all_to_all | solution.py:884
  797.2 35.2 %all-to-all-start.2 = ((f32[16,1,2336]{2,1,0:T(1,128)}), f32[16,1,2336]{2,1,0:T(1,128)}, u32[]{:S(2)}, u32[]{:S(2)}) async-start(f32[16,1,2336]{2,1,0:T(1,128)} %all_to_all.23), calls=%async_computation.5 | async-start | bytes 311296 | tf_op jit(solution)/shard_map/all_to_all | solution.py:978
  805.9 24.6 %collective-permute-start.96 = (bf16[128,640]{1,0:T(8,128)(2,1)}, bf16[128,640]{1,0:T(8,128)(2,1)}, u32[]{:S(2)}, u32[]{:S(2)}) collective-permute-start(bf16[128,640]{1,0:T(8,128)(2,1)} %select_bitcast_fusion.51), channel_id=1, source_target_pairs={{0,16},{1,17},{2,18},{3,19},{4,20},{5,21},{6,22},{7,23},{8,24},{9,... | collective-permute-start | bytes 491528 | tf_op jit(solution)/shard_map/ppermute | solution.py:376
  808.6 25.4 %collective-permute-start.97 = (bf16[128,896]{1,0:T(8,128)(2,1)}, bf16[128,896]{1,0:T(8,128)(2,1)}, u32[]{:S(2)}, u32[]{:S(2)}) collective-permute-start(bf16[128,896]{1,0:T(8,128)(2,1)} %select_bitcast_fusion.44), channel_id=1, source_target_pairs={{0,16},{1,17},{2,18},{3,19},{4,20},{5,21},{6,22},{7,23},{8,24},{9,... | collective-permute-start | bytes 688136 | tf_op jit(solution)/shard_map/ppermute | solution.py:376
  (244 other events, 1995.4 us)
Sparse Core Ops, SparseCore 0:
  149.9 13.4 all-gather.7
  164.9 17.1 all-gather.9
  183.6 17.1 all-gather.11
  284.8 15.6 all-gather.13
  576.2 13.4 reduce-scatter.3
  679.3 11.8 reduce-scatter.5
  729.9 12.8 reduce-scatter.7
